TPU v7x, 128 devices: a whole 4x4x4 slice. The times are simulated.
128 devices in a mesh: section: 8 (over z_hi, x), tensor: 16 (over y, z_lo, core).
Axes of the slice: x: 4, y: 4, z: 4 (z_hi: 2, z_lo: 2; z = z_hi * 2 + z_lo), core: 2. Of those that a mesh axis runs over, the one named last changes fastest.
Arguments:
- local_codes: bfloat16 [8, 2, 512, 4096], P('section', None, 'tensor'), may hold values from -4 to 4
- local_scales: bfloat16 [8, 2, 512], P('section', None, 'tensor'), may hold values from 0.19921875 to 5
- parked_codes: bfloat16 [8, 2, 512, 4096], P('section', None, 'tensor'), may hold values from -4 to 4
- parked_scales: bfloat16 [8, 2, 512], P('section', None, 'tensor'), may hold values from 0.19921875 to 5
- keep_count: int32 [8], replicated, may hold values from 1 to 2, as said below
- roster: int32 [8], replicated, may hold values from 0 to 3, as said below
- norm_gain: float32 [8, 4096], P('section'), may hold values from 0.1 to 1.9
- w_gate: bfloat16 [8, 4096, 14336], P('section', None, 'tensor'), may hold values from -0.09375 to 0.09375
- w_up: bfloat16 [8, 4096, 14336], P('section', None, 'tensor'), may hold values from -0.09375 to 0.09375
- w_down: bfloat16 [8, 14336, 4096], P('section', 'tensor'), may hold values from -0.046875 to 0.046875
- pending: bfloat16 [8, 512, 4096], P('section', 'tensor'), may hold values from -6 to 6
Outputs:
- input_grad: bfloat16 [8, 512, 4096], P('section', 'tensor')
Inputs may be any that keep to these rules, and one draw needn't show every extreme that they name: Sections s >= 4 keep every stash: keep_count[s] = 2. roster[s] < keep_count[s] + 2 for s < 4, and roster[s] < keep_count[s] for the other sections.
All inputs are finite; a program needn't handle non-finite values.
Results may differ from a plain program's by a relative error of at most 0.0058.
Values may be sent and summed in bfloat16 or wider, within the bound.
No kernel may reach another device: no remote copies, remote signals or barrier semaphores. Data moves between devices by JAX's collectives and lax.ppermute only.
A program may use at most 128 MiB of HBM per device.

v0:
```python
import jax
import jax.numpy as jnp
from jax import lax
from jax.sharding import PartitionSpec as P

LOCAL_SLOTS = 2
PARK_SLOTS = 2


def partner(shard, axis, distance):
    return lax.ppermute(shard, axis, [(i, i ^ 1 << distance) for i in range(lax.axis_size(axis))])


def shifted(shard, axis, by):
    peers = lax.axis_size(axis)
    return lax.ppermute(shard, axis, [(i, (i + by) % peers) for i in range(peers)])


def on_device(
    local_codes,
    local_scales,
    parked_codes,
    parked_scales,
    keep_count,
    roster,
    norm_gain,
    w_gate,
    w_up,
    w_down,
    pending,
):
    sections = lax.axis_size("section")
    mine = lax.axis_index("section")
    my_keep = keep_count[mine]
    my_slot = roster[mine]
    is_parked = my_slot >= my_keep
    local_slot = jnp.clip(my_slot, 0, LOCAL_SLOTS - 1)
    own_codes = lax.dynamic_index_in_dim(local_codes[0], local_slot, 0, keepdims=False)
    own_scales = lax.dynamic_index_in_dim(local_scales[0], local_slot, 0, keepdims=False)
    levels = sections.bit_length() - 1
    payload = (parked_codes[0], parked_scales[0])
    for level in range(levels):
        payload = partner((payload[0], payload[1]), "section", level)
    park_slot = jnp.clip(my_slot - my_keep, 0, PARK_SLOTS - 1)
    fetched_codes = lax.dynamic_index_in_dim(payload[0], park_slot, 0, keepdims=False)
    fetched_scales = lax.dynamic_index_in_dim(payload[1], park_slot, 0, keepdims=False)
    codes = jnp.where(is_parked, fetched_codes, own_codes)
    scales = jnp.where(is_parked, fetched_scales, own_scales)
    x_rows = codes.astype(jnp.float32) * scales.astype(jnp.float32)[:, None]
    inv_rms = lax.rsqrt(jnp.mean(x_rows * x_rows, axis=-1, keepdims=True) + 1e-05)
    unit = x_rows * inv_rms
    gain = norm_gain[0]
    normed = (unit * gain).astype(jnp.bfloat16)
    gate_w = w_gate[0]
    up_w = w_up[0]
    down_w = w_down[0]
    hidden_local = gate_w.shape[1]
    piece = lax.all_gather(normed, "tensor", axis=0, tiled=True)
    both = jnp.concatenate(
        [
            jnp.dot(piece, gate_w, preferred_element_type=jnp.float32),
            jnp.dot(piece, up_w, preferred_element_type=jnp.float32),
        ],
        axis=1,
    )
    gate = both[:, :hidden_local]
    up = both[:, hidden_local:]
    cot_rows = shifted(pending[0], "section", -1)
    dh = lax.dot_general(
        lax.all_gather(cot_rows, "tensor", axis=0, tiled=True),
        down_w,
        (((1,), (1,)), ((), ())),
        preferred_element_type=jnp.float32,
    )
    sig = jax.nn.sigmoid(gate)
    dgate = (dh * up * sig * (1.0 + gate * (1.0 - sig))).astype(jnp.bfloat16)
    dup = (dh * gate * sig).astype(jnp.bfloat16)
    dn = lax.psum_scatter(
        lax.dot_general(dgate, gate_w, (((1,), (1,)), ((), ())), preferred_element_type=jnp.float32)
        + lax.dot_general(dup, up_w, (((1,), (1,)), ((), ())), preferred_element_type=jnp.float32),
        "tensor",
        scatter_dimension=0,
        tiled=True,
    )
    scaled = dn * gain
    result = cot_rows.astype(jnp.float32) + inv_rms * (
        scaled - unit * jnp.mean(scaled * unit, axis=-1, keepdims=True)
    )
    return result.astype(jnp.bfloat16)[None]


def solution(mesh):
    placed = (
        P("section", None, "tensor", None),
        P("section", None, "tensor"),
        P("section", None, "tensor", None),
        P("section", None, "tensor"),
        P(),
        P(),
        P("section", None),
        P("section", None, "tensor"),
        P("section", None, "tensor"),
        P("section", "tensor", None),
        P("section", "tensor", None),
    )
    return jax.shard_map(
        on_device,
        mesh=mesh,
        in_specs=placed,
        out_specs=P("section", "tensor", None),
        check_vma=False,
    )
```

profile of v0, /device:TPU:1, one launch (start us, length us, event | category | flops | bytes accessed | tf_op | source)
XLA Modules:
  0.0 257.7 jit_solution(8165870157774877751)
XLA Ops:
  6.5 6.6 %collective-permute-start = (bf16[32,4096]{1,0:T(8,128)(2,1)}, bf16[32,4096]{1,0:T(8,128)(2,1)S(1)}, u32[]{:S(2)}, u32[]{:S(2)}) collective-permute-start(bf16[32,4096]{1,0:T(8,128)(2,1)} %bitcast.49), channel_id=1, source_target_pairs={{0,112},{16,0},{32,16},{48,32},{64,48},{80,64},{96,80},{112,96},{1... | collective-permute-start | bytes 786440 | tf_op jit(solution)/shard_map/ppermute | solution.py:16
  13.2 5.3 %collective-permute-done = bf16[32,4096]{1,0:T(8,128)(2,1)S(1)} collective-permute-done((bf16[32,4096]{1,0:T(8,128)(2,1)}, bf16[32,4096]{1,0:T(8,128)(2,1)S(1)}, u32[]{:S(2)}, u32[]{:S(2)}) %collective-permute-start) | collective-permute-done | bytes 262176 | tf_op jit(solution)/shard_map/ppermute | solution.py:16
  18.5 0.7 copy-done
  19.2 0.0 all-gather.3.cloned.1.call-update
  19.2 0.0 all-gather.5.cloned.1.call-start
  19.2 0.1 collective-permute-start.1
  19.3 12.1 %collective-permute-done.1 = bf16[2,32,4096]{2,1,0:T(8,128)(2,1)S(1)} collective-permute-done((bf16[2,32,4096]{2,1,0:T(8,128)(2,1)}, bf16[2,32,4096]{2,1,0:T(8,128)(2,1)S(1)}, u32[]{:S(2)}, u32[]{:S(2)}) %collective-permute-start.1) | collective-permute-done | bytes 524320 | tf_op jit(solution)/shard_map/ppermute | solution.py:11
  31.4 2.4 collective-permute-start.2
  33.8 10.1 %collective-permute-done.2 = bf16[2,32,4096]{2,1,0:T(8,128)(2,1)S(1)} collective-permute-done((bf16[2,32,4096]{2,1,0:T(8,128)(2,1)S(1)}, bf16[2,32,4096]{2,1,0:T(8,128)(2,1)S(1)}, u32[]{:S(2)}, u32[]{:S(2)}) %collective-permute-start.2) | collective-permute-done | bytes 524320 | tf_op jit(solution)/shard_map/ppermute | solution.py:11
  43.8 4.7 %collective-permute-start.3 = (bf16[2,32,4096]{2,1,0:T(8,128)(2,1)S(1)}, bf16[2,32,4096]{2,1,0:T(8,128)(2,1)S(1)}, u32[]{:S(2)}, u32[]{:S(2)}) collective-permute-start(bf16[2,32,4096]{2,1,0:T(8,128)(2,1)S(1)} %collective-permute-done.2), channel_id=1, source_target_pairs={{0,64},{16,80},{32,96},{48,112},{64,0},{80,16},{96,32},{112,48},{1... | collective-permute-start | bytes 1572872 | tf_op jit(solution)/shard_map/ppermute | solution.py:11
  48.5 1.2 dynamic_slice.20
  49.8 1.3 dynamic_slice.21
  53.8 0.0 collective-permute-done.4
  53.8 2.1 collective-permute-start.5
  56.5 1.5 collective-permute-done.5
  58.0 0.0 collective-permute-start.6
  58.0 9.9 %collective-permute-done.6 = bf16[2,32]{1,0:T(2,128)(2,1)S(1)} collective-permute-done((bf16[2,32]{1,0:T(2,128)(2,1)S(1)}, bf16[2,32]{1,0:T(2,128)(2,1)S(1)}, u32[]{:S(2)}, u32[]{:S(2)}) %collective-permute-start.6) | collective-permute-done | bytes 160 | tf_op jit(solution)/shard_map/ppermute | solution.py:11
  67.9 0.7 fusion.20
  68.6 1.2 multiply_reduce_fusion.1
  69.8 1.6 multiply_convert_fusion.3
  71.3 0.0 all-gather.5.cloned.1.call-update
  71.4 0.0 reduce-scatter.2.cloned.1.call-start
  71.4 0.0 all-gather.3.cloned.1.call-done
  71.4 10.5 %fusion.8 = f32[512,896]{1,0:T(8,128)S(1)} fusion(bf16[512,4096]{1,0:T(8,128)(2,1)} %all-gather.3.cloned.1.call-done, bf16[1,896,4096]{2,1,0:T(8,128)(2,1)} %param.20), kind=kOutput, calls=%fused_computation.8 | convolution fusion | flops 3758096384 | bytes 13369344 | tf_op jit(solution)/shard_map/dot_general | solution.py:69
  81.9 26.1 %all-gather.5.cloned.1.call-done = bf16[512,4096]{1,0:T(8,128)(2,1)} async-done(((bf16[32,4096]{1,0:T(8,128)(2,1)}), bf16[512,4096]{1,0:T(8,128)(2,1)}) %all-gather.5.cloned.1.call-update) | async-done | bytes 4194320 | tf_op jit(solution)/shard_map/all_gather | solution.py:58
  108.0 10.1 %fusion.2 = f32[512,896]{1,0:T(8,128)} fusion(bf16[512,4096]{1,0:T(8,128)(2,1)} %all-gather.5.cloned.1.call-done, bf16[1,4096,896]{2,1,0:T(8,128)(2,1)} %param.18), kind=kOutput, calls=%fused_computation.2 | convolution fusion | flops 3758096384 | bytes 13369344 | tf_op jit(solution)/shard_map/dot_general | solution.py:61
  118.2 19.2 %fusion = f32[512,4096]{1,0:T(8,128)} fusion(bf16[1,4096,896]{2,1,0:T(8,128)(2,1)} %param.18, f32[512,896]{1,0:T(8,128)} %fusion.2, f32[512,896]{1,0:T(8,128)S(1)} %fusion.8, bf16[512,4096]{1,0:T(8,128)(2,1)} %all-gather.5.cloned.1.call-done, bf16[1,4096,896]{2,1,0:T(8,128)(2,1)} %param.19), kind=kOutput, calls=%fused_computation | convolution fusion | flops 7520780288 | bytes 30932992 | tf_op jit(solution)/shard_map/dot_general | solution.py:79
  137.4 13.8 %fusion.10 = f32[512,4096]{1,0:T(8,128)} fusion(f32[512,4096]{1,0:T(8,128)} %fusion, bf16[1,4096,896]{2,1,0:T(8,128)(2,1)} %param.19, f32[512,896]{1,0:T(8,128)S(1)} %fusion.8, f32[512,896]{1,0:T(8,128)} %fusion.2), kind=kOutput, calls=%fused_computation.10 | convolution fusion | flops 3762946048 | bytes 27787264 | tf_op jit(solution)/shard_map/dot_general | solution.py:80
  151.2 0.0 reduce-scatter.2.cloned.1.call-update
  151.2 96.7 %reduce-scatter.2.cloned.1.call-done = f32[32,4096]{1,0:T(8,128)} async-done(((f32[512,4096]{1,0:T(8,128)}), f32[32,4096]{1,0:T(8,128)}) %reduce-scatter.2.cloned.1.call-update) | async-done | bytes 524304 | tf_op jit(solution)/shard_map/reduce_scatter | solution.py:78
  247.9 1.3 multiply_reduce_fusion
  249.2 2.0 fusion.19
  (10 shorter events, 0.0 us)
Async XLA Ops:
  6.5 64.9 %all-gather.3.cloned.1.call-start = ((), (), s32[]{:S(2)}) async-start(), calls=%async_computation.1 | async-start | bytes 4456448 | tf_op jit(solution)/shard_map/all_gather | solution.py:70
  6.5 11.9 %collective-permute-start = (bf16[32,4096]{1,0:T(8,128)(2,1)}, bf16[32,4096]{1,0:T(8,128)(2,1)S(1)}, u32[]{:S(2)}, u32[]{:S(2)}) collective-permute-start(bf16[32,4096]{1,0:T(8,128)(2,1)} %bitcast.49), channel_id=1, source_target_pairs={{0,112},{16,0},{32,16},{48,32},{64,48},{80,64},{96,80},{112,96},{1... | collective-permute-start | bytes 786440 | tf_op jit(solution)/shard_map/ppermute | solution.py:16
  18.4 0.7 copy-start
  19.2 88.9 %all-gather.5.cloned.1.call-start = ((), (), s32[]{:S(2)}) async-start(), calls=%async_computation.2 | async-start | bytes 4456448 | tf_op jit(solution)/shard_map/all_gather | solution.py:58
  19.2 12.2 %collective-permute-start.1 = (bf16[2,32,4096]{2,1,0:T(8,128)(2,1)}, bf16[2,32,4096]{2,1,0:T(8,128)(2,1)S(1)}, u32[]{:S(2)}, u32[]{:S(2)}) collective-permute-start(bf16[2,32,4096]{2,1,0:T(8,128)(2,1)} %bitcast.48), channel_id=1, source_target_pairs={{0,16},{16,0},{32,48},{48,32},{64,80},{80,64},{96,112},{112,96},{1... | collective-permute-start | bytes 1572872 | tf_op jit(solution)/shard_map/ppermute | solution.py:11
  31.4 12.5 %collective-permute-start.2 = (bf16[2,32,4096]{2,1,0:T(8,128)(2,1)S(1)}, bf16[2,32,4096]{2,1,0:T(8,128)(2,1)S(1)}, u32[]{:S(2)}, u32[]{:S(2)}) collective-permute-start(bf16[2,32,4096]{2,1,0:T(8,128)(2,1)S(1)} %collective-permute-done.1), channel_id=1, source_target_pairs={{0,32},{16,48},{32,0},{48,16},{64,96},{80,112},{96,64},{112,80},{1... | collective-permute-start | bytes 1572872 | tf_op jit(solution)/shard_map/ppermute | solution.py:11
  43.8 24.7 %collective-permute-start.3 = (bf16[2,32,4096]{2,1,0:T(8,128)(2,1)S(1)}, bf16[2,32,4096]{2,1,0:T(8,128)(2,1)S(1)}, u32[]{:S(2)}, u32[]{:S(2)}) collective-permute-start(bf16[2,32,4096]{2,1,0:T(8,128)(2,1)S(1)} %collective-permute-done.2), channel_id=1, source_target_pairs={{0,64},{16,80},{32,96},{48,112},{64,0},{80,16},{96,32},{112,48},{1... | collective-permute-start | bytes 1572872 | tf_op jit(solution)/shard_map/ppermute | solution.py:11
  48.5 5.2 %collective-permute-start.4 = (bf16[2,32]{1,0:T(2,128)(2,1)}, bf16[2,32]{1,0:T(2,128)(2,1)S(1)}, u32[]{:S(2)}, u32[]{:S(2)}) collective-permute-start(bf16[2,32]{1,0:T(2,128)(2,1)} %bitcast.50), channel_id=1, source_target_pairs={{0,16},{16,0},{32,48},{48,32},{64,80},{80,64},{96,112},{112,96},{1... | collective-permute-start | bytes 392 | tf_op jit(solution)/shard_map/ppermute | solution.py:11
  53.8 4.3 %collective-permute-start.5 = (bf16[2,32]{1,0:T(2,128)(2,1)S(1)}, bf16[2,32]{1,0:T(2,128)(2,1)S(1)}, u32[]{:S(2)}, u32[]{:S(2)}) collective-permute-start(bf16[2,32]{1,0:T(2,128)(2,1)S(1)} %collective-permute-done.4), channel_id=1, source_target_pairs={{0,32},{16,48},{32,0},{48,16},{64,96},{80,112},{96,64},{112,80},{1... | collective-permute-start | bytes 392 | tf_op jit(solution)/shard_map/ppermute | solution.py:11
  58.0 9.9 %collective-permute-start.6 = (bf16[2,32]{1,0:T(2,128)(2,1)S(1)}, bf16[2,32]{1,0:T(2,128)(2,1)S(1)}, u32[]{:S(2)}, u32[]{:S(2)}) collective-permute-start(bf16[2,32]{1,0:T(2,128)(2,1)S(1)} %collective-permute-done.5), channel_id=1, source_target_pairs={{0,64},{16,80},{32,96},{48,112},{64,0},{80,16},{96,32},{112,48},{1... | collective-permute-start | bytes 392 | tf_op jit(solution)/shard_map/ppermute | solution.py:11
  71.4 176.5 %reduce-scatter.2.cloned.1.call-start = ((), (), s32[]{:S(2)}) async-start(), calls=%async_computation.3 | async-start | bytes 8912896 | tf_op jit(solution)/shard_map/reduce_scatter | solution.py:78
  151.2 96.7 %copy-start.2 = (f32[1,4096]{1,0:T(1,128)S(1)}, f32[1,4096]{1,0:T(1,128)}, u32[]{:S(2)}) copy-start(f32[1,4096]{1,0:T(1,128)} %param.17) | copy-start | bytes 49156
  151.2 98.0 %copy-start.1 = (bf16[32,4096]{1,0:T(8,128)(2,1)S(1)}, bf16[32,4096]{1,0:T(8,128)(2,1)}, u32[]{:S(2)}) copy-start(bf16[32,4096]{1,0:T(8,128)(2,1)} %copy-done) | copy-start | bytes 786436
Sparse Core Ops, SparseCore 0:
  19.3 44.2 all-gather.2
  71.5 36.5 all-gather.4
  151.3 96.5 reduce-scatter.1
where the time goes:
time: 258 us
  waiting for transfers between devices  162 us (63%)
  matrix products  53.6 us (21%)
  between operations  16.5 us (6%)
  starting transfers between devices  16 us (6%)
  other arithmetic  6.71 us (3%)
  local copies, waits for them, and re-layouts  3.27 us (1%)
    reduce_scatter x1, waiting for transfers between devices, on_device(): lax.psum_scatter(lax.dot_general(dgate, gate_w, (((1,), (1,)), ((), ())),...  96.7 us
    ppermute x6, waiting for transfers between devices, partner(): lax.ppermute(shard, axis, [(i, i ^ 1 << distance) for i in range(lax.axis...  33.5 us
    all_gather x1, waiting for transfers between devices, on_device(): piece = lax.all_gather(normed, 'tensor', axis=0, tiled=True)  26.1 us
    dot_general x1, matrix products, on_device(): lax.dot_general(dgate, gate_w, (((1,), (1,)), ((), ())), preferred_elemen...  19.2 us
    dot_general x1, matrix products, on_device(): lax.dot_general(dup, up_w, (((1,), (1,)), ((), ())), preferred_element_ty...  13.8 us
    dot_general x1, matrix products, on_device(): lax.dot_general(lax.all_gather(cot_rows, 'tensor', axis=0, tiled=True), d...  10.5 us
    dot_general x1, matrix products, on_device(): jnp.dot(piece, gate_w, preferred_element_type=jnp.float32)  10.1 us
    ppermute x6, starting transfers between devices, partner(): lax.ppermute(shard, axis, [(i, i ^ 1 << distance) for i in range(lax.axis...  9.27 us
  transfers between devices with their start and end apart: 10, of which 7 were waited for; matrix products, arithmetic and copies ran while one was open for 6% of the time, Pallas kernels for 0%

commit v1 on v0

v1 whole, which is shorter than its diff:
```python
import functools

import jax
import jax.numpy as jnp
from jax import lax
from jax.experimental import pallas as pl
from jax.experimental.pallas import tpu as pltpu
from jax.sharding import PartitionSpec as P

bf16 = jnp.bfloat16
f32 = jnp.float32
VMEM = pl.BlockSpec(memory_space=pltpu.VMEM)
SMEM = pl.BlockSpec(memory_space=pltpu.SMEM)
MIB = 1024 * 1024


def like(*shape, dtype=bf16):
    return jax.ShapeDtypeStruct(shape, dtype)


def local_kernel(body, outs, *operands, limit=16, in_specs=None, scratch=(), flops=0, touched=0):
    return pl.pallas_call(
        body,
        out_shape=outs,
        in_specs=in_specs or [VMEM] * len(operands),
        out_specs=jax.tree.map(lambda _: VMEM, outs),
        scratch_shapes=scratch,
        compiler_params=pltpu.CompilerParams(vmem_limit_bytes=limit * MIB),
        cost_estimate=pl.CostEstimate(flops=flops, bytes_accessed=touched, transcendentals=0),
    )(*operands)


def over_tensor(shard, move):
    return lax.ppermute(shard, "tensor", [(i, move(i)) for i in range(lax.axis_size("tensor"))])


def other_core(i):
    return i ^ 1


def other_z(i):
    return i ^ 2


def along_y(i, sign=1):
    step = sign * (1 if i % 2 == 0 else -1)
    return (i // 4 + step) % 4 * 4 + i % 4


def back_y(i):
    return along_y(i, -1)


def join(*pieces):
    rows = [p.shape[0] for p in pieces]

    def body(*refs):
        out, at = refs[-1], 0
        for ref, n in zip(refs[:-1], rows):
            out[at : at + n] = ref[...]
            at += n

    return local_kernel(body, like(sum(rows), pieces[0].shape[1]), *pieces)


def norm_kernel(pick, codes, scales, parked, gain, normed, unit, inv):
    d = codes.shape[-1]

    def rows(which, scale):
        x = which.astype(f32) * scale.astype(f32)[:, :1]
        inv_rms = lax.rsqrt(jnp.mean(x * x, axis=-1, keepdims=True) + 1e-05)
        u = x * inv_rms
        unit[...] = u
        inv[...] = jnp.broadcast_to(inv_rms, inv.shape)
        normed[...] = (u * gain[...]).astype(bf16)

    @pl.when(pick[0] == 0)
    def _():
        rows(codes[0], scales[0])

    @pl.when(pick[0] == 1)
    def _():
        rows(codes[1], scales[1])

    @pl.when(pick[0] == 2)
    def _():
        rows(parked[:, :d], parked[:, d:])


def gather_normed(own):
    from_z = over_tensor(own, other_z)
    mine = join(own, from_z)
    chip = join(mine, over_tensor(mine, other_core))
    ahead = over_tensor(chip, along_y)
    behind = over_tensor(ahead, other_core)
    far = over_tensor(ahead[:64], along_y)
    far_other = over_tensor(far, other_core)
    return chip, ahead, behind, far, far_other


def gather_cot(own):
    other = over_tensor(own, other_core)
    ahead = over_tensor(join(own, other), along_y)
    far = over_tensor(ahead[:32], along_y)
    from_z = over_tensor(join(own, ahead, far), other_z)
    return own, other, ahead, far, from_z, over_tensor(join(ahead, far), other_core), over_tensor(from_z, other_core)


def dh_kernel(own, other, ahead, far, from_z, swapped, swapped_z, w_down, dh, rows):
    at = 0

    def put(ref, k):
        nonlocal at
        rows[at : at + 32] = ref[32 * k : 32 * k + 32]
        at += 32

    for block in (own, (ahead, 0), (ahead, 1), far):
        ref, k = block if isinstance(block, tuple) else (block, 0)
        put(ref, k)
        put(from_z, at // 64)
    for ref, k in ((other, 0), (swapped, 0), (swapped, 1), (swapped, 2)):
        put(ref, k)
        put(swapped_z, (at - 256) // 64)
    dh[...] = lax.dot_general(rows[...], w_down[...], (((1,), (1,)), ((), ())), preferred_element_type=f32)


def hidden_kernel(blocks, *refs):
    pieces, (dh, w_gate, w_up, dgate, dup, rows) = refs[:-6], refs[-6:]
    for (piece, start, count, at, dh_at) in blocks:
        rows[at : at + count] = pieces[piece][start : start + count]
    gate = jnp.dot(rows[...], w_gate[...], preferred_element_type=f32)
    up = jnp.dot(rows[...], w_up[...], preferred_element_type=f32)
    for (piece, start, count, at, dh_at) in blocks:
        g, u, d = gate[at : at + count], up[at : at + count], dh[dh_at : dh_at + count]
        sig = jax.nn.sigmoid(g)
        dgate[at : at + count] = (d * u * sig * (1.0 + g * (1.0 - sig))).astype(bf16)
        dup[at : at + count] = (d * g * sig).astype(bf16)


def back_kernel(half, near_g, near_u, far_g, far_u, w_gate, w_up, keep, send, g_rows, u_rows):
    for rows, near, far in ((g_rows, near_g, far_g), (u_rows, near_u, far_u)):
        rows[0:192] = near[0:192]
        rows[192:256] = far[0:64]
        rows[256:448] = near[192:384]
        rows[448:512] = far[64:128]
    n = keep.shape[1]
    cols = slice(half * n, half * n + n)
    transposed = (((1,), (1,)), ((), ()))
    dn = lax.dot_general(g_rows[...], w_gate[cols, :], transposed, preferred_element_type=f32) + lax.dot_general(
        u_rows[...], w_up[cols, :], transposed, preferred_element_type=f32
    )
    keep[...] = dn[:256].astype(bf16)
    send[...] = dn[256:].astype(bf16)


def add(*pieces, spans, rows):
    def body(*refs):
        for at, count, terms in spans:
            total = None
            for piece, start in terms:
                term = refs[piece][start : start + count].astype(f32)
                total = term if total is None else total + term
            refs[-1][at : at + count] = total.astype(bf16)

    return local_kernel(body, like(rows, pieces[0].shape[1]), *pieces)


def scatter_y_first(keep, send):
    got = over_tensor(send, other_core)
    far = add(keep, got, spans=[(0, 64, ((0, 192), (1, 192)))], rows=64)
    far_got = over_tensor(far, back_y)
    ahead = add(keep, got, far_got, spans=[(0, 64, ((0, 64), (1, 64), (2, 0))), (64, 64, ((0, 128), (1, 128)))], rows=128)
    home = over_tensor(ahead, back_y)
    home_other = over_tensor(home[64:], other_core)
    total = add(keep, got, home, home_other, spans=[(0, 64, ((0, 0), (1, 0), (2, 0), (3, 0)))], rows=64)
    return total, over_tensor(total[32:], other_z)


def scatter_z_first(keep, send):
    got = over_tensor(send, other_core)
    away = add(keep, got, spans=[(32 * b, 32, ((0, 64 * b + 32), (1, 64 * b + 32))) for b in range(4)], rows=128)
    from_z = over_tensor(away, other_z)
    held = add(keep, got, from_z, spans=[(32 * b, 32, ((0, 64 * b), (1, 64 * b), (2, 32 * b))) for b in range(4)], rows=128)
    far_got = over_tensor(held[96:], back_y)
    ahead = add(held, far_got, spans=[(0, 32, ((0, 32), (1, 0))), (32, 32, ((0, 64),))], rows=64)
    home = over_tensor(ahead, back_y)
    return held, home, over_tensor(home[32:], other_core)


def final_kernel(total, from_z, held, home, home_other, cot, unit, inv, gain, out):
    half = total.shape[1]
    dn_a = total[:32].astype(f32) + from_z[...].astype(f32)
    dn_b = held[:32].astype(f32) + home[:32].astype(f32) + home_other[...].astype(f32)
    g_a, g_b = dn_a * gain[:, :half], dn_b * gain[:, half:]
    u_a, u_b = unit[:, :half], unit[:, half:]
    mean = (
        jnp.sum(g_a * u_a, axis=-1, keepdims=True) + jnp.sum(g_b * u_b, axis=-1, keepdims=True)
    ) / (2 * half)
    scale = inv[:, :1]
    out[:, :half] = (cot[:, :half].astype(f32) + scale * (g_a - u_a * mean)).astype(bf16)
    out[:, half:] = (cot[:, half:].astype(f32) + scale * (g_b - u_b * mean)).astype(bf16)


def on_device(
    local_codes,
    local_scales,
    parked_codes,
    parked_scales,
    keep_count,
    roster,
    norm_gain,
    w_gate,
    w_up,
    w_down,
    pending,
):
    sections = lax.axis_size("section")
    mine = lax.axis_index("section")
    _, _, shard, d = local_codes.shape
    hidden = w_gate.shape[2]
    rows = 16 * shard

    cot = lax.ppermute(pending[0], "section", [((i + 1) % sections, i) for i in range(sections)])
    mirror = sections - 1 - mine
    asked = jnp.clip(roster[mirror] - keep_count[mirror], 0, 1)
    payload = jnp.concatenate(
        [
            lax.dynamic_index_in_dim(parked_codes[0], asked, 0, keepdims=False),
            jnp.broadcast_to(lax.dynamic_index_in_dim(parked_scales[0], asked, 0, keepdims=False)[:, None], (shard, 128)),
        ],
        axis=1,
    )
    fetched = lax.ppermute(payload, "section", [(sections - 1 - i, i) for i in range(sections // 2)])
    is_parked = roster[mine] >= keep_count[mine]
    pick = jnp.where(is_parked, 2, jnp.clip(roster[mine], 0, 1)).astype(jnp.int32)[None]

    gain = norm_gain
    normed, unit, inv = local_kernel(
        norm_kernel,
        (like(shard, d), like(shard, d, dtype=f32), like(shard, 128, dtype=f32)),
        pick,
        local_codes[0],
        jnp.broadcast_to(local_scales[0][:, :, None], (2, shard, 128)),
        fetched,
        gain,
        in_specs=[SMEM] + [VMEM] * 4,
    )

    cots = gather_cot(cot)
    chip, ahead, behind, far, far_other = gather_normed(normed)

    dh = local_kernel(
        dh_kernel,
        like(rows, hidden, dtype=f32),
        *cots,
        w_down[0],
        limit=26,
        scratch=[pltpu.VMEM((rows, d), bf16)],
        flops=2 * rows * d * hidden,
    )
    near_blocks = ((0, 0, 64, 0, 0), (1, 0, 128, 64, 64), (0, 64, 64, 192, 256), (2, 0, 128, 256, 320))
    far_blocks = ((0, 0, 64, 0, 192), (1, 0, 64, 64, 448))
    near_g, near_u = local_kernel(
        functools.partial(hidden_kernel, near_blocks),
        (like(384, hidden), like(384, hidden)),
        chip,
        ahead,
        behind,
        dh,
        w_gate[0],
        w_up[0],
        limit=34,
        scratch=[pltpu.VMEM((384, d), bf16)],
        flops=4 * 384 * d * hidden,
    )
    far_g, far_u = local_kernel(
        functools.partial(hidden_kernel, far_blocks),
        (like(128, hidden), like(128, hidden)),
        far,
        far_other,
        dh,
        w_gate[0],
        w_up[0],
        limit=34,
        scratch=[pltpu.VMEM((128, d), bf16)],
        flops=4 * 128 * d * hidden,
    )

    def back(half):
        return local_kernel(
            functools.partial(back_kernel, half),
            (like(256, d // 2), like(256, d // 2)),
            near_g,
            near_u,
            far_g,
            far_u,
            w_gate[0],
            w_up[0],
            limit=34,
            scratch=[pltpu.VMEM((rows, hidden), bf16)] * 2,
            flops=2 * rows * d * hidden,
        )

    held, home, home_other = scatter_z_first(*back(1))
    total, from_z = scatter_y_first(*back(0))
    return local_kernel(
        final_kernel, like(shard, d), total, from_z, held, home, home_other, cot, unit, inv, gain
    )[None]


def solution(mesh):
    placed = (
        P("section", None, "tensor", None),
        P("section", None, "tensor"),
        P("section", None, "tensor", None),
        P("section", None, "tensor"),
        P(),
        P(),
        P("section", None),
        P("section", None, "tensor"),
        P("section", None, "tensor"),
        P("section", "tensor", None),
        P("section", "tensor", None),
    )
    return jax.shard_map(
        on_device,
        mesh=mesh,
        in_specs=placed,
        out_specs=P("section", "tensor", None),
        check_vma=False,
    )
```

time: 258 us -> 145 us (0.56)
  waiting for transfers between devices: 162 us -> 77.8 us
  matrix products: 53.6 us -> 0 us
  Pallas kernels: 0 us -> 28.3 us
  between operations: 16.5 us -> 3.52 us
  starting transfers between devices: 16 us -> 27 us
  other arithmetic: 6.71 us -> 0.02 us
  local copies, waits for them, and re-layouts: 3.27 us -> 7.86 us
    reduce_scatter x1 -> x0, waiting for transfers between devices: 96.7 us -> none  [on_device(): lax.psum_scatter(lax.dot_general(dgate, gate_w, (((1,), (1,)), ((), ())),...]
    dot_general x4 -> x0, matrix products: 53.6 us -> none  [the longest x1 19.2 us: on_device(): lax.dot_general(dgate, gate_w, (((1,), (1,)), ((), ())), preferred_elemen...]
    ppermute x7 -> x24, waiting for transfers between devices: 38.8 us -> 77.8 us  [the longest x22 65 us: over_tensor(): lax.ppermute(shard, 'tensor', [(i, move(i)) for i in range(lax.axis_size(...]
    pallas_call x0 -> x18, Pallas kernels: none -> 28.3 us  [local_kernel(): pl.pallas_call(body, out_shape=outs, in_specs=in_specs or [VMEM] * len(op...]
    all_gather x2 -> x0, waiting for transfers between devices: 26.1 us -> none  [the longest x1 26.1 us: on_device(): piece = lax.all_gather(normed, 'tensor', axis=0, tiled=True)]
    ppermute x7 -> x24, starting transfers between devices: 15.9 us -> 27 us  [the longest x22 19.1 us: over_tensor(): lax.ppermute(shard, 'tensor', [(i, move(i)) for i in range(lax.axis_size(...]
    unnamed x6 -> x20, local copies, waits for them, and re-layouts: 0.71 us -> 4.88 us
  transfers between devices with their start and end apart: 10 -> 24, of which waited for: 7 -> 13; matrix products, arithmetic and copies ran while one was open for 6% -> 2% of each run, Pallas kernels for 0% -> 9%
where the time goes in v1:
time: 145 us
  waiting for transfers between devices  77.8 us (54%)
  Pallas kernels  28.3 us (20%)
  starting transfers between devices  27 us (19%)
  local copies, waits for them, and re-layouts  7.86 us (5%)
  between operations  3.52 us (2%)
    ppermute x22, waiting for transfers between devices, over_tensor(): lax.ppermute(shard, 'tensor', [(i, move(i)) for i in range(lax.axis_size(...  65 us
    pallas_call x18, Pallas kernels, local_kernel(): pl.pallas_call(body, out_shape=outs, in_specs=in_specs or [VMEM] * len(op...  28.3 us
    ppermute x22, starting transfers between devices, over_tensor(): lax.ppermute(shard, 'tensor', [(i, move(i)) for i in range(lax.axis_size(...  19.1 us
    ppermute x1, waiting for transfers between devices, on_device(): lax.ppermute(payload, 'section', [(sections - 1 - i, i) for i in range(se...  10.2 us
    ppermute x1, starting transfers between devices, on_device(): lax.ppermute(pending[0], 'section', [((i + 1) % sections, i) for i in ran...  6.62 us
    unnamed x20, local copies, waits for them, and re-layouts  4.88 us
  transfers between devices with their start and end apart: 24, of which 13 were waited for; matrix products, arithmetic and copies ran while one was open for 2% of the time, Pallas kernels for 9%

profile of v1, /device:TPU:1, one launch (start us, length us, event | category | flops | bytes accessed | tf_op | source)
XLA Modules:
  0.0 144.5 jit_solution(15642555504356107058)
XLA Ops:
  0.0 6.6 %collective-permute-start.5 = (bf16[32,4096]{1,0:T(8,128)(2,1)}, bf16[32,4096]{1,0:T(8,128)(2,1)S(1)}, u32[]{:S(2)}, u32[]{:S(2)}) collective-permute-start(bf16[32,4096]{1,0:T(8,128)(2,1)} %bitcast.27), channel_id=1, source_target_pairs={{16,0},{32,16},{48,32},{64,48},{80,64},{96,80},{112,96},{0,112},{1... | collective-permute-start | bytes 786440 | tf_op jit(solution)/shard_map/ppermute | solution.py:223
  6.6 1.4 fusion
  9.3 2.6 %collective-permute-done.5.refs_0_.own.cot = bf16[32,4096]{1,0:T(8,128)(2,1)S(1)} collective-permute-done((bf16[32,4096]{1,0:T(8,128)(2,1)}, bf16[32,4096]{1,0:T(8,128)(2,1)S(1)}, u32[]{:S(2)}, u32[]{:S(2)}) %collective-permute-start.5) | collective-permute-done | bytes 262176 | tf_op jit(solution)/shard_map/ppermute | solution.py:223
  11.9 1.5 %collective-permute-start.6 = (bf16[32,4096]{1,0:T(8,128)(2,1)S(1)}, bf16[32,4096]{1,0:T(8,128)(2,1)S(1)}, u32[]{:S(2)}, u32[]{:S(2)}) collective-permute-start(bf16[32,4096]{1,0:T(8,128)(2,1)S(1)} %collective-permute-done.5.refs_0_.own.cot), channel_id=1, source_target_pairs={{0,1},{1,0},{2,3},{3,2},{4,5},{5,4},{6,7},{7,6},{8,9},{9,8},{10,11... | collective-permute-start | bytes 786440 | tf_op jit(solution)/shard_map/ppermute | solution.py:34
  14.7 2.8 %collective-permute-start.7 = (bf16[64,4096]{1,0:T(8,128)(2,1)S(1)}, bf16[64,4096]{1,0:T(8,128)(2,1)S(1)}, u32[]{:S(2)}, u32[]{:S(2)}) collective-permute-start(bf16[64,4096]{1,0:T(8,128)(2,1)S(1)} %shard_map.112), channel_id=1, source_target_pairs={{0,4},{1,13},{2,6},{3,15},{4,8},{5,1},{6,10},{7,3},{8,12},{9,5},{1... | collective-permute-start | bytes 1572872 | tf_op jit(solution)/shard_map/ppermute | solution.py:34
  17.6 1.3 collective-permute-start
  20.7 10.2 %collective-permute-done.parked = bf16[32,4224]{1,0:T(8,128)(2,1)S(1)} collective-permute-done((bf16[32,4224]{1,0:T(8,128)(2,1)S(1)}, bf16[32,4224]{1,0:T(8,128)(2,1)S(1)}, u32[]{:S(2)}, u32[]{:S(2)}) %collective-permute-start) | collective-permute-done | bytes 270368 | tf_op jit(solution)/shard_map/ppermute | solution.py:233
  31.7 1.0 copy-done.2
  33.7 0.8 collective-permute-start.1
  35.2 6.1 %collective-permute-done.1.refs_1_ = bf16[32,4096]{1,0:T(8,128)(2,1)S(1)} collective-permute-done((bf16[32,4096]{1,0:T(8,128)(2,1)S(1)}, bf16[32,4096]{1,0:T(8,128)(2,1)S(1)}, u32[]{:S(2)}, u32[]{:S(2)}) %collective-permute-start.1) | collective-permute-done | bytes 262176 | tf_op jit(solution)/shard_map/ppermute | solution.py:34
  41.4 1.3 collective-permute-start.2
  42.7 0.8 collective-permute-start.9
  44.9 22.5 %collective-permute-done.9.from_z = bf16[128,4096]{1,0:T(8,128)(2,1)S(1)} collective-permute-done((bf16[128,4096]{1,0:T(8,128)(2,1)S(1)}, bf16[128,4096]{1,0:T(8,128)(2,1)S(1)}, u32[]{:S(2)}, u32[]{:S(2)}) %collective-permute-start.9) | collective-permute-done | bytes 1048608 | tf_op jit(solution)/shard_map/ppermute | solution.py:34
  67.4 1.0 collective-permute-start.11
  69.2 7.7 %collective-permute-done.12.refs_0_ = bf16[64,4096]{1,0:T(8,128)(2,1)S(1)} collective-permute-done((bf16[64,4096]{1,0:T(8,128)(2,1)S(1)}, bf16[64,4096]{1,0:T(8,128)(2,1)S(1)}, u32[]{:S(2)}, u32[]{:S(2)}) %collective-permute-start.12) | collective-permute-done | bytes 524320 | tf_op jit(solution)/shard_map/ppermute | solution.py:34
  77.0 2.6 %collective-permute-start.13 = (bf16[64,4096]{1,0:T(8,128)(2,1)S(1)}, bf16[64,4096]{1,0:T(8,128)(2,1)S(1)}, u32[]{:S(2)}, u32[]{:S(2)}) collective-permute-start(bf16[64,4096]{1,0:T(8,128)(2,1)S(1)} %collective-permute-done.12.refs_0_), channel_id=1, source_target_pairs={{0,1},{1,0},{2,3},{3,2},{4,5},{5,4},{6,7},{7,6},{8,9},{9,8},{10,11... | collective-permute-start | bytes 1572872 | tf_op jit(solution)/shard_map/ppermute | solution.py:34
  79.6 4.5 %shard_map.115.refs_3_.refs_2_ = f32[512,896]{1,0:T(8,128)S(1)} custom-call(bf16[32,4096]{1,0:T(8,128)(2,1)S(1)} %collective-permute-done.5.refs_0_.own.cot, bf16[32,4096]{1,0:T(8,128)(2,1)S(1)} %collective-permute-done.6.refs_1_.other, bf16[64,4096]{1,0:T(8,128)(2,1)S(1)} %collective-permute-done.7.refs_1_.refs_0_.ahead, ...), custom_call_target="tpu_custom_call" | custom-call | flops 3758096384 | tf_op jit(solution)/shard_map/pallas_call | solution.py:22
  84.2 2.4 %shard_map.117 = (bf16[128,896]{1,0:T(8,128)(2,1)S(1)}, bf16[128,896]{1,0:T(8,128)(2,1)S(1)}) custom-call(bf16[64,4096]{1,0:T(8,128)(2,1)S(1)} %collective-permute-done.12.refs_0_, bf16[64,4096]{1,0:T(8,128)(2,1)S(1)} %collective-permute-done.13.refs_1_, f32[512,896]{1,0:T(8,128)S(1)} %shard_map.115.refs_3_.refs_2_, bf16[4096,896]{1,0:T(8,128)(2,1)S(1)} %bitcast.14, ...), custom_call_target="tpu_custom_call" | custom-call | flops 1879048192 | tf_op jit(solution)/shard_map/pallas_call | solution.py:22
  86.6 9.9 %shard_map.116 = (bf16[384,896]{1,0:T(8,128)(2,1)S(1)}, bf16[384,896]{1,0:T(8,128)(2,1)S(1)}) custom-call(bf16[128,4096]{1,0:T(8,128)(2,1)S(1)} %shard_map.111.refs_0_, bf16[128,4096]{1,0:T(8,128)(2,1)S(1)} %collective-permute-done.3.refs_1_, bf16[128,4096]{1,0:T(8,128)(2,1)S(1)} %collective-permute-done.4.refs_2_, ...), custom_call_target="tpu_custom_call" | custom-call | flops 5637144576 | tf_op jit(solution)/shard_map/pallas_call | solution.py:22
  96.5 3.1 %copy-done.1 = bf16[1,4096,896]{2,1,0:T(8,128)(2,1)S(1)} copy-done((bf16[1,4096,896]{2,1,0:T(8,128)(2,1)S(1)}, bf16[1,4096,896]{2,1,0:T(8,128)(2,1)}, u32[]{:S(2)}) %copy-start.1) | copy-done | bytes 7340056
  99.6 4.7 %shard_map.118 = (bf16[256,2048]{1,0:T(8,128)(2,1)S(1)}, bf16[256,2048]{1,0:T(8,128)(2,1)S(1)}) custom-call(bf16[384,896]{1,0:T(8,128)(2,1)S(1)} %get-tuple-element.17.near_g, bf16[384,896]{1,0:T(8,128)(2,1)S(1)} %get-tuple-element.18.near_u, bf16[128,896]{1,0:T(8,128)(2,1)S(1)} %get-tuple-element.19.far_g, bf16[128,896]{1,0:T(8,128)(2,1)S(1)} %get-tuple-element.20.far_u, ...), custom_call_target="tpu_custom_call" | custom-call | flops 3758096384 | tf_op jit(solution)/shard_map/pallas_call | solution.py:22
  104.4 4.5 %shard_map.122 = (bf16[256,2048]{1,0:T(8,128)(2,1)S(1)}, bf16[256,2048]{1,0:T(8,128)(2,1)S(1)}) custom-call(bf16[384,896]{1,0:T(8,128)(2,1)S(1)} %get-tuple-element.17.near_g, bf16[384,896]{1,0:T(8,128)(2,1)S(1)} %get-tuple-element.18.near_u, bf16[128,896]{1,0:T(8,128)(2,1)S(1)} %get-tuple-element.19.far_g, bf16[128,896]{1,0:T(8,128)(2,1)S(1)} %get-tuple-element.20.far_u, ...), custom_call_target="tpu_custom_call" | custom-call | flops 3758096384 | tf_op jit(solution)/shard_map/pallas_call | solution.py:22
  109.7 2.1 %collective-permute-done.19.refs_1_ = bf16[256,2048]{1,0:T(8,128)(2,1)S(1)} collective-permute-done((bf16[256,2048]{1,0:T(8,128)(2,1)S(1)}, bf16[256,2048]{1,0:T(8,128)(2,1)S(1)}, u32[]{:S(2)}, u32[]{:S(2)}) %collective-permute-start.19) | collective-permute-done | bytes 1048608 | tf_op jit(solution)/shard_map/ppermute | solution.py:34
  111.9 0.8 collective-permute-start.20
  112.7 3.4 %collective-permute-done.15.refs_2_ = bf16[64,2048]{1,0:T(8,128)(2,1)S(1)} collective-permute-done((bf16[64,2048]{1,0:T(8,128)(2,1)S(1)}, bf16[64,2048]{1,0:T(8,128)(2,1)S(1)}, u32[]{:S(2)}, u32[]{:S(2)}) %collective-permute-start.15) | collective-permute-done | bytes 262176 | tf_op jit(solution)/shard_map/ppermute | solution.py:34
  116.4 8.8 %collective-permute-done.20.refs_2_ = bf16[128,2048]{1,0:T(8,128)(2,1)S(1)} collective-permute-done((bf16[128,2048]{1,0:T(8,128)(2,1)S(1)}, bf16[128,2048]{1,0:T(8,128)(2,1)S(1)}, u32[]{:S(2)}, u32[]{:S(2)}) %collective-permute-start.20) | collective-permute-done | bytes 524320 | tf_op jit(solution)/shard_map/ppermute | solution.py:34
  125.5 5.0 %collective-permute-done.21.refs_1_ = bf16[32,2048]{1,0:T(8,128)(2,1)S(1)} collective-permute-done((bf16[32,2048]{1,0:T(8,128)(2,1)S(1)}, bf16[32,2048]{1,0:T(8,128)(2,1)S(1)}, u32[]{:S(2)}, u32[]{:S(2)}) %collective-permute-start.21) | collective-permute-done | bytes 131104 | tf_op jit(solution)/shard_map/ppermute | solution.py:34
  130.6 2.6 %collective-permute-start.17 = (bf16[64,2048]{1,0:T(8,128)(2,1)S(1)}, bf16[64,2048]{1,0:T(8,128)(2,1)S(1)}, u32[]{:S(2)}, u32[]{:S(2)}) collective-permute-start(bf16[64,2048]{1,0:T(8,128)(2,1)S(1)} %slice.26), channel_id=1, source_target_pairs={{0,1},{1,0},{2,3},{3,2},{4,5},{5,4},{6,7},{7,6},{8,9},{9,8},{10,11... | collective-permute-start | bytes 786440 | tf_op jit(solution)/shard_map/ppermute | solution.py:34
  133.2 3.8 %collective-permute-done.22.home = bf16[64,2048]{1,0:T(8,128)(2,1)S(1)} collective-permute-done((bf16[64,2048]{1,0:T(8,128)(2,1)S(1)}, bf16[64,2048]{1,0:T(8,128)(2,1)S(1)}, u32[]{:S(2)}, u32[]{:S(2)}) %collective-permute-start.22) | collective-permute-done | bytes 262176 | tf_op jit(solution)/shard_map/ppermute | solution.py:34
  137.0 1.2 collective-permute-start.23
  139.2 4.4 %collective-permute-done.18.from_z = bf16[32,2048]{1,0:T(8,128)(2,1)S(1)} collective-permute-done((bf16[32,2048]{1,0:T(8,128)(2,1)S(1)}, bf16[32,2048]{1,0:T(8,128)(2,1)S(1)}, u32[]{:S(2)}, u32[]{:S(2)}) %collective-permute-start.18) | collective-permute-done | bytes 131104 | tf_op jit(solution)/shard_map/ppermute | solution.py:34
  143.5 1.0 shard_map.126
  (68 shorter events, 8.5 us)
Async XLA Ops:
  0.0 13.5 %copy-start = (bf16[1,2,32,4096]{3,2,1,0:T(8,128)(2,1)S(1)}, bf16[1,2,32,4096]{3,2,1,0:T(8,128)(2,1)}, u32[]{:S(2)}) copy-start(bf16[1,2,32,4096]{3,2,1,0:T(8,128)(2,1)} %param.13) | copy-start | bytes 1572868
  0.0 11.9 %collective-permute-start.5 = (bf16[32,4096]{1,0:T(8,128)(2,1)}, bf16[32,4096]{1,0:T(8,128)(2,1)S(1)}, u32[]{:S(2)}, u32[]{:S(2)}) collective-permute-start(bf16[32,4096]{1,0:T(8,128)(2,1)} %bitcast.27), channel_id=1, source_target_pairs={{16,0},{32,16},{48,32},{64,48},{80,64},{96,80},{112,96},{0,112},{1... | collective-permute-start | bytes 786440 | tf_op jit(solution)/shard_map/ppermute | solution.py:223
  11.9 2.7 %collective-permute-start.6 = (bf16[32,4096]{1,0:T(8,128)(2,1)S(1)}, bf16[32,4096]{1,0:T(8,128)(2,1)S(1)}, u32[]{:S(2)}, u32[]{:S(2)}) collective-permute-start(bf16[32,4096]{1,0:T(8,128)(2,1)S(1)} %collective-permute-done.5.refs_0_.own.cot), channel_id=1, source_target_pairs={{0,1},{1,0},{2,3},{3,2},{4,5},{5,4},{6,7},{7,6},{8,9},{9,8},{10,11... | collective-permute-start | bytes 786440 | tf_op jit(solution)/shard_map/ppermute | solution.py:34
  14.7 19.9 %collective-permute-start.7 = (bf16[64,4096]{1,0:T(8,128)(2,1)S(1)}, bf16[64,4096]{1,0:T(8,128)(2,1)S(1)}, u32[]{:S(2)}, u32[]{:S(2)}) collective-permute-start(bf16[64,4096]{1,0:T(8,128)(2,1)S(1)} %shard_map.112), channel_id=1, source_target_pairs={{0,4},{1,13},{2,6},{3,15},{4,8},{5,1},{6,10},{7,3},{8,12},{9,5},{1... | collective-permute-start | bytes 1572872 | tf_op jit(solution)/shard_map/ppermute | solution.py:34
  17.6 13.4 %collective-permute-start = (bf16[32,4224]{1,0:T(8,128)(2,1)S(1)}, bf16[32,4224]{1,0:T(8,128)(2,1)S(1)}, u32[]{:S(2)}, u32[]{:S(2)}) collective-permute-start(bf16[32,4224]{1,0:T(8,128)(2,1)S(1)} %pad_maximum_fusion), channel_id=1, source_target_pairs={{112,0},{96,16},{80,32},{64,48},{113,1},{97,17},{81,33},{65,49},{1... | collective-permute-start | bytes 811016 | tf_op jit(solution)/shard_map/ppermute | solution.py:233
  33.4 46.1 %copy-start.5 = (bf16[1,896,4096]{2,1,0:T(8,128)(2,1)S(1)}, bf16[1,896,4096]{2,1,0:T(8,128)(2,1)}, u32[]{:S(2)}) copy-start(bf16[1,896,4096]{2,1,0:T(8,128)(2,1)} %param.20) | copy-start | bytes 22020100
  33.7 7.6 %collective-permute-start.1 = (bf16[32,4096]{1,0:T(8,128)(2,1)S(1)}, bf16[32,4096]{1,0:T(8,128)(2,1)S(1)}, u32[]{:S(2)}, u32[]{:S(2)}) collective-permute-start(bf16[32,4096]{1,0:T(8,128)(2,1)S(1)} %get-tuple-element.16.refs_0_), channel_id=1, source_target_pairs={{0,2},{1,3},{2,0},{3,1},{4,6},{5,7},{6,4},{7,5},{8,10},{9,11},{10,... | collective-permute-start | bytes 786440 | tf_op jit(solution)/shard_map/ppermute | solution.py:34
  34.6 8.1 %collective-permute-start.8 = (bf16[32,4096]{1,0:T(8,128)(2,1)S(1)}, bf16[32,4096]{1,0:T(8,128)(2,1)S(1)}, u32[]{:S(2)}, u32[]{:S(2)}) collective-permute-start(bf16[32,4096]{1,0:T(8,128)(2,1)S(1)} %slice.24), channel_id=1, source_target_pairs={{0,4},{1,13},{2,6},{3,15},{4,8},{5,1},{6,10},{7,3},{8,12},{9,5},{1... | collective-permute-start | bytes 786440 | tf_op jit(solution)/shard_map/ppermute | solution.py:34
  41.4 2.8 %collective-permute-start.2 = (bf16[64,4096]{1,0:T(8,128)(2,1)S(1)}, bf16[64,4096]{1,0:T(8,128)(2,1)S(1)}, u32[]{:S(2)}, u32[]{:S(2)}) collective-permute-start(bf16[64,4096]{1,0:T(8,128)(2,1)S(1)} %shard_map.110.refs_0_), channel_id=1, source_target_pairs={{0,1},{1,0},{2,3},{3,2},{4,5},{5,4},{6,7},{7,6},{8,9},{9,8},{10,11... | collective-permute-start | bytes 1572872 | tf_op jit(solution)/shard_map/ppermute | solution.py:34
  42.6 41.5 %slice-start.2 = ((s8[7340032]{0:T(1024)(128)(4,1)}), s8[4194304]{0:T(1024)(128)(4,1)S(1)}, s32[]{:S(2)}) async-start(s8[7340032]{0:T(1024)(128)(4,1)} %bitcast.19), calls=%async_computation.2 | async-start | bytes 8388608
  42.7 24.6 %collective-permute-start.9 = (bf16[128,4096]{1,0:T(8,128)(2,1)S(1)}, bf16[128,4096]{1,0:T(8,128)(2,1)S(1)}, u32[]{:S(2)}, u32[]{:S(2)}) collective-permute-start(bf16[128,4096]{1,0:T(8,128)(2,1)S(1)} %shard_map.113), channel_id=1, source_target_pairs={{0,2},{1,3},{2,0},{3,1},{4,6},{5,7},{6,4},{7,5},{8,10},{9,11},{10,... | collective-permute-start | bytes 3145736 | tf_op jit(solution)/shard_map/ppermute | solution.py:34
  44.2 24.3 %collective-permute-start.3 = (bf16[128,4096]{1,0:T(8,128)(2,1)S(1)}, bf16[128,4096]{1,0:T(8,128)(2,1)S(1)}, u32[]{:S(2)}, u32[]{:S(2)}) collective-permute-start(bf16[128,4096]{1,0:T(8,128)(2,1)S(1)} %shard_map.111.refs_0_), channel_id=1, source_target_pairs={{0,4},{1,13},{2,6},{3,15},{4,8},{5,1},{6,10},{7,3},{8,12},{9,5},{1... | collective-permute-start | bytes 3145736 | tf_op jit(solution)/shard_map/ppermute | solution.py:34
  67.4 12.2 %collective-permute-start.11 = (bf16[128,4096]{1,0:T(8,128)(2,1)S(1)}, bf16[128,4096]{1,0:T(8,128)(2,1)S(1)}, u32[]{:S(2)}, u32[]{:S(2)}) collective-permute-start(bf16[128,4096]{1,0:T(8,128)(2,1)S(1)} %collective-permute-done.9.from_z), channel_id=1, source_target_pairs={{0,1},{1,0},{2,3},{3,2},{4,5},{5,4},{6,7},{7,6},{8,9},{9,8},{10,11... | collective-permute-start | bytes 3145736 | tf_op jit(solution)/shard_map/ppermute | solution.py:34
  68.4 15.7 %slice-start = ((s8[7340032]{0:T(1024)(128)(4,1)}), s8[4194304]{0:T(1024)(128)(4,1)S(1)}, s32[]{:S(2)}) async-start(s8[7340032]{0:T(1024)(128)(4,1)} %bitcast.12), calls=%async_computation | async-start | bytes 8388608
  68.4 11.1 %collective-permute-start.10 = (bf16[96,4096]{1,0:T(8,128)(2,1)S(1)}, bf16[96,4096]{1,0:T(8,128)(2,1)S(1)}, u32[]{:S(2)}, u32[]{:S(2)}) collective-permute-start(bf16[96,4096]{1,0:T(8,128)(2,1)S(1)} %shard_map.114), channel_id=1, source_target_pairs={{0,1},{1,0},{2,3},{3,2},{4,5},{5,4},{6,7},{7,6},{8,9},{9,8},{10,11... | collective-permute-start | bytes 2359304 | tf_op jit(solution)/shard_map/ppermute | solution.py:34
  68.6 8.4 %collective-permute-start.12 = (bf16[64,4096]{1,0:T(8,128)(2,1)S(1)}, bf16[64,4096]{1,0:T(8,128)(2,1)S(1)}, u32[]{:S(2)}, u32[]{:S(2)}) collective-permute-start(bf16[64,4096]{1,0:T(8,128)(2,1)S(1)} %slice.25), channel_id=1, source_target_pairs={{0,4},{1,13},{2,6},{3,15},{4,8},{5,1},{6,10},{7,3},{8,12},{9,5},{1... | collective-permute-start | bytes 1572872 | tf_op jit(solution)/shard_map/ppermute | solution.py:34
  69.2 17.4 %collective-permute-start.4 = (bf16[128,4096]{1,0:T(8,128)(2,1)S(1)}, bf16[128,4096]{1,0:T(8,128)(2,1)S(1)}, u32[]{:S(2)}, u32[]{:S(2)}) collective-permute-start(bf16[128,4096]{1,0:T(8,128)(2,1)S(1)} %collective-permute-done.3.refs_1_), channel_id=1, source_target_pairs={{0,1},{1,0},{2,3},{3,2},{4,5},{5,4},{6,7},{7,6},{8,9},{9,8},{10,11... | collective-permute-start | bytes 3145736 | tf_op jit(solution)/shard_map/ppermute | solution.py:34
  77.0 7.1 %collective-permute-start.13 = (bf16[64,4096]{1,0:T(8,128)(2,1)S(1)}, bf16[64,4096]{1,0:T(8,128)(2,1)S(1)}, u32[]{:S(2)}, u32[]{:S(2)}) collective-permute-start(bf16[64,4096]{1,0:T(8,128)(2,1)S(1)} %collective-permute-done.12.refs_0_), channel_id=1, source_target_pairs={{0,1},{1,0},{2,3},{3,2},{4,5},{5,4},{6,7},{7,6},{8,9},{9,8},{10,11... | collective-permute-start | bytes 1572872 | tf_op jit(solution)/shard_map/ppermute | solution.py:34
  79.5 4.6 %slice-start.1 = ((s8[7340032]{0:T(1024)(128)(4,1)}), s8[3145728]{0:T(1024)(128)(4,1)S(1)}, s32[]{:S(2)}) async-start(s8[7340032]{0:T(1024)(128)(4,1)} %bitcast.12), calls=%async_computation.1 | async-start | bytes 6291456
  79.6 4.6 %slice-start.3 = ((s8[7340032]{0:T(1024)(128)(4,1)}), s8[3145728]{0:T(1024)(128)(4,1)S(1)}, s32[]{:S(2)}) async-start(s8[7340032]{0:T(1024)(128)(4,1)} %bitcast.19), calls=%async_computation.3 | async-start | bytes 6291456
  96.5 3.1 %copy-start.1 = (bf16[1,4096,896]{2,1,0:T(8,128)(2,1)S(1)}, bf16[1,4096,896]{2,1,0:T(8,128)(2,1)}, u32[]{:S(2)}) copy-start(bf16[1,4096,896]{2,1,0:T(8,128)(2,1)} %param.19) | copy-start | bytes 22020100
  104.3 5.2 %collective-permute-start.14 = (bf16[256,2048]{1,0:T(8,128)(2,1)S(1)}, bf16[256,2048]{1,0:T(8,128)(2,1)S(1)}, u32[]{:S(2)}, u32[]{:S(2)}) collective-permute-start(bf16[256,2048]{1,0:T(8,128)(2,1)S(1)} %get-tuple-element.22), channel_id=1, source_target_pairs={{0,1},{1,0},{2,3},{3,2},{4,5},{5,4},{6,7},{7,6},{8,9},{9,8},{10,11... | collective-permute-start | bytes 3145736 | tf_op jit(solution)/shard_map/ppermute | solution.py:34
  109.0 2.9 %collective-permute-start.19 = (bf16[256,2048]{1,0:T(8,128)(2,1)S(1)}, bf16[256,2048]{1,0:T(8,128)(2,1)S(1)}, u32[]{:S(2)}, u32[]{:S(2)}) collective-permute-start(bf16[256,2048]{1,0:T(8,128)(2,1)S(1)} %get-tuple-element.24), channel_id=1, source_target_pairs={{0,1},{1,0},{2,3},{3,2},{4,5},{5,4},{6,7},{7,6},{8,9},{9,8},{10,11... | collective-permute-start | bytes 3145736 | tf_op jit(solution)/shard_map/ppermute | solution.py:34
  109.6 33.9 %copy-start.4 = (f32[1,4096]{1,0:T(1,128)S(1)}, f32[1,4096]{1,0:T(1,128)}, u32[]{:S(2)}) copy-start(f32[1,4096]{1,0:T(1,128)} %gain.3) | copy-start | bytes 49156
  109.6 6.5 %collective-permute-start.15 = (bf16[64,2048]{1,0:T(8,128)(2,1)S(1)}, bf16[64,2048]{1,0:T(8,128)(2,1)S(1)}, u32[]{:S(2)}, u32[]{:S(2)}) collective-permute-start(bf16[64,2048]{1,0:T(8,128)(2,1)S(1)} %shard_map.119), channel_id=1, source_target_pairs={{0,12},{1,5},{2,14},{3,7},{4,0},{5,9},{6,2},{7,11},{8,4},{9,13},{1... | collective-permute-start | bytes 786440 | tf_op jit(solution)/shard_map/ppermute | solution.py:34
  111.9 13.2 %collective-permute-start.20 = (bf16[128,2048]{1,0:T(8,128)(2,1)S(1)}, bf16[128,2048]{1,0:T(8,128)(2,1)S(1)}, u32[]{:S(2)}, u32[]{:S(2)}) collective-permute-start(bf16[128,2048]{1,0:T(8,128)(2,1)S(1)} %shard_map.123), channel_id=1, source_target_pairs={{0,2},{1,3},{2,0},{3,1},{4,6},{5,7},{6,4},{7,5},{8,10},{9,11},{10,... | collective-permute-start | bytes 1572872 | tf_op jit(solution)/shard_map/ppermute | solution.py:34
  116.3 14.3 %collective-permute-start.16 = (bf16[128,2048]{1,0:T(8,128)(2,1)S(1)}, bf16[128,2048]{1,0:T(8,128)(2,1)S(1)}, u32[]{:S(2)}, u32[]{:S(2)}) collective-permute-start(bf16[128,2048]{1,0:T(8,128)(2,1)S(1)} %shard_map.120), channel_id=1, source_target_pairs={{0,12},{1,5},{2,14},{3,7},{4,0},{5,9},{6,2},{7,11},{8,4},{9,13},{1... | collective-permute-start | bytes 1572872 | tf_op jit(solution)/shard_map/ppermute | solution.py:34
  125.4 5.1 %collective-permute-start.21 = (bf16[32,2048]{1,0:T(8,128)(2,1)S(1)}, bf16[32,2048]{1,0:T(8,128)(2,1)S(1)}, u32[]{:S(2)}, u32[]{:S(2)}) collective-permute-start(bf16[32,2048]{1,0:T(8,128)(2,1)S(1)} %slice.28), channel_id=1, source_target_pairs={{0,12},{1,5},{2,14},{3,7},{4,0},{5,9},{6,2},{7,11},{8,4},{9,13},{1... | collective-permute-start | bytes 393224 | tf_op jit(solution)/shard_map/ppermute | solution.py:34
  130.5 6.5 %collective-permute-start.22 = (bf16[64,2048]{1,0:T(8,128)(2,1)S(1)}, bf16[64,2048]{1,0:T(8,128)(2,1)S(1)}, u32[]{:S(2)}, u32[]{:S(2)}) collective-permute-start(bf16[64,2048]{1,0:T(8,128)(2,1)S(1)} %shard_map.125), channel_id=1, source_target_pairs={{0,12},{1,5},{2,14},{3,7},{4,0},{5,9},{6,2},{7,11},{8,4},{9,13},{1... | collective-permute-start | bytes 786440 | tf_op jit(solution)/shard_map/ppermute | solution.py:34
  130.6 7.6 %collective-permute-start.17 = (bf16[64,2048]{1,0:T(8,128)(2,1)S(1)}, bf16[64,2048]{1,0:T(8,128)(2,1)S(1)}, u32[]{:S(2)}, u32[]{:S(2)}) collective-permute-start(bf16[64,2048]{1,0:T(8,128)(2,1)S(1)} %slice.26), channel_id=1, source_target_pairs={{0,1},{1,0},{2,3},{3,2},{4,5},{5,4},{6,7},{7,6},{8,9},{9,8},{10,11... | collective-permute-start | bytes 786440 | tf_op jit(solution)/shard_map/ppermute | solution.py:34
  137.0 2.1 %collective-permute-start.23 = (bf16[32,2048]{1,0:T(8,128)(2,1)S(1)}, bf16[32,2048]{1,0:T(8,128)(2,1)S(1)}, u32[]{:S(2)}, u32[]{:S(2)}) collective-permute-start(bf16[32,2048]{1,0:T(8,128)(2,1)S(1)} %slice.29), channel_id=1, source_target_pairs={{0,1},{1,0},{2,3},{3,2},{4,5},{5,4},{6,7},{7,6},{8,9},{9,8},{10,11... | collective-permute-start | bytes 393224 | tf_op jit(solution)/shard_map/ppermute | solution.py:34
  138.3 5.2 %collective-permute-start.18 = (bf16[32,2048]{1,0:T(8,128)(2,1)S(1)}, bf16[32,2048]{1,0:T(8,128)(2,1)S(1)}, u32[]{:S(2)}, u32[]{:S(2)}) collective-permute-start(bf16[32,2048]{1,0:T(8,128)(2,1)S(1)} %slice.27), channel_id=1, source_target_pairs={{0,2},{1,3},{2,0},{3,1},{4,6},{5,7},{6,4},{7,5},{8,10},{9,11},{10,... | collective-permute-start | bytes 393224 | tf_op jit(solution)/shard_map/ppermute | solution.py:34
  (2 other events, 1.8 us)

commit v2 on v0

v2 whole, which is shorter than its diff:
```python
import functools

import jax
import jax.numpy as jnp
from jax import lax
from jax.experimental import pallas as pl
from jax.experimental.pallas import tpu as pltpu
from jax.sharding import PartitionSpec as P

bf16 = jnp.bfloat16
f32 = jnp.float32
VMEM = pl.BlockSpec(memory_space=pltpu.VMEM)
MIB = 1024 * 1024
LONG = 10**11
Y_FIRST = 1792
EXTRA = 512
HIDDEN_LIMIT = 14
BACK_LIMIT = 16


def like(*shape, dtype=bf16):
    return jax.ShapeDtypeStruct(shape, dtype)


def local_kernel(name, body, outs, *operands, after=(), hbm=False, limit=12, scratch=(), flops=1):
    n_in, n_after = len(operands), len(after)
    anywhere = pl.BlockSpec(memory_space=pl.ANY)
    if hbm:
        operands = tuple(pltpu.with_memory_space_constraint(o, pltpu.HBM) for o in operands)

    def run(*refs):
        body(*refs[:n_in], *refs[n_in + n_after :])

    return pl.pallas_call(
        run,
        out_shape=outs,
        in_specs=[anywhere if hbm else VMEM] * n_in + [anywhere] * n_after,
        out_specs=jax.tree.map(lambda _: VMEM, outs),
        scratch_shapes=scratch,
        compiler_params=pltpu.CompilerParams(vmem_limit_bytes=limit * MIB),
        cost_estimate=pl.CostEstimate(flops=flops, bytes_accessed=1, transcendentals=0),
        name=name,
    )(*operands, *after)


def over_tensor(name, shard, move):
    with jax.named_scope(name):
        return lax.ppermute(shard, "tensor", [(i, move(i)) for i in range(lax.axis_size("tensor"))])


def other_core(i):
    return i ^ 1


def other_z(i):
    return i ^ 2


def along_y(i, sign=1):
    step = sign * (1 if i % 2 == 0 else -1)
    return (i // 4 + step) % 4 * 4 + i % 4


def back_y(i):
    return along_y(i, -1)


def across_y(i):
    return (i + 8) % 16


def join(name, *pieces, after=(), flops=1):
    pieces = [p if isinstance(p, tuple) else (p, 0, p.shape[0]) for p in pieces]

    def body(*refs):
        out, at = refs[-1], 0
        for ref, (_, start, n) in zip(refs[:-1], pieces):
            out[at : at + n] = ref[start : start + n]
            at += n

    rows = sum(n for _, _, n in pieces)
    return local_kernel(name, body, like(rows, pieces[0][0].shape[1]), *[p for p, _, _ in pieces], after=after, flops=flops)


def prepare_kernel(keep_hbm, roster_hbm, parked, parked_scale, local, local_scale, gain, pending,
                   payload, own, gain_copy, cot, codes, scales, keep, roster, sems):
    mine = lax.axis_index("section")
    mirror = lax.axis_size("section") - 1 - mine
    d = gain.shape[1]
    copies = [
        pltpu.make_async_copy(source, target, sems.at[k])
        for k, (source, target) in enumerate(
            (
                (parked, codes.at[0]),
                (parked_scale, scales.at[0]),
                (local, codes.at[1]),
                (local_scale, scales.at[1]),
                (gain, gain_copy),
                (pending, cot),
                (keep_hbm, keep),
                (roster_hbm, roster),
            )
        )
    ]
    for copy in copies:
        copy.start()

    def put(out, which, slot):
        rows = codes.shape[2]
        eye = lax.broadcasted_iota(jnp.int32, (rows, rows), 0) == lax.broadcasted_iota(jnp.int32, (rows, rows), 1)

        def choose(k):
            out[:, :d] = codes[which, k]
            row = jnp.broadcast_to(scales[which, k : k + 1, :].astype(f32), (rows, rows))
            column = jnp.sum(jnp.where(eye, row, 0.0), axis=1, keepdims=True)
            out[:, d : d + EXTRA] = jnp.broadcast_to(column, (rows, EXTRA)).astype(bf16)

        pl.when(slot <= 0)(lambda: choose(0))
        pl.when(slot > 0)(lambda: choose(1))

    for k in (6, 7, 0, 1):
        copies[k].wait()
    put(payload, 0, roster[mirror] - keep[mirror])
    copies[2].wait()
    copies[3].wait()
    put(own, 1, roster[mine])
    is_parked = (roster[mine] >= keep[mine]).astype(f32)
    own[:, d + EXTRA :] = jnp.full((own.shape[0], 128), is_parked, f32).astype(bf16)
    copies[4].wait()
    copies[5].wait()


def norm_kernel(own, parked, gain, normed, unit, inv):
    d = gain.shape[1]
    is_parked = own[:, d + EXTRA : d + EXTRA + 1] > 0
    codes = jnp.where(is_parked, parked[:, :d], own[:, :d])
    scale = jnp.where(is_parked, parked[:, d : d + 1], own[:, d : d + 1])
    x = codes.astype(f32) * scale.astype(f32)
    inv_rms = lax.rsqrt(jnp.mean(x * x, axis=-1, keepdims=True) + 1e-05)
    u = x * inv_rms
    unit[...] = u
    inv[...] = jnp.broadcast_to(inv_rms, inv.shape)
    normed[...] = (u * gain[...]).astype(bf16)


def hidden_kernel(cot_blocks, normed_blocks, n_cot, n_normed, *refs):
    cots, normeds = refs[:n_cot], refs[n_cot : n_cot + n_normed]
    w_gate, w_up, w_down, dgate, dup, rows, dh = refs[n_cot + n_normed :]

    def fill(pieces, blocks):
        at = 0
        for piece, start, count in blocks:
            rows[at : at + count] = pieces[piece][start : start + count]
            at += count

    fill(cots, cot_blocks)
    dh[...] = lax.dot_general(rows[...], w_down[...], (((1,), (1,)), ((), ())), preferred_element_type=f32)
    fill(normeds, normed_blocks)
    gate = jnp.dot(rows[...], w_gate[...], preferred_element_type=f32)
    up = jnp.dot(rows[...], w_up[...], preferred_element_type=f32)
    d = dh[...]
    sig = jax.nn.sigmoid(gate)
    dgate[...] = (d * up * sig * (1.0 + gate * (1.0 - sig))).astype(bf16)
    dup[...] = (d * gate * sig).astype(bf16)


def hidden(name, cots, cot_blocks, normeds, normed_blocks, weights, after=()):
    n_rows = sum(count for _, _, count in cot_blocks)
    d, units = weights[0].shape
    return local_kernel(
        name,
        functools.partial(hidden_kernel, cot_blocks, normed_blocks, len(cots), len(normeds)),
        (like(n_rows, units), like(n_rows, units)),
        *cots,
        *normeds,
        *weights,
        after=after,
        scratch=[pltpu.VMEM((n_rows, d), bf16), pltpu.VMEM((n_rows, units), f32)],
        flops=LONG,
        limit=HIDDEN_LIMIT,
    )


def back_kernel(start, g0, u0, g1, u1, g2, u2, w_gate, w_up, keep, send, g_rows, u_rows):
    for rows, home, side, far in ((g_rows, g0, g1, g2), (u_rows, u0, u1, u2)):
        rows[0:64] = home[0:64]
        rows[64:192] = side[0:128]
        rows[192:256] = far[0:64]
        rows[256:320] = home[64:128]
        rows[320:448] = side[128:256]
        rows[448:512] = far[64:128]
    n = keep.shape[1]
    cols = slice(start, start + n)
    transposed = (((1,), (1,)), ((), ()))
    dn = lax.dot_general(g_rows[...], w_gate[cols, :], transposed, preferred_element_type=f32) + lax.dot_general(
        u_rows[...], w_up[cols, :], transposed, preferred_element_type=f32
    )
    keep[...] = dn[:256].astype(bf16)
    send[...] = dn[256:].astype(bf16)


def back(name, start, n, grads, w_gate, w_up, after=()):
    units = w_gate.shape[1]
    return local_kernel(
        name,
        functools.partial(back_kernel, start),
        (like(256, n), like(256, n)),
        *grads,
        w_gate,
        w_up,
        after=after,
        scratch=[pltpu.VMEM((512, units), bf16)] * 2,
        flops=LONG,
        limit=BACK_LIMIT,
    )


def add(name, outs, *columns, after=()):
    widths = [pieces[0].shape[1] for pieces in columns]
    n_in = sum(len(pieces) for pieces in columns)

    def body(*refs):
        for out, spans in zip(refs[n_in:], outs):
            left, at_piece = 0, 0
            for pieces, width in zip(columns, widths):
                at = 0
                for count, terms in spans:
                    total = None
                    for piece, start in terms:
                        term = refs[at_piece + piece][start : start + count].astype(f32)
                        total = term if total is None else total + term
                    out[at : at + count, left : left + width] = total.astype(bf16)
                    at += count
                left += width
                at_piece += len(pieces)

    shapes = tuple(like(sum(count for count, _ in spans), sum(widths)) for spans in outs)
    results = local_kernel(name, body, shapes, *[p for pieces in columns for p in pieces], after=after)
    return results if len(outs) > 1 else results[0]


def final_kernel(held, far_b, home_b, other_b, total, total_z, cot, unit, inv, gain, out):
    split = total.shape[1]
    dn_a = total[...].astype(f32) + total_z[...].astype(f32)
    dn_b = held[...].astype(f32) + far_b[...].astype(f32) + home_b[:32].astype(f32) + other_b[...].astype(f32)
    g_a, g_b = dn_a * gain[:, :split], dn_b * gain[:, split:]
    u_a, u_b = unit[:, :split], unit[:, split:]
    mean = (
        jnp.sum(g_a * u_a, axis=-1, keepdims=True) + jnp.sum(g_b * u_b, axis=-1, keepdims=True)
    ) / unit.shape[1]
    scale = inv[:, :1]
    out[:, :split] = (cot[:, :split].astype(f32) + scale * (g_a - u_a * mean)).astype(bf16)
    out[:, split:] = (cot[:, split:].astype(f32) + scale * (g_b - u_b * mean)).astype(bf16)


def on_device(
    local_codes,
    local_scales,
    parked_codes,
    parked_scales,
    keep_count,
    roster,
    norm_gain,
    w_gate,
    w_up,
    w_down,
    pending,
):
    sections = lax.axis_size("section")
    _, _, shard, d = local_codes.shape
    stash_pairs = [(sections - 1 - i, i) for i in range(sections // 2)]
    shift_pairs = [((i + 1) % sections, i) for i in range(sections)]

    payload, own_stash, gain, cot_source = local_kernel(
        "prepare",
        prepare_kernel,
        (like(shard, d + EXTRA), like(shard, d + EXTRA + 128), like(1, d, dtype=f32), like(shard, d)),
        keep_count,
        roster,
        parked_codes[0],
        parked_scales[0],
        local_codes[0],
        local_scales[0],
        norm_gain,
        pending[0],
        hbm=True,
        scratch=[
            pltpu.VMEM((2, 2, shard, d), bf16),
            pltpu.VMEM((2, 2, shard), bf16),
            pltpu.SMEM(keep_count.shape, jnp.int32),
            pltpu.SMEM(roster.shape, jnp.int32),
            pltpu.SemaphoreType.DMA((8,)),
        ],
    )
    with jax.named_scope("fetched"):
        fetched = lax.ppermute(payload, "section", stash_pairs)
    with jax.named_scope("shift"):
        cot = lax.ppermute(cot_source, "section", shift_pairs)
    w_gate, w_up, w_down = w_gate[0], w_up[0], w_down[0]
    weights = w_gate, w_up, w_down
    cot = join("cot", cot, after=(own_stash,))
    cot_z = over_tensor("cot_z", cot, other_z)
    cot_core = over_tensor("cot_core", cot, other_core)
    cot_chip = join("cot_chip", cot, cot_core)
    cot_ahead = over_tensor("cot_ahead", cot_chip, along_y)

    normed, unit, inv = local_kernel(
        "norm",
        norm_kernel,
        (like(shard, d), like(shard, d, dtype=f32), like(shard, 128, dtype=f32)),
        own_stash,
        fetched,
        gain,
        after=(cot_chip,),
        flops=LONG,
    )
    normed_z = over_tensor("normed_z", normed, other_z)
    normed_core = over_tensor("normed_core", normed, other_core)
    cot_part = join("cot_part", (cot_ahead, 0, 32), after=(normed, cot_z))
    cot_far = over_tensor("cot_far", cot_part, along_y)
    cot_ahead_z = over_tensor("cot_ahead_z", cot_ahead, other_z)
    cot_behind = over_tensor("cot_behind", cot_ahead, other_core)
    cot_z_core = over_tensor("cot_z_core", cot_z, other_core)

    ahead = over_tensor("ahead", join("chip", normed, normed_core), along_y)
    normed_z_core = over_tensor("normed_z_core", join("normed_z_copy", normed_z, after=(cot_part,)), other_core)
    chip_z = join("chip_z", normed_z, normed_z_core)
    ahead_z = over_tensor("ahead_z", chip_z, along_y)
    cot_far_z = over_tensor("cot_far_z", cot_far, other_z)
    cot_far_core = over_tensor("cot_far_core", cot_far, other_core)
    g0, u0 = hidden(
        "hidden_home",
        (cot, cot_z, cot_core, cot_z_core),
        tuple((k, 0, 32) for k in range(4)),
        (normed, normed_z, normed_core, normed_z_core),
        tuple((k, 0, 32) for k in range(4)),
        weights,
        after=(cot_ahead_z, cot_far),
    )
    cot_behind_z = over_tensor("cot_behind_z", cot_ahead_z, other_core)
    far = over_tensor("far", join("part", (ahead, 0, 32), (ahead_z, 0, 32), after=(g0,)), along_y)
    behind = over_tensor("behind", join("ahead_copy", ahead, after=(g0,)), other_core)
    behind_z = over_tensor("behind_z", join("ahead_z_copy", ahead_z, after=(g0,)), other_core)
    sides = tuple((k + j, 32 * h, 32) for k in (0, 2) for h in range(2) for j in range(2))
    g1, u1 = hidden(
        "hidden_sides",
        (cot_ahead, cot_ahead_z, cot_behind, cot_behind_z),
        sides,
        (ahead, ahead_z, behind, behind_z),
        sides,
        weights,
    )
    cot_far_z_core = over_tensor("cot_far_z_core", join("cot_far_z_copy", cot_far_z, after=(g1,)), other_core)
    far_core = over_tensor("far_core", join("far_copy", far, after=(g1,)), other_core)
    g2, u2 = hidden(
        "hidden_far",
        (cot_far, cot_far_z, cot_far_core, cot_far_z_core),
        tuple((k, 0, 32) for k in range(4)),
        (far, far_core),
        ((0, 0, 64), (1, 0, 64)),
        weights,
    )
    grads = (g0, u0, g1, u1, g2, u2)

    keep_a, send_a = back("back_a", 0, Y_FIRST, grads, w_gate, w_up)
    got_a = over_tensor("got_a", send_a, other_core)
    keep_b, send_b = back("back_b", Y_FIRST, d - Y_FIRST, grads, w_gate, w_up, after=(keep_a,))
    got_b = over_tensor("got_b", send_b, other_core)
    both = keep_a, got_a
    to_far = add("to_far", [[(64, ((0, 192), (1, 192)))]], both, after=(keep_b,))
    from_far = over_tensor("from_far", to_far, back_y)
    away = add("away", [[(32, ((0, 64 * k + 32), (1, 64 * k + 32))) for k in range(4)]], (keep_b, got_b), after=(to_far,))
    from_z = over_tensor("from_z", away, other_z)
    near, side = add("near_side", [[(64, ((0, 0), (1, 0)))], [(128, ((0, 64), (1, 64)))]], both, after=(away,))
    to_home = add("to_home", [[(64, ((0, 0), (1, 0))), (64, ((0, 64),))]], (side, from_far))
    home = over_tensor("home", to_home, back_y)
    held, held_side, held_far = add(
        "held",
        [
            [(32, ((0, 64 * k), (1, 64 * k), (2, 32 * k))) for k in ks]
            for ks in ((0,), (1, 2), (3,))
        ],
        (keep_b, got_b, from_z),
    )
    home_core = tuple(
        over_tensor(name, join(name + "_part", (home, at, 32), after=(held,)), other_core)
        for name, at in (("home_core", 64), ("home_core_z", 96))
    )
    total, total_away = add(
        "total", [[(32, ((0, at), (1, at), (2 + at // 32, 0)))] for at in (0, 32)], (near, home, *home_core)
    )
    total_z = over_tensor("total_z", total_away, other_z)
    home_b = over_tensor("home_b", held_side, back_y)
    far_b = over_tensor("far_b", held_far, across_y)
    home_b_core = over_tensor("home_b_core", join("home_b_part", (home_b, 32, 32), after=(total, far_b)), other_core)
    return local_kernel(
        "final", final_kernel, like(shard, d), held, far_b, home_b, home_b_core, total, total_z, cot, unit, inv, gain
    )[None]


def solution(mesh):
    placed = (
        P("section", None, "tensor", None),
        P("section", None, "tensor"),
        P("section", None, "tensor", None),
        P("section", None, "tensor"),
        P(),
        P(),
        P("section", None),
        P("section", None, "tensor"),
        P("section", None, "tensor"),
        P("section", "tensor", None),
        P("section", "tensor", None),
    )
    return jax.shard_map(
        on_device,
        mesh=mesh,
        in_specs=placed,
        out_specs=P("section", "tensor", None),
        check_vma=False,
    )
```

time: 258 us -> 116 us (0.45)
  waiting for transfers between devices: 162 us -> 43.3 us
  matrix products: 53.6 us -> 0 us
  Pallas kernels: 0 us -> 28.8 us
  starting transfers between devices: 16 us -> 42.6 us
  between operations: 16.5 us -> 0.29 us
  other arithmetic: 6.71 us -> 0 us
  local copies, waits for them, and re-layouts: 3.27 us -> 0.04 us
    reduce_scatter x1 -> x0, waiting for transfers between devices: 96.7 us -> none  [on_device(): lax.psum_scatter(lax.dot_general(dgate, gate_w, (((1,), (1,)), ((), ())),...]
    dot_general x4 -> x0, matrix products: 53.6 us -> none  [the longest x1 19.2 us: on_device(): lax.dot_general(dgate, gate_w, (((1,), (1,)), ((), ())), preferred_elemen...]
    pallas_call x0 -> x28, Pallas kernels: none -> 28.8 us  [local_kernel(): pl.pallas_call(run, out_shape=outs, in_specs=[anywhere if hbm else VMEM]...]
    ppermute x7 -> x33, starting transfers between devices: 15.9 us -> 42.6 us  [the longest x31 34.6 us: over_tensor(): lax.ppermute(shard, 'tensor', [(i, move(i)) for i in range(lax.axis_size(...]
    all_gather x2 -> x0, waiting for transfers between devices: 26.1 us -> none  [the longest x1 26.1 us: on_device(): piece = lax.all_gather(normed, 'tensor', axis=0, tiled=True)]
    ppermute x7 -> x33, waiting for transfers between devices: 38.8 us -> 43.3 us  [the longest x31 37.2 us: over_tensor(): lax.ppermute(shard, 'tensor', [(i, move(i)) for i in range(lax.axis_size(...]
  transfers between devices with their start and end apart: 10 -> 33, of which waited for: 7 -> 19; matrix products, arithmetic and copies ran while one was open for 6% -> 0% of each run, Pallas kernels for 0% -> 11%
where the time goes in v2:
time: 116 us; the launch traced here: 115 us
  waiting for transfers between devices  43.3 us (37%)
  starting transfers between devices  42.6 us (37%)
  Pallas kernels  28.8 us (25%)
    ppermute x31, waiting for transfers between devices, over_tensor(): lax.ppermute(shard, 'tensor', [(i, move(i)) for i in range(lax.axis_size(...  37.2 us
    ppermute x31, starting transfers between devices, over_tensor(): lax.ppermute(shard, 'tensor', [(i, move(i)) for i in range(lax.axis_size(...  34.6 us
    pallas_call x28, Pallas kernels, local_kernel(): pl.pallas_call(run, out_shape=outs, in_specs=[anywhere if hbm else VMEM]...  28.8 us
    ppermute x1, starting transfers between devices, on_device(): cot = lax.ppermute(cot_source, 'section', shift_pairs)  6.69 us
    ppermute x1, waiting for transfers between devices, on_device(): cot = lax.ppermute(cot_source, 'section', shift_pairs)  3.69 us
    ppermute x1, waiting for transfers between devices, on_device(): fetched = lax.ppermute(payload, 'section', stash_pairs)  2.42 us
  transfers between devices with their start and end apart: 33, of which 19 were waited for; matrix products, arithmetic and copies ran while one was open for 0% of the time, Pallas kernels for 11%

profile of v2, /device:TPU:1, one launch (start us, length us, event | category | flops | bytes accessed | tf_op | source)
XLA Modules:
  0.0 114.9 jit_solution(16559329431162352598)
XLA Ops:
  0.0 1.4 %prepare.1 = (bf16[32,4608]{1,0:T(8,128)(2,1)S(1)}, bf16[32,4736]{1,0:T(8,128)(2,1)S(1)}, f32[1,4096]{1,0:T(1,128)S(1)}, bf16[32,4096]{1,0:T(8,128)(2,1)S(1)}) custom-call(s32[8]{0:T(128)} %refs_0_.1, s32[8]{0:T(128)} %refs_1_.1, bf16[2,32,4096]{2,1,0:T(8,128)(2,1)} %bitcast.22, bf16[2,32]{1,0:T(2,128)(2,1)} %bitcast.25, bf16[2,32,4096]{2,1,0:T(8,128)(2,1)} %bitcast.23, ...), custom_call_target="tpu_custom_call" | custom-call | flops 1 | bytes 1 | tf_op jit(solution)/shard_map/prepare/pallas_call | solution.py:34
  1.4 6.7 %collective-permute-start = (bf16[32,4096]{1,0:T(8,128)(2,1)S(1)}, bf16[32,4096]{1,0:T(8,128)(2,1)S(1)}, u32[]{:S(2)}, u32[]{:S(2)}) collective-permute-start(bf16[32,4096]{1,0:T(8,128)(2,1)S(1)} %get-tuple-element.29), channel_id=1, source_target_pairs={{16,0},{32,16},{48,32},{64,48},{80,64},{96,80},{112,96},{0,112},{1... | collective-permute-start | bytes 786440 | tf_op jit(solution)/shard_map/shift/ppermute | solution.py:298
  8.1 1.3 %collective-permute-start.4 = (bf16[32,4608]{1,0:T(8,128)(2,1)S(1)}, bf16[32,4608]{1,0:T(8,128)(2,1)S(1)}, u32[]{:S(2)}, u32[]{:S(2)}) collective-permute-start(bf16[32,4608]{1,0:T(8,128)(2,1)S(1)} %get-tuple-element.31), channel_id=1, source_target_pairs={{112,0},{96,16},{80,32},{64,48},{113,1},{97,17},{81,33},{65,49},{1... | collective-permute-start | bytes 884744 | tf_op jit(solution)/shard_map/fetched/ppermute | solution.py:296
  9.4 3.7 %collective-permute-done.refs_0_ = bf16[32,4096]{1,0:T(8,128)(2,1)S(1)} collective-permute-done((bf16[32,4096]{1,0:T(8,128)(2,1)S(1)}, bf16[32,4096]{1,0:T(8,128)(2,1)S(1)}, u32[]{:S(2)}, u32[]{:S(2)}) %collective-permute-start) | collective-permute-done | bytes 262176 | tf_op jit(solution)/shard_map/shift/ppermute | solution.py:298
  13.1 1.6 %collective-permute-start.2 = (bf16[32,4096]{1,0:T(8,128)(2,1)S(1)}, bf16[32,4096]{1,0:T(8,128)(2,1)S(1)}, u32[]{:S(2)}, u32[]{:S(2)}) collective-permute-start(bf16[32,4096]{1,0:T(8,128)(2,1)S(1)} %cot.1.refs_0_.refs_6_), channel_id=1, source_target_pairs={{0,1},{1,0},{2,3},{3,2},{4,5},{5,4},{6,7},{7,6},{8,9},{9,8},{10,11... | collective-permute-start | bytes 786440 | tf_op jit(solution)/shard_map/cot_core/ppermute | solution.py:48
  15.9 2.8 %collective-permute-start.7 = (bf16[64,4096]{1,0:T(8,128)(2,1)S(1)}, bf16[64,4096]{1,0:T(8,128)(2,1)S(1)}, u32[]{:S(2)}, u32[]{:S(2)}) collective-permute-start(bf16[64,4096]{1,0:T(8,128)(2,1)S(1)} %cot_chip.1.refs_3_), channel_id=1, source_target_pairs={{0,4},{1,13},{2,6},{3,15},{4,8},{5,1},{6,10},{7,3},{8,12},{9,5},{1... | collective-permute-start | bytes 1572872 | tf_op jit(solution)/shard_map/cot_ahead/ppermute | solution.py:48
  18.7 2.4 %collective-permute-done.4.refs_1_ = bf16[32,4608]{1,0:T(8,128)(2,1)S(1)} collective-permute-done((bf16[32,4608]{1,0:T(8,128)(2,1)S(1)}, bf16[32,4608]{1,0:T(8,128)(2,1)S(1)}, u32[]{:S(2)}, u32[]{:S(2)}) %collective-permute-start.4) | collective-permute-done | bytes 294944 | tf_op jit(solution)/shard_map/fetched/ppermute | solution.py:296
  22.3 2.5 %collective-permute-done.7.refs_0_ = bf16[64,4096]{1,0:T(8,128)(2,1)S(1)} collective-permute-done((bf16[64,4096]{1,0:T(8,128)(2,1)S(1)}, bf16[64,4096]{1,0:T(8,128)(2,1)S(1)}, u32[]{:S(2)}, u32[]{:S(2)}) %collective-permute-start.7) | collective-permute-done | bytes 524320 | tf_op jit(solution)/shard_map/cot_ahead/ppermute | solution.py:48
  25.6 2.2 %collective-permute-start.6 = (bf16[32,4096]{1,0:T(8,128)(2,1)S(1)}, bf16[32,4096]{1,0:T(8,128)(2,1)S(1)}, u32[]{:S(2)}, u32[]{:S(2)}) collective-permute-start(bf16[32,4096]{1,0:T(8,128)(2,1)S(1)} %get-tuple-element.33.refs_1_.refs_4_.refs_0_), channel_id=1, source_target_pairs={{0,1},{1,0},{2,3},{3,2},{4,5},{5,4},{6,7},{7,6},{8,9},{9,8},{10,11... | collective-permute-start | bytes 786440 | tf_op jit(solution)/shard_map/normed_core/ppermute | solution.py:48
  27.8 4.8 %collective-permute-start.8 = (bf16[32,4096]{1,0:T(8,128)(2,1)S(1)}, bf16[32,4096]{1,0:T(8,128)(2,1)S(1)}, u32[]{:S(2)}, u32[]{:S(2)}) collective-permute-start(bf16[32,4096]{1,0:T(8,128)(2,1)S(1)} %normed_z_copy.1), channel_id=1, source_target_pairs={{0,1},{1,0},{2,3},{3,2},{4,5},{5,4},{6,7},{7,6},{8,9},{9,8},{10,11... | collective-permute-start | bytes 786440 | tf_op jit(solution)/shard_map/normed_z_core/ppermute | solution.py:48
  32.7 2.3 %collective-permute-start.10 = (bf16[32,4096]{1,0:T(8,128)(2,1)S(1)}, bf16[32,4096]{1,0:T(8,128)(2,1)S(1)}, u32[]{:S(2)}, u32[]{:S(2)}) collective-permute-start(bf16[32,4096]{1,0:T(8,128)(2,1)S(1)} %cot_part.1.refs_1_), channel_id=1, source_target_pairs={{0,4},{1,13},{2,6},{3,15},{4,8},{5,1},{6,10},{7,3},{8,12},{9,5},{1... | collective-permute-start | bytes 786440 | tf_op jit(solution)/shard_map/cot_far/ppermute | solution.py:48
  35.1 1.2 %collective-permute-start.13 = (bf16[64,4096]{1,0:T(8,128)(2,1)S(1)}, bf16[64,4096]{1,0:T(8,128)(2,1)S(1)}, u32[]{:S(2)}, u32[]{:S(2)}) collective-permute-start(bf16[64,4096]{1,0:T(8,128)(2,1)S(1)} %chip.1), channel_id=1, source_target_pairs={{0,4},{1,13},{2,6},{3,15},{4,8},{5,1},{6,10},{7,3},{8,12},{9,5},{1... | collective-permute-start | bytes 1572872 | tf_op jit(solution)/shard_map/ahead/ppermute | solution.py:48
  36.7 1.4 %collective-permute-start.14 = (bf16[64,4096]{1,0:T(8,128)(2,1)S(1)}, bf16[64,4096]{1,0:T(8,128)(2,1)S(1)}, u32[]{:S(2)}, u32[]{:S(2)}) collective-permute-start(bf16[64,4096]{1,0:T(8,128)(2,1)S(1)} %chip_z.1), channel_id=1, source_target_pairs={{0,4},{1,13},{2,6},{3,15},{4,8},{5,1},{6,10},{7,3},{8,12},{9,5},{1... | collective-permute-start | bytes 1572872 | tf_op jit(solution)/shard_map/ahead_z/ppermute | solution.py:48
  38.8 4.6 %hidden_home.1 = (bf16[128,896]{1,0:T(8,128)(2,1)S(1)}, bf16[128,896]{1,0:T(8,128)(2,1)S(1)}) custom-call(bf16[32,4096]{1,0:T(8,128)(2,1)S(1)} %cot.1.refs_0_.refs_6_, bf16[32,4096]{1,0:T(8,128)(2,1)S(1)} %collective-permute-done.1.refs_2_.refs_1_, bf16[32,4096]{1,0:T(8,128)(2,1)S(1)} %collective-permute-done.2.refs_1_.refs_2_, ...), custom_call_target="tpu_custom_call" | custom-call | flops 99999997952 | bytes 1 | tf_op jit(solution)/shard_map/hidden_home/pallas_call | solution.py:34
  44.0 2.5 %collective-permute-start.15 = (bf16[64,4096]{1,0:T(8,128)(2,1)S(1)}, bf16[64,4096]{1,0:T(8,128)(2,1)S(1)}, u32[]{:S(2)}, u32[]{:S(2)}) collective-permute-start(bf16[64,4096]{1,0:T(8,128)(2,1)S(1)} %ahead_copy.1), channel_id=1, source_target_pairs={{0,1},{1,0},{2,3},{3,2},{4,5},{5,4},{6,7},{7,6},{8,9},{9,8},{10,11... | collective-permute-start | bytes 1572872 | tf_op jit(solution)/shard_map/behind/ppermute | solution.py:48
  46.6 3.0 %collective-permute-done.14.refs_0_.refs_5_.refs_1_ = bf16[64,4096]{1,0:T(8,128)(2,1)S(1)} collective-permute-done((bf16[64,4096]{1,0:T(8,128)(2,1)S(1)}, bf16[64,4096]{1,0:T(8,128)(2,1)S(1)}, u32[]{:S(2)}, u32[]{:S(2)}) %collective-permute-start.14) | collective-permute-done | bytes 524320 | tf_op jit(solution)/shard_map/ahead_z/ppermute | solution.py:48
  49.6 2.5 %collective-permute-start.16 = (bf16[64,4096]{1,0:T(8,128)(2,1)S(1)}, bf16[64,4096]{1,0:T(8,128)(2,1)S(1)}, u32[]{:S(2)}, u32[]{:S(2)}) collective-permute-start(bf16[64,4096]{1,0:T(8,128)(2,1)S(1)} %ahead_z_copy.1), channel_id=1, source_target_pairs={{0,1},{1,0},{2,3},{3,2},{4,5},{5,4},{6,7},{7,6},{8,9},{9,8},{10,11... | collective-permute-start | bytes 1572872 | tf_op jit(solution)/shard_map/behind_z/ppermute | solution.py:48
  53.0 1.3 %collective-permute-start.20 = (bf16[64,4096]{1,0:T(8,128)(2,1)S(1)}, bf16[64,4096]{1,0:T(8,128)(2,1)S(1)}, u32[]{:S(2)}, u32[]{:S(2)}) collective-permute-start(bf16[64,4096]{1,0:T(8,128)(2,1)S(1)} %part.1), channel_id=1, source_target_pairs={{0,4},{1,13},{2,6},{3,15},{4,8},{5,1},{6,10},{7,3},{8,12},{9,5},{1... | collective-permute-start | bytes 1572872 | tf_op jit(solution)/shard_map/far/ppermute | solution.py:48
  54.3 6.8 %hidden_sides.1 = (bf16[256,896]{1,0:T(8,128)(2,1)S(1)}, bf16[256,896]{1,0:T(8,128)(2,1)S(1)}) custom-call(bf16[64,4096]{1,0:T(8,128)(2,1)S(1)} %collective-permute-done.7.refs_0_, bf16[64,4096]{1,0:T(8,128)(2,1)S(1)} %collective-permute-done.9.refs_11_.refs_1_, bf16[64,4096]{1,0:T(8,128)(2,1)S(1)} %collective-permute-done.11.refs_2_, ...), custom_call_target="tpu_custom_call" | custom-call | flops 99999997952 | bytes 1 | tf_op jit(solution)/shard_map/hidden_sides/pallas_call | solution.py:34
  61.6 2.5 %collective-permute-start.21 = (bf16[64,4096]{1,0:T(8,128)(2,1)S(1)}, bf16[64,4096]{1,0:T(8,128)(2,1)S(1)}, u32[]{:S(2)}, u32[]{:S(2)}) collective-permute-start(bf16[64,4096]{1,0:T(8,128)(2,1)S(1)} %far_copy.1), channel_id=1, source_target_pairs={{0,1},{1,0},{2,3},{3,2},{4,5},{5,4},{6,7},{7,6},{8,9},{9,8},{10,11... | collective-permute-start | bytes 1572872 | tf_op jit(solution)/shard_map/far_core/ppermute | solution.py:48
  64.9 1.1 collective-permute-done.18.refs_2_
  66.4 4.6 %hidden_far.1 = (bf16[128,896]{1,0:T(8,128)(2,1)S(1)}, bf16[128,896]{1,0:T(8,128)(2,1)S(1)}) custom-call(bf16[32,4096]{1,0:T(8,128)(2,1)S(1)} %collective-permute-done.10.refs_12_.refs_0_, bf16[32,4096]{1,0:T(8,128)(2,1)S(1)} %collective-permute-done.17.refs_0_.refs_1_, bf16[32,4096]{1,0:T(8,128)(2,1)S(1)} %collective-permute-done.18.refs_2_, ...), custom_call_target="tpu_custom_call" | custom-call | flops 99999997952 | bytes 1 | tf_op jit(solution)/shard_map/hidden_far/pallas_call | solution.py:34
  71.0 4.0 %back_a.1 = (bf16[256,1792]{1,0:T(8,128)(2,1)S(1)}, bf16[256,1792]{1,0:T(8,128)(2,1)S(1)}) custom-call(bf16[128,896]{1,0:T(8,128)(2,1)S(1)} %copy-done.3, bf16[128,896]{1,0:T(8,128)(2,1)S(1)} %get-tuple-element.35.refs_1_, bf16[256,896]{1,0:T(8,128)(2,1)S(1)} %get-tuple-element.36.refs_1_.refs_2_, bf16[256,896]{1,0:T(8,128)(2,1)S(1)} %get-tuple-element.37.refs_3_, ...), custom_call_target="tpu_custom_call" | custom-call | flops 99999997952 | bytes 1 | tf_op jit(solution)/shard_map/back_a/pallas_call | solution.py:34
  75.0 5.1 %back_b.1 = (bf16[256,2304]{1,0:T(8,128)(2,1)S(1)}, bf16[256,2304]{1,0:T(8,128)(2,1)S(1)}) custom-call(bf16[128,896]{1,0:T(8,128)(2,1)S(1)} %copy-done.3, bf16[128,896]{1,0:T(8,128)(2,1)S(1)} %get-tuple-element.35.refs_1_, bf16[256,896]{1,0:T(8,128)(2,1)S(1)} %get-tuple-element.36.refs_1_.refs_2_, bf16[256,896]{1,0:T(8,128)(2,1)S(1)} %get-tuple-element.37.refs_3_, ...), custom_call_target="tpu_custom_call" | custom-call | flops 99999997952 | bytes 1 | tf_op jit(solution)/shard_map/back_b/pallas_call | solution.py:34
  80.7 3.6 %collective-permute-done.23.refs_1_ = bf16[256,1792]{1,0:T(8,128)(2,1)S(1)} collective-permute-done((bf16[256,1792]{1,0:T(8,128)(2,1)S(1)}, bf16[256,1792]{1,0:T(8,128)(2,1)S(1)}, u32[]{:S(2)}, u32[]{:S(2)}) %collective-permute-start.23) | collective-permute-done | bytes 917536 | tf_op jit(solution)/shard_map/got_a/ppermute | solution.py:48
  85.4 5.9 %collective-permute-done.27.refs_1_ = bf16[64,1792]{1,0:T(8,128)(2,1)S(1)} collective-permute-done((bf16[64,1792]{1,0:T(8,128)(2,1)S(1)}, bf16[64,1792]{1,0:T(8,128)(2,1)S(1)}, u32[]{:S(2)}, u32[]{:S(2)}) %collective-permute-start.27) | collective-permute-done | bytes 229408 | tf_op jit(solution)/shard_map/from_far/ppermute | solution.py:48
  91.5 7.7 %collective-permute-done.24.refs_2_ = bf16[128,2304]{1,0:T(8,128)(2,1)S(1)} collective-permute-done((bf16[128,2304]{1,0:T(8,128)(2,1)S(1)}, bf16[128,2304]{1,0:T(8,128)(2,1)S(1)}, u32[]{:S(2)}, u32[]{:S(2)}) %collective-permute-start.24) | collective-permute-done | bytes 589856 | tf_op jit(solution)/shard_map/from_z/ppermute | solution.py:48
  99.5 1.1 collective-permute-start.25
  100.6 1.5 %collective-permute-start.29 = (bf16[32,1792]{1,0:T(8,128)(2,1)S(1)}, bf16[32,1792]{1,0:T(8,128)(2,1)S(1)}, u32[]{:S(2)}, u32[]{:S(2)}) collective-permute-start(bf16[32,1792]{1,0:T(8,128)(2,1)S(1)} %home_core_part.1), channel_id=1, source_target_pairs={{0,1},{1,0},{2,3},{3,2},{4,5},{5,4},{6,7},{7,6},{8,9},{9,8},{10,11... | collective-permute-start | bytes 344072 | tf_op jit(solution)/shard_map/home_core/ppermute | solution.py:48
  103.6 4.0 %collective-permute-done.25.refs_2_.refs_1_ = bf16[32,2304]{1,0:T(8,128)(2,1)S(1)} collective-permute-done((bf16[32,2304]{1,0:T(8,128)(2,1)S(1)}, bf16[32,2304]{1,0:T(8,128)(2,1)S(1)}, u32[]{:S(2)}, u32[]{:S(2)}) %collective-permute-start.25) | collective-permute-done | bytes 147488 | tf_op jit(solution)/shard_map/far_b/ppermute | solution.py:48
  107.6 1.9 %collective-permute-done.26.refs_0_.refs_2_ = bf16[64,2304]{1,0:T(8,128)(2,1)S(1)} collective-permute-done((bf16[64,2304]{1,0:T(8,128)(2,1)S(1)}, bf16[64,2304]{1,0:T(8,128)(2,1)S(1)}, u32[]{:S(2)}, u32[]{:S(2)}) %collective-permute-start.26) | collective-permute-done | bytes 294944 | tf_op jit(solution)/shard_map/home_b/ppermute | solution.py:48
  110.3 3.7 %collective-permute-done.32.refs_5_ = bf16[32,1792]{1,0:T(8,128)(2,1)S(1)} collective-permute-done((bf16[32,1792]{1,0:T(8,128)(2,1)S(1)}, bf16[32,1792]{1,0:T(8,128)(2,1)S(1)}, u32[]{:S(2)}, u32[]{:S(2)}) %collective-permute-start.32) | collective-permute-done | bytes 114720 | tf_op jit(solution)/shard_map/total_z/ppermute | solution.py:48
  (80 shorter events, 13.1 us)
Async XLA Ops:
  1.4 11.7 %collective-permute-start = (bf16[32,4096]{1,0:T(8,128)(2,1)S(1)}, bf16[32,4096]{1,0:T(8,128)(2,1)S(1)}, u32[]{:S(2)}, u32[]{:S(2)}) collective-permute-start(bf16[32,4096]{1,0:T(8,128)(2,1)S(1)} %get-tuple-element.29), channel_id=1, source_target_pairs={{16,0},{32,16},{48,32},{64,48},{80,64},{96,80},{112,96},{0,112},{1... | collective-permute-start | bytes 786440 | tf_op jit(solution)/shard_map/shift/ppermute | solution.py:298
  8.1 13.1 %collective-permute-start.4 = (bf16[32,4608]{1,0:T(8,128)(2,1)S(1)}, bf16[32,4608]{1,0:T(8,128)(2,1)S(1)}, u32[]{:S(2)}, u32[]{:S(2)}) collective-permute-start(bf16[32,4608]{1,0:T(8,128)(2,1)S(1)} %get-tuple-element.31), channel_id=1, source_target_pairs={{112,0},{96,16},{80,32},{64,48},{113,1},{97,17},{81,33},{65,49},{1... | collective-permute-start | bytes 884744 | tf_op jit(solution)/shard_map/fetched/ppermute | solution.py:296
  13.1 2.8 %collective-permute-start.2 = (bf16[32,4096]{1,0:T(8,128)(2,1)S(1)}, bf16[32,4096]{1,0:T(8,128)(2,1)S(1)}, u32[]{:S(2)}, u32[]{:S(2)}) collective-permute-start(bf16[32,4096]{1,0:T(8,128)(2,1)S(1)} %cot.1.refs_0_.refs_6_), channel_id=1, source_target_pairs={{0,1},{1,0},{2,3},{3,2},{4,5},{5,4},{6,7},{7,6},{8,9},{9,8},{10,11... | collective-permute-start | bytes 786440 | tf_op jit(solution)/shard_map/cot_core/ppermute | solution.py:48
  14.7 13.1 %collective-permute-start.1 = (bf16[32,4096]{1,0:T(8,128)(2,1)S(1)}, bf16[32,4096]{1,0:T(8,128)(2,1)S(1)}, u32[]{:S(2)}, u32[]{:S(2)}) collective-permute-start(bf16[32,4096]{1,0:T(8,128)(2,1)S(1)} %cot.1.refs_0_.refs_6_), channel_id=1, source_target_pairs={{0,2},{1,3},{2,0},{3,1},{4,6},{5,7},{6,4},{7,5},{8,10},{9,11},{10,... | collective-permute-start | bytes 786440 | tf_op jit(solution)/shard_map/cot_z/ppermute | solution.py:48
  15.9 8.9 %collective-permute-start.7 = (bf16[64,4096]{1,0:T(8,128)(2,1)S(1)}, bf16[64,4096]{1,0:T(8,128)(2,1)S(1)}, u32[]{:S(2)}, u32[]{:S(2)}) collective-permute-start(bf16[64,4096]{1,0:T(8,128)(2,1)S(1)} %cot_chip.1.refs_3_), channel_id=1, source_target_pairs={{0,4},{1,13},{2,6},{3,15},{4,8},{5,1},{6,10},{7,3},{8,12},{9,5},{1... | collective-permute-start | bytes 1572872 | tf_op jit(solution)/shard_map/cot_ahead/ppermute | solution.py:48
  21.4 6.4 %collective-permute-start.5 = (bf16[32,4096]{1,0:T(8,128)(2,1)S(1)}, bf16[32,4096]{1,0:T(8,128)(2,1)S(1)}, u32[]{:S(2)}, u32[]{:S(2)}) collective-permute-start(bf16[32,4096]{1,0:T(8,128)(2,1)S(1)} %get-tuple-element.33.refs_1_.refs_4_.refs_0_), channel_id=1, source_target_pairs={{0,2},{1,3},{2,0},{3,1},{4,6},{5,7},{6,4},{7,5},{8,10},{9,11},{10,... | collective-permute-start | bytes 786440 | tf_op jit(solution)/shard_map/normed_z/ppermute | solution.py:48
  24.9 13.9 %collective-permute-start.9 = (bf16[64,4096]{1,0:T(8,128)(2,1)S(1)}, bf16[64,4096]{1,0:T(8,128)(2,1)S(1)}, u32[]{:S(2)}, u32[]{:S(2)}) collective-permute-start(bf16[64,4096]{1,0:T(8,128)(2,1)S(1)} %collective-permute-done.7.refs_0_), channel_id=1, source_target_pairs={{0,2},{1,3},{2,0},{3,1},{4,6},{5,7},{6,4},{7,5},{8,10},{9,11},{10,... | collective-permute-start | bytes 1572872 | tf_op jit(solution)/shard_map/cot_ahead_z/ppermute | solution.py:48
  25.6 9.5 %collective-permute-start.6 = (bf16[32,4096]{1,0:T(8,128)(2,1)S(1)}, bf16[32,4096]{1,0:T(8,128)(2,1)S(1)}, u32[]{:S(2)}, u32[]{:S(2)}) collective-permute-start(bf16[32,4096]{1,0:T(8,128)(2,1)S(1)} %get-tuple-element.33.refs_1_.refs_4_.refs_0_), channel_id=1, source_target_pairs={{0,1},{1,0},{2,3},{3,2},{4,5},{5,4},{6,7},{7,6},{8,9},{9,8},{10,11... | collective-permute-start | bytes 786440 | tf_op jit(solution)/shard_map/normed_core/ppermute | solution.py:48
  27.8 8.4 %collective-permute-start.8 = (bf16[32,4096]{1,0:T(8,128)(2,1)S(1)}, bf16[32,4096]{1,0:T(8,128)(2,1)S(1)}, u32[]{:S(2)}, u32[]{:S(2)}) collective-permute-start(bf16[32,4096]{1,0:T(8,128)(2,1)S(1)} %normed_z_copy.1), channel_id=1, source_target_pairs={{0,1},{1,0},{2,3},{3,2},{4,5},{5,4},{6,7},{7,6},{8,9},{9,8},{10,11... | collective-permute-start | bytes 786440 | tf_op jit(solution)/shard_map/normed_z_core/ppermute | solution.py:48
  32.7 4.0 %collective-permute-start.3 = (bf16[32,4096]{1,0:T(8,128)(2,1)S(1)}, bf16[32,4096]{1,0:T(8,128)(2,1)S(1)}, u32[]{:S(2)}, u32[]{:S(2)}) collective-permute-start(bf16[32,4096]{1,0:T(8,128)(2,1)S(1)} %collective-permute-done.1.refs_2_.refs_1_), channel_id=1, source_target_pairs={{0,1},{1,0},{2,3},{3,2},{4,5},{5,4},{6,7},{7,6},{8,9},{9,8},{10,11... | collective-permute-start | bytes 786440 | tf_op jit(solution)/shard_map/cot_z_core/ppermute | solution.py:48
  32.7 5.6 %collective-permute-start.10 = (bf16[32,4096]{1,0:T(8,128)(2,1)S(1)}, bf16[32,4096]{1,0:T(8,128)(2,1)S(1)}, u32[]{:S(2)}, u32[]{:S(2)}) collective-permute-start(bf16[32,4096]{1,0:T(8,128)(2,1)S(1)} %cot_part.1.refs_1_), channel_id=1, source_target_pairs={{0,4},{1,13},{2,6},{3,15},{4,8},{5,1},{6,10},{7,3},{8,12},{9,5},{1... | collective-permute-start | bytes 786440 | tf_op jit(solution)/shard_map/cot_far/ppermute | solution.py:48
  35.1 8.9 %collective-permute-start.13 = (bf16[64,4096]{1,0:T(8,128)(2,1)S(1)}, bf16[64,4096]{1,0:T(8,128)(2,1)S(1)}, u32[]{:S(2)}, u32[]{:S(2)}) collective-permute-start(bf16[64,4096]{1,0:T(8,128)(2,1)S(1)} %chip.1), channel_id=1, source_target_pairs={{0,4},{1,13},{2,6},{3,15},{4,8},{5,1},{6,10},{7,3},{8,12},{9,5},{1... | collective-permute-start | bytes 1572872 | tf_op jit(solution)/shard_map/ahead/ppermute | solution.py:48
  36.2 16.7 %collective-permute-start.11 = (bf16[64,4096]{1,0:T(8,128)(2,1)S(1)}, bf16[64,4096]{1,0:T(8,128)(2,1)S(1)}, u32[]{:S(2)}, u32[]{:S(2)}) collective-permute-start(bf16[64,4096]{1,0:T(8,128)(2,1)S(1)} %collective-permute-done.7.refs_0_), channel_id=1, source_target_pairs={{0,1},{1,0},{2,3},{3,2},{4,5},{5,4},{6,7},{7,6},{8,9},{9,8},{10,11... | collective-permute-start | bytes 1572872 | tf_op jit(solution)/shard_map/cot_behind/ppermute | solution.py:48
  36.7 12.9 %collective-permute-start.14 = (bf16[64,4096]{1,0:T(8,128)(2,1)S(1)}, bf16[64,4096]{1,0:T(8,128)(2,1)S(1)}, u32[]{:S(2)}, u32[]{:S(2)}) collective-permute-start(bf16[64,4096]{1,0:T(8,128)(2,1)S(1)} %chip_z.1), channel_id=1, source_target_pairs={{0,4},{1,13},{2,6},{3,15},{4,8},{5,1},{6,10},{7,3},{8,12},{9,5},{1... | collective-permute-start | bytes 1572872 | tf_op jit(solution)/shard_map/ahead_z/ppermute | solution.py:48
  44.0 10.3 %collective-permute-start.15 = (bf16[64,4096]{1,0:T(8,128)(2,1)S(1)}, bf16[64,4096]{1,0:T(8,128)(2,1)S(1)}, u32[]{:S(2)}, u32[]{:S(2)}) collective-permute-start(bf16[64,4096]{1,0:T(8,128)(2,1)S(1)} %ahead_copy.1), channel_id=1, source_target_pairs={{0,1},{1,0},{2,3},{3,2},{4,5},{5,4},{6,7},{7,6},{8,9},{9,8},{10,11... | collective-permute-start | bytes 1572872 | tf_op jit(solution)/shard_map/behind/ppermute | solution.py:48
  46.5 7.8 %collective-permute-start.12 = (bf16[64,4096]{1,0:T(8,128)(2,1)S(1)}, bf16[64,4096]{1,0:T(8,128)(2,1)S(1)}, u32[]{:S(2)}, u32[]{:S(2)}) collective-permute-start(bf16[64,4096]{1,0:T(8,128)(2,1)S(1)} %collective-permute-done.9.refs_11_.refs_1_), channel_id=1, source_target_pairs={{0,1},{1,0},{2,3},{3,2},{4,5},{5,4},{6,7},{7,6},{8,9},{9,8},{10,11... | collective-permute-start | bytes 1572872 | tf_op jit(solution)/shard_map/cot_behind_z/ppermute | solution.py:48
  49.6 4.7 %collective-permute-start.16 = (bf16[64,4096]{1,0:T(8,128)(2,1)S(1)}, bf16[64,4096]{1,0:T(8,128)(2,1)S(1)}, u32[]{:S(2)}, u32[]{:S(2)}) collective-permute-start(bf16[64,4096]{1,0:T(8,128)(2,1)S(1)} %ahead_z_copy.1), channel_id=1, source_target_pairs={{0,1},{1,0},{2,3},{3,2},{4,5},{5,4},{6,7},{7,6},{8,9},{9,8},{10,11... | collective-permute-start | bytes 1572872 | tf_op jit(solution)/shard_map/behind_z/ppermute | solution.py:48
  52.1 12.1 %collective-permute-start.17 = (bf16[32,4096]{1,0:T(8,128)(2,1)S(1)}, bf16[32,4096]{1,0:T(8,128)(2,1)S(1)}, u32[]{:S(2)}, u32[]{:S(2)}) collective-permute-start(bf16[32,4096]{1,0:T(8,128)(2,1)S(1)} %collective-permute-done.10.refs_12_.refs_0_), channel_id=1, source_target_pairs={{0,2},{1,3},{2,0},{3,1},{4,6},{5,7},{6,4},{7,5},{8,10},{9,11},{10,... | collective-permute-start | bytes 786440 | tf_op jit(solution)/shard_map/cot_far_z/ppermute | solution.py:48
  53.0 8.6 %collective-permute-start.20 = (bf16[64,4096]{1,0:T(8,128)(2,1)S(1)}, bf16[64,4096]{1,0:T(8,128)(2,1)S(1)}, u32[]{:S(2)}, u32[]{:S(2)}) collective-permute-start(bf16[64,4096]{1,0:T(8,128)(2,1)S(1)} %part.1), channel_id=1, source_target_pairs={{0,4},{1,13},{2,6},{3,15},{4,8},{5,1},{6,10},{7,3},{8,12},{9,5},{1... | collective-permute-start | bytes 1572872 | tf_op jit(solution)/shard_map/far/ppermute | solution.py:48
  61.6 4.8 %collective-permute-start.21 = (bf16[64,4096]{1,0:T(8,128)(2,1)S(1)}, bf16[64,4096]{1,0:T(8,128)(2,1)S(1)}, u32[]{:S(2)}, u32[]{:S(2)}) collective-permute-start(bf16[64,4096]{1,0:T(8,128)(2,1)S(1)} %far_copy.1), channel_id=1, source_target_pairs={{0,1},{1,0},{2,3},{3,2},{4,5},{5,4},{6,7},{7,6},{8,9},{9,8},{10,11... | collective-permute-start | bytes 1572872 | tf_op jit(solution)/shard_map/far_core/ppermute | solution.py:48
  64.1 1.9 %collective-permute-start.18 = (bf16[32,4096]{1,0:T(8,128)(2,1)S(1)}, bf16[32,4096]{1,0:T(8,128)(2,1)S(1)}, u32[]{:S(2)}, u32[]{:S(2)}) collective-permute-start(bf16[32,4096]{1,0:T(8,128)(2,1)S(1)} %collective-permute-done.10.refs_12_.refs_0_), channel_id=1, source_target_pairs={{0,1},{1,0},{2,3},{3,2},{4,5},{5,4},{6,7},{7,6},{8,9},{9,8},{10,11... | collective-permute-start | bytes 786440 | tf_op jit(solution)/shard_map/cot_far_core/ppermute | solution.py:48
  64.2 2.2 %collective-permute-start.19 = (bf16[32,4096]{1,0:T(8,128)(2,1)S(1)}, bf16[32,4096]{1,0:T(8,128)(2,1)S(1)}, u32[]{:S(2)}, u32[]{:S(2)}) collective-permute-start(bf16[32,4096]{1,0:T(8,128)(2,1)S(1)} %cot_far_z_copy.1), channel_id=1, source_target_pairs={{0,1},{1,0},{2,3},{3,2},{4,5},{5,4},{6,7},{7,6},{8,9},{9,8},{10,11... | collective-permute-start | bytes 786440 | tf_op jit(solution)/shard_map/cot_far_z_core/ppermute | solution.py:48
  80.1 4.3 %collective-permute-start.22 = (bf16[256,2304]{1,0:T(8,128)(2,1)S(1)}, bf16[256,2304]{1,0:T(8,128)(2,1)S(1)}, u32[]{:S(2)}, u32[]{:S(2)}) collective-permute-start(bf16[256,2304]{1,0:T(8,128)(2,1)S(1)} %get-tuple-element.42), channel_id=1, source_target_pairs={{0,1},{1,0},{2,3},{3,2},{4,5},{5,4},{6,7},{7,6},{8,9},{9,8},{10,11... | collective-permute-start | bytes 3538952 | tf_op jit(solution)/shard_map/got_b/ppermute | solution.py:48
  80.5 3.8 %collective-permute-start.23 = (bf16[256,1792]{1,0:T(8,128)(2,1)S(1)}, bf16[256,1792]{1,0:T(8,128)(2,1)S(1)}, u32[]{:S(2)}, u32[]{:S(2)}) collective-permute-start(bf16[256,1792]{1,0:T(8,128)(2,1)S(1)} %get-tuple-element.43), channel_id=1, source_target_pairs={{0,1},{1,0},{2,3},{3,2},{4,5},{5,4},{6,7},{7,6},{8,9},{9,8},{10,11... | collective-permute-start | bytes 2752520 | tf_op jit(solution)/shard_map/got_a/ppermute | solution.py:48
  84.5 14.6 %collective-permute-start.24 = (bf16[128,2304]{1,0:T(8,128)(2,1)S(1)}, bf16[128,2304]{1,0:T(8,128)(2,1)S(1)}, u32[]{:S(2)}, u32[]{:S(2)}) collective-permute-start(bf16[128,2304]{1,0:T(8,128)(2,1)S(1)} %away.1.refs_2_), channel_id=1, source_target_pairs={{0,2},{1,3},{2,0},{3,1},{4,6},{5,7},{6,4},{7,5},{8,10},{9,11},{10,... | collective-permute-start | bytes 1769480 | tf_op jit(solution)/shard_map/from_z/ppermute | solution.py:48
  85.3 6.1 %collective-permute-start.27 = (bf16[64,1792]{1,0:T(8,128)(2,1)S(1)}, bf16[64,1792]{1,0:T(8,128)(2,1)S(1)}, u32[]{:S(2)}, u32[]{:S(2)}) collective-permute-start(bf16[64,1792]{1,0:T(8,128)(2,1)S(1)} %to_far.1.refs_2_), channel_id=1, source_target_pairs={{0,12},{1,5},{2,14},{3,7},{4,0},{5,9},{6,2},{7,11},{8,4},{9,13},{1... | collective-permute-start | bytes 688136 | tf_op jit(solution)/shard_map/from_far/ppermute | solution.py:48
  91.4 9.2 %collective-permute-start.28 = (bf16[128,1792]{1,0:T(8,128)(2,1)S(1)}, bf16[128,1792]{1,0:T(8,128)(2,1)S(1)}, u32[]{:S(2)}, u32[]{:S(2)}) collective-permute-start(bf16[128,1792]{1,0:T(8,128)(2,1)S(1)} %to_home.1), channel_id=1, source_target_pairs={{0,12},{1,5},{2,14},{3,7},{4,0},{5,9},{6,2},{7,11},{8,4},{9,13},{1... | collective-permute-start | bytes 1376264 | tf_op jit(solution)/shard_map/home/ppermute | solution.py:48
  99.4 10.0 %collective-permute-start.26 = (bf16[64,2304]{1,0:T(8,128)(2,1)S(1)}, bf16[64,2304]{1,0:T(8,128)(2,1)S(1)}, u32[]{:S(2)}, u32[]{:S(2)}) collective-permute-start(bf16[64,2304]{1,0:T(8,128)(2,1)S(1)} %get-tuple-element.46), channel_id=1, source_target_pairs={{0,12},{1,5},{2,14},{3,7},{4,0},{5,9},{6,2},{7,11},{8,4},{9,13},{1... | collective-permute-start | bytes 884744 | tf_op jit(solution)/shard_map/home_b/ppermute | solution.py:48
  99.5 8.1 %collective-permute-start.25 = (bf16[32,2304]{1,0:T(8,128)(2,1)S(1)}, bf16[32,2304]{1,0:T(8,128)(2,1)S(1)}, u32[]{:S(2)}, u32[]{:S(2)}) collective-permute-start(bf16[32,2304]{1,0:T(8,128)(2,1)S(1)} %get-tuple-element.45), channel_id=1, source_target_pairs={{0,8},{1,9},{2,10},{3,11},{4,12},{5,13},{6,14},{7,15},{8,0},{9,1},... | collective-permute-start | bytes 442376 | tf_op jit(solution)/shard_map/far_b/ppermute | solution.py:48
  100.6 2.4 %collective-permute-start.29 = (bf16[32,1792]{1,0:T(8,128)(2,1)S(1)}, bf16[32,1792]{1,0:T(8,128)(2,1)S(1)}, u32[]{:S(2)}, u32[]{:S(2)}) collective-permute-start(bf16[32,1792]{1,0:T(8,128)(2,1)S(1)} %home_core_part.1), channel_id=1, source_target_pairs={{0,1},{1,0},{2,3},{3,2},{4,5},{5,4},{6,7},{7,6},{8,9},{9,8},{10,11... | collective-permute-start | bytes 344072 | tf_op jit(solution)/shard_map/home_core/ppermute | solution.py:48
  109.4 4.5 %collective-permute-start.31 = (bf16[32,2304]{1,0:T(8,128)(2,1)S(1)}, bf16[32,2304]{1,0:T(8,128)(2,1)S(1)}, u32[]{:S(2)}, u32[]{:S(2)}) collective-permute-start(bf16[32,2304]{1,0:T(8,128)(2,1)S(1)} %home_b_part.1), channel_id=1, source_target_pairs={{0,1},{1,0},{2,3},{3,2},{4,5},{5,4},{6,7},{7,6},{8,9},{9,8},{10,11... | collective-permute-start | bytes 442376 | tf_op jit(solution)/shard_map/home_b_core/ppermute | solution.py:48
  109.5 4.4 %collective-permute-start.32 = (bf16[32,1792]{1,0:T(8,128)(2,1)S(1)}, bf16[32,1792]{1,0:T(8,128)(2,1)S(1)}, u32[]{:S(2)}, u32[]{:S(2)}) collective-permute-start(bf16[32,1792]{1,0:T(8,128)(2,1)S(1)} %get-tuple-element.50), channel_id=1, source_target_pairs={{0,2},{1,3},{2,0},{3,1},{4,6},{5,7},{6,4},{7,5},{8,10},{9,11},{10,... | collective-permute-start | bytes 344072 | tf_op jit(solution)/shard_map/total_z/ppermute | solution.py:48
  (10 other events, 175.6 us)

commit v3 on v2

--- a/solution.py
+++ b/solution.py
@@ -12,10 +12,12 @@
 VMEM = pl.BlockSpec(memory_space=pltpu.VMEM)
 MIB = 1024 * 1024
 LONG = 10**11
-Y_FIRST = 1792
+Y_FIRST = 2688
 EXTRA = 512
-HIDDEN_LIMIT = 14
-BACK_LIMIT = 16
+SHORT = 10**9
+PARTS = (0, 48), (48, 16)
+HIDDEN_LIMIT = 10
+BACK_LIMIT = 10
 
 
 def like(*shape, dtype=bf16):
@@ -69,17 +71,21 @@
     return (i + 8) % 16
 
 
-def join(name, *pieces, after=(), flops=1):
+def join(name, *pieces, after=(), columns=None, flops=1):
     pieces = [p if isinstance(p, tuple) else (p, 0, p.shape[0]) for p in pieces]
+    columns = columns or pieces[0][0].shape[1]
 
     def body(*refs):
         out, at = refs[-1], 0
         for ref, (_, start, n) in zip(refs[:-1], pieces):
-            out[at : at + n] = ref[start : start + n]
+            have = min(columns, ref.shape[1])
+            out[at : at + n, :have] = ref[start : start + n, :have]
+            if have < columns:
+                out[at : at + n, have:] = ref[start : start + n, : columns - have]
             at += n
 
     rows = sum(n for _, _, n in pieces)
-    return local_kernel(name, body, like(rows, pieces[0][0].shape[1]), *[p for p, _, _ in pieces], after=after, flops=flops)
+    return local_kernel(name, body, like(rows, columns), *[p for p, _, _ in pieces], after=after, flops=flops)
 
 
 def prepare_kernel(keep_hbm, roster_hbm, parked, parked_scale, local, local_scale, gain, pending,
@@ -150,7 +156,7 @@
     def fill(pieces, blocks):
         at = 0
         for piece, start, count in blocks:
-            rows[at : at + count] = pieces[piece][start : start + count]
+            rows[at : at + count] = pieces[piece][start : start + count, : rows.shape[1]]
             at += count
 
     fill(cots, cot_blocks)
@@ -164,7 +170,7 @@
     dup[...] = (d * gate * sig).astype(bf16)
 
 
-def hidden(name, cots, cot_blocks, normeds, normed_blocks, weights, after=()):
+def hidden(name, cots, cot_blocks, normeds, normed_blocks, weights, after=(), flops=1):
     n_rows = sum(count for _, _, count in cot_blocks)
     d, units = weights[0].shape
     return local_kernel(
@@ -176,73 +182,52 @@
         *weights,
         after=after,
         scratch=[pltpu.VMEM((n_rows, d), bf16), pltpu.VMEM((n_rows, units), f32)],
-        flops=LONG,
+        flops=flops,
         limit=HIDDEN_LIMIT,
     )
 
 
-def back_kernel(start, g0, u0, g1, u1, g2, u2, w_gate, w_up, keep, send, g_rows, u_rows):
-    for rows, home, side, far in ((g_rows, g0, g1, g2), (u_rows, u0, u1, u2)):
-        rows[0:64] = home[0:64]
-        rows[64:192] = side[0:128]
-        rows[192:256] = far[0:64]
-        rows[256:320] = home[64:128]
-        rows[320:448] = side[128:256]
-        rows[448:512] = far[64:128]
-    n = keep.shape[1]
-    cols = slice(start, start + n)
-    transposed = (((1,), (1,)), ((), ()))
-    dn = lax.dot_general(g_rows[...], w_gate[cols, :], transposed, preferred_element_type=f32) + lax.dot_general(
-        u_rows[...], w_up[cols, :], transposed, preferred_element_type=f32
-    )
-    keep[...] = dn[:256].astype(bf16)
-    send[...] = dn[256:].astype(bf16)
-
-
-def back(name, start, n, grads, w_gate, w_up, after=()):
-    units = w_gate.shape[1]
-    return local_kernel(
-        name,
-        functools.partial(back_kernel, start),
-        (like(256, n), like(256, n)),
-        *grads,
-        w_gate,
-        w_up,
-        after=after,
-        scratch=[pltpu.VMEM((512, units), bf16)] * 2,
-        flops=LONG,
-        limit=BACK_LIMIT,
-    )
-
-
-def add(name, outs, *columns, after=()):
-    widths = [pieces[0].shape[1] for pieces in columns]
-    n_in = sum(len(pieces) for pieces in columns)
+def back(name, start, n, outs, grads, w_gate, w_up, after=(), flops=1):
+    def body(g, u, w_gate, w_up, *results):
+        cols = slice(start, start + n)
+        transposed = (((1,), (1,)), ((), ()))
+        dn = lax.dot_general(g[...], w_gate[cols, :], transposed, preferred_element_type=f32) + lax.dot_general(
+            u[...], w_up[cols, :], transposed, preferred_element_type=f32
+        )
+        for result, spans in zip(results, outs):
+            at = 0
+            for first, count in spans:
+                result[at : at + count] = dn[first : first + count].astype(bf16)
+                at += count
+
+    shapes = tuple(like(sum(count for _, count in spans), n) for spans in outs)
+    return local_kernel(name, body, shapes, *grads, w_gate, w_up, after=after, flops=flops, limit=BACK_LIMIT)
+
+
+def add(name, width, outs, *pieces, after=()):
+    pieces = [p if isinstance(p, tuple) else (p, 0) for p in pieces]
 
     def body(*refs):
-        for out, spans in zip(refs[n_in:], outs):
-            left, at_piece = 0, 0
-            for pieces, width in zip(columns, widths):
-                at = 0
-                for count, terms in spans:
-                    total = None
-                    for piece, start in terms:
-                        term = refs[at_piece + piece][start : start + count].astype(f32)
-                        total = term if total is None else total + term
-                    out[at : at + count, left : left + width] = total.astype(bf16)
-                    at += count
-                left += width
-                at_piece += len(pieces)
-
-    shapes = tuple(like(sum(count for count, _ in spans), sum(widths)) for spans in outs)
-    results = local_kernel(name, body, shapes, *[p for pieces in columns for p in pieces], after=after)
+        for out, spans in zip(refs[len(pieces) :], outs):
+            at = 0
+            for count, terms in spans:
+                total = None
+                for piece, start in terms:
+                    left = pieces[piece][1]
+                    term = refs[piece][start : start + count, left : left + width].astype(f32)
+                    total = term if total is None else total + term
+                out[at : at + count] = total.astype(out.dtype)
+                at += count
+
+    shapes = tuple(like(sum(count for count, _ in spans), width) for spans in outs)
+    results = local_kernel(name, body, shapes, *[p for p, _ in pieces], after=after)
     return results if len(outs) > 1 else results[0]
 
 
-def final_kernel(held, far_b, home_b, other_b, total, total_z, cot, unit, inv, gain, out):
+def final_kernel(held, home_far, home_b, other_b, total, total_z, cot, unit, inv, gain, out):
     split = total.shape[1]
     dn_a = total[...].astype(f32) + total_z[...].astype(f32)
-    dn_b = held[...].astype(f32) + far_b[...].astype(f32) + home_b[:32].astype(f32) + other_b[...].astype(f32)
+    dn_b = held[...].astype(f32) + home_far[...].astype(f32) + home_b[:32].astype(f32) + other_b[...].astype(f32)
     g_a, g_b = dn_a * gain[:, :split], dn_b * gain[:, split:]
     u_a, u_b = unit[:, :split], unit[:, split:]
     mean = (
@@ -316,85 +301,118 @@
     )
     normed_z = over_tensor("normed_z", normed, other_z)
     normed_core = over_tensor("normed_core", normed, other_core)
-    cot_part = join("cot_part", (cot_ahead, 0, 32), after=(normed, cot_z))
+    chip = join("chip", normed, normed_core, after=(cot_z,))
+    ahead = over_tensor("ahead", chip, along_y)
+    cot_part = join("cot_part", (cot_ahead, 0, 32), after=(normed, chip), columns=d + EXTRA)
     cot_far = over_tensor("cot_far", cot_part, along_y)
     cot_ahead_z = over_tensor("cot_ahead_z", cot_ahead, other_z)
-    cot_behind = over_tensor("cot_behind", cot_ahead, other_core)
     cot_z_core = over_tensor("cot_z_core", cot_z, other_core)
 
-    ahead = over_tensor("ahead", join("chip", normed, normed_core), along_y)
-    normed_z_core = over_tensor("normed_z_core", join("normed_z_copy", normed_z, after=(cot_part,)), other_core)
-    chip_z = join("chip_z", normed_z, normed_z_core)
+    normed_z_copies = [
+        join(f"normed_z_copy_{at}", (normed_z, at, 16), after=(cot_part,), flops=SHORT) for at in (0, 16)
+    ]
+    normed_z_core = [over_tensor("normed_z_core", part, other_core) for part in normed_z_copies]
+    chip_z = join("chip_z", normed_z, *normed_z_core)
     ahead_z = over_tensor("ahead_z", chip_z, along_y)
-    cot_far_z = over_tensor("cot_far_z", cot_far, other_z)
-    cot_far_core = over_tensor("cot_far_core", cot_far, other_core)
-    g0, u0 = hidden(
-        "hidden_home",
-        (cot, cot_z, cot_core, cot_z_core),
-        tuple((k, 0, 32) for k in range(4)),
-        (normed, normed_z, normed_core, normed_z_core),
-        tuple((k, 0, 32) for k in range(4)),
+    behind = [over_tensor(f"behind_{at}", join(f"behind_{at}", (ahead, at, n)), other_core) for at, n in PARTS]
+    cot_behind_z = [
+        over_tensor(f"cot_behind_z_{at}", join(f"cot_behind_z_{at}", (cot_ahead_z, at, n)), other_core) for at, n in PARTS
+    ]
+    cot_far_core = over_tensor("cot_far_core", join("cot_far_part", cot_far, (cot_ahead, 0, 16), columns=d), other_core)
+    cot_behind = over_tensor("cot_behind", join("cot_behind_part", (cot_ahead, 16, 48)), other_core)
+    cot_far_z = over_tensor("cot_far_z", join("cot_far_copy", cot_far, columns=d), other_z)
+    part = join("part", (ahead, 0, 32), (ahead_z, 0, 32))
+    far = over_tensor("far", part, along_y)
+    behind_z = over_tensor("behind_z", ahead_z, other_core)
+
+    home_blocks = tuple((k, 0, 32) for k in range(4))
+    near_blocks = home_blocks + tuple((4 + k, 32 * h, 32) for h in range(2) for k in range(2))
+    g1, u1 = hidden(
+        "hidden_near",
+        (cot, cot_z, cot_core, cot_z_core, cot_ahead, cot_ahead_z),
+        near_blocks,
+        (normed, normed_z, normed_core, chip_z, ahead, ahead_z),
+        tuple((k, 32 if k == 3 else start, n) for k, start, n in near_blocks),
         weights,
-        after=(cot_ahead_z, cot_far),
-    )
-    cot_behind_z = over_tensor("cot_behind_z", cot_ahead_z, other_core)
-    far = over_tensor("far", join("part", (ahead, 0, 32), (ahead_z, 0, 32), after=(g0,)), along_y)
-    behind = over_tensor("behind", join("ahead_copy", ahead, after=(g0,)), other_core)
-    behind_z = over_tensor("behind_z", join("ahead_z_copy", ahead_z, after=(g0,)), other_core)
-    sides = tuple((k + j, 32 * h, 32) for k in (0, 2) for h in range(2) for j in range(2))
-    g1, u1 = hidden(
-        "hidden_sides",
-        (cot_ahead, cot_ahead_z, cot_behind, cot_behind_z),
-        sides,
-        (ahead, ahead_z, behind, behind_z),
-        sides,
+        after=(*cot_behind_z, *behind, cot_far_core, cot_behind),
+        flops=LONG,
+    )
+    far_copy = join("far_copy", far, after=(g1,))
+    far_core = over_tensor("far_core", far_copy, other_core)
+    cot_far_z_copy = join("cot_far_z_copy", cot_far_z, after=(g1,))
+    cot_far_z_core = over_tensor("cot_far_z_core", cot_far_z_copy, other_core)
+    home_keep, home_send, ahead_keep = back(
+        "back_near",
+        0,
+        d,
+        (((0, 64),), ((64, 64),), ((128, 128),)),
+        (g1, u1),
+        w_gate,
+        w_up,
+        after=(behind_z, far_copy, cot_far_z_copy),
+    )
+    home_got = over_tensor("home_got", home_send, other_core)
+    g2, u2 = hidden(
+        "hidden_rest",
+        (cot_far_core, cot_behind, *cot_behind_z, cot_far, cot_far_z, cot_far_z_core),
+        ((0, 32, 16), (1, 0, 16), (2, 0, 32), (1, 16, 32), (2, 32, 16), (3, 0, 16),
+         (4, 0, 32), (5, 0, 32), (0, 0, 32), (6, 0, 32)),
+        (*behind, behind_z, far, far_core),
+        ((0, 0, 32), (2, 0, 32), (0, 32, 16), (1, 0, 16), (2, 32, 32), (3, 0, 64), (4, 0, 64)),
         weights,
-    )
-    cot_far_z_core = over_tensor("cot_far_z_core", join("cot_far_z_copy", cot_far_z, after=(g1,)), other_core)
-    far_core = over_tensor("far_core", join("far_copy", far, after=(g1,)), other_core)
-    g2, u2 = hidden(
-        "hidden_far",
-        (cot_far, cot_far_z, cot_far_core, cot_far_z_core),
-        tuple((k, 0, 32) for k in range(4)),
-        (far, far_core),
-        ((0, 0, 64), (1, 0, 64)),
-        weights,
-    )
-    grads = (g0, u0, g1, u1, g2, u2)
-
-    keep_a, send_a = back("back_a", 0, Y_FIRST, grads, w_gate, w_up)
+        after=(home_send,),
+        flops=LONG,
+    )
+    split = Y_FIRST
+    rest = ((0, 128), (192, 64)), ((128, 64),)
+    send_a, far_a = back("back_a", 0, split, rest, (g2, u2), w_gate, w_up, after=(home_got,), flops=LONG)
     got_a = over_tensor("got_a", send_a, other_core)
-    keep_b, send_b = back("back_b", Y_FIRST, d - Y_FIRST, grads, w_gate, w_up, after=(keep_a,))
+    send_b, far_b = back("back_b", split, d - split, rest, (g2, u2), w_gate, w_up, after=(far_a,), flops=LONG)
     got_b = over_tensor("got_b", send_b, other_core)
-    both = keep_a, got_a
-    to_far = add("to_far", [[(64, ((0, 192), (1, 192)))]], both, after=(keep_b,))
+
+    to_far = add("to_far", split, [[(64, ((0, 0), (1, 128)))]], far_a, got_a, after=(far_b,))
     from_far = over_tensor("from_far", to_far, back_y)
-    away = add("away", [[(32, ((0, 64 * k + 32), (1, 64 * k + 32))) for k in range(4)]], (keep_b, got_b), after=(to_far,))
+    to_home_x = add("to_home_x", split, [[(64, ((0, 64), (1, 64)))]], ahead_keep, got_a, after=(to_far,))
+    home_x = over_tensor("home_x", to_home_x, back_y)
+    pieces_b = (home_keep, split), (home_got, split), (ahead_keep, split), got_b, far_b
+
+    def terms_b(z):
+        at = 32 * z
+        return ((0, at), (1, at)), ((2, at), (3, at)), ((2, 64 + at), (3, 64 + at)), ((4, at), (3, 128 + at))
+
+    away = add("away", d - split, [[(32, t) for t in terms_b(1)]], *pieces_b, after=(to_home_x,))
     from_z = over_tensor("from_z", away, other_z)
-    near, side = add("near_side", [[(64, ((0, 0), (1, 0)))], [(128, ((0, 64), (1, 64)))]], both, after=(away,))
-    to_home = add("to_home", [[(64, ((0, 0), (1, 0))), (64, ((0, 64),))]], (side, from_far))
+    near = add("near", split, [[(64, ((0, 0), (1, 0)))]], home_keep, home_got, after=(away,))
+    to_home = add("to_home", split, [[(64, ((0, 0), (1, 0), (2, 0)))]], ahead_keep, got_a, from_far, after=(near,))
     home = over_tensor("home", to_home, back_y)
+    home_x_core = tuple(
+        over_tensor(name, join(name + "_part", (home_x, at, 32), after=(to_home,)), other_core)
+        for name, at in (("home_x_core", 0), ("home_x_core_z", 32))
+    )
+    home_own = join("home_own", home_x, after=(to_home,))
     held, held_side, held_far = add(
         "held",
-        [
-            [(32, ((0, 64 * k), (1, 64 * k), (2, 32 * k))) for k in ks]
-            for ks in ((0,), (1, 2), (3,))
-        ],
-        (keep_b, got_b, from_z),
-    )
-    home_core = tuple(
-        over_tensor(name, join(name + "_part", (home, at, 32), after=(held,)), other_core)
-        for name, at in (("home_core", 64), ("home_core_z", 96))
-    )
+        d - split,
+        [[(32, terms_b(0)[k] + ((5, 32 * k),)) for k in ks] for ks in ((0,), (1, 2), (3,))],
+        *pieces_b,
+        from_z,
+        after=(home_own,),
+    )
+    home_b = over_tensor("home_b", held_side, back_y)
+    home_far = over_tensor("home_far", held_far, across_y)
     total, total_away = add(
-        "total", [[(32, ((0, at), (1, at), (2 + at // 32, 0)))] for at in (0, 32)], (near, home, *home_core)
+        "total",
+        split,
+        [[(32, ((0, at), (1, at), (2 + at // 32, 0)))] for at in (0, 32)],
+        near,
+        home,
+        *home_x_core,
+        after=(held,),
     )
     total_z = over_tensor("total_z", total_away, other_z)
-    home_b = over_tensor("home_b", held_side, back_y)
-    far_b = over_tensor("far_b", held_far, across_y)
-    home_b_core = over_tensor("home_b_core", join("home_b_part", (home_b, 32, 32), after=(total, far_b)), other_core)
+    home_b_core = over_tensor("home_b_core", join("home_b_part", (home_b, 32, 32), after=(total, home_far)), other_core)
     return local_kernel(
-        "final", final_kernel, like(shard, d), held, far_b, home_b, home_b_core, total, total_z, cot, unit, inv, gain
+        "final", final_kernel, like(shard, d), held, home_far, home_b, home_b_core, total, total_z, cot, unit, inv, gain
     )[None]
 
 

time: 116 us -> 99.3 us (0.86)
  waiting for transfers between devices: 43.3 us -> 28.3 us
  Pallas kernels: 28.8 us -> 27 us
    ppermute x31 -> x36, waiting for transfers between devices: 37.2 us -> 22.2 us  [over_tensor(): lax.ppermute(shard, 'tensor', [(i, move(i)) for i in range(lax.axis_size(...]
    pallas_call x28 -> x36, Pallas kernels: 28.8 us -> 27 us  [local_kernel(): pl.pallas_call(run, out_shape=outs, in_specs=[anywhere if hbm else VMEM]...]
    ppermute x31 -> x36, starting transfers between devices: 34.6 us -> 35.4 us  [over_tensor(): lax.ppermute(shard, 'tensor', [(i, move(i)) for i in range(lax.axis_size(...]
  transfers between devices with their start and end apart: 33 -> 38, of which waited for: 19 -> 16; matrix products, arithmetic and copies ran while one was open for 0% -> 0% of each run, Pallas kernels for 11% -> 22%
where the time goes in v3:
time: 99.3 us; the launch traced here: 99.1 us
  starting transfers between devices  43.4 us (44%)
  waiting for transfers between devices  28.3 us (28%)
  Pallas kernels  27 us (27%)
    ppermute x36, starting transfers between devices, over_tensor(): lax.ppermute(shard, 'tensor', [(i, move(i)) for i in range(lax.axis_size(...  35.4 us
    pallas_call x36, Pallas kernels, local_kernel(): pl.pallas_call(run, out_shape=outs, in_specs=[anywhere if hbm else VMEM]...  27 us
    ppermute x36, waiting for transfers between devices, over_tensor(): lax.ppermute(shard, 'tensor', [(i, move(i)) for i in range(lax.axis_size(...  22.2 us
    ppermute x1, starting transfers between devices, on_device(): cot = lax.ppermute(cot_source, 'section', shift_pairs)  6.69 us
    ppermute x1, waiting for transfers between devices, on_device(): cot = lax.ppermute(cot_source, 'section', shift_pairs)  3.69 us
    ppermute x1, waiting for transfers between devices, on_device(): fetched = lax.ppermute(payload, 'section', stash_pairs)  2.42 us
  transfers between devices with their start and end apart: 38, of which 16 were waited for; matrix products, arithmetic and copies ran while one was open for 0% of the time, Pallas kernels for 22%

profile of v3, /device:TPU:1, one launch (start us, length us, event | category | flops | bytes accessed | tf_op | source)
XLA Modules:
  0.0 99.1 jit_solution(15988947935112513107)
XLA Ops:
  0.0 1.4 %prepare.1 = (bf16[32,4608]{1,0:T(8,128)(2,1)S(1)}, bf16[32,4736]{1,0:T(8,128)(2,1)S(1)}, f32[1,4096]{1,0:T(1,128)S(1)}, bf16[32,4096]{1,0:T(8,128)(2,1)S(1)}) custom-call(s32[8]{0:T(128)} %refs_0_.1, s32[8]{0:T(128)} %refs_1_.1, bf16[2,32,4096]{2,1,0:T(8,128)(2,1)} %bitcast.27, bf16[2,32]{1,0:T(2,128)(2,1)} %bitcast.30, bf16[2,32,4096]{2,1,0:T(8,128)(2,1)} %bitcast.28, ...), custom_call_target="tpu_custom_call" | custom-call | flops 1 | bytes 1 | tf_op jit(solution)/shard_map/prepare/pallas_call | solution.py:36
  1.4 6.7 %collective-permute-start = (bf16[32,4096]{1,0:T(8,128)(2,1)S(1)}, bf16[32,4096]{1,0:T(8,128)(2,1)S(1)}, u32[]{:S(2)}, u32[]{:S(2)}) collective-permute-start(bf16[32,4096]{1,0:T(8,128)(2,1)S(1)} %get-tuple-element.28), channel_id=1, source_target_pairs={{16,0},{32,16},{48,32},{64,48},{80,64},{96,80},{112,96},{0,112},{1... | collective-permute-start | bytes 786440 | tf_op jit(solution)/shard_map/shift/ppermute | solution.py:283
  8.1 1.3 %collective-permute-start.6 = (bf16[32,4608]{1,0:T(8,128)(2,1)S(1)}, bf16[32,4608]{1,0:T(8,128)(2,1)S(1)}, u32[]{:S(2)}, u32[]{:S(2)}) collective-permute-start(bf16[32,4608]{1,0:T(8,128)(2,1)S(1)} %get-tuple-element.30), channel_id=1, source_target_pairs={{112,0},{96,16},{80,32},{64,48},{113,1},{97,17},{81,33},{65,49},{1... | collective-permute-start | bytes 884744 | tf_op jit(solution)/shard_map/fetched/ppermute | solution.py:281
  9.4 3.7 %collective-permute-done.refs_0_ = bf16[32,4096]{1,0:T(8,128)(2,1)S(1)} collective-permute-done((bf16[32,4096]{1,0:T(8,128)(2,1)S(1)}, bf16[32,4096]{1,0:T(8,128)(2,1)S(1)}, u32[]{:S(2)}, u32[]{:S(2)}) %collective-permute-start) | collective-permute-done | bytes 262176 | tf_op jit(solution)/shard_map/shift/ppermute | solution.py:283
  13.1 1.6 %collective-permute-start.2 = (bf16[32,4096]{1,0:T(8,128)(2,1)S(1)}, bf16[32,4096]{1,0:T(8,128)(2,1)S(1)}, u32[]{:S(2)}, u32[]{:S(2)}) collective-permute-start(bf16[32,4096]{1,0:T(8,128)(2,1)S(1)} %cot.1.refs_0_.refs_6_), channel_id=1, source_target_pairs={{0,1},{1,0},{2,3},{3,2},{4,5},{5,4},{6,7},{7,6},{8,9},{9,8},{10,11... | collective-permute-start | bytes 786440 | tf_op jit(solution)/shard_map/cot_core/ppermute | solution.py:50
  15.9 2.8 %collective-permute-start.4 = (bf16[64,4096]{1,0:T(8,128)(2,1)S(1)}, bf16[64,4096]{1,0:T(8,128)(2,1)S(1)}, u32[]{:S(2)}, u32[]{:S(2)}) collective-permute-start(bf16[64,4096]{1,0:T(8,128)(2,1)S(1)} %cot_chip.1.refs_3_), channel_id=1, source_target_pairs={{0,4},{1,13},{2,6},{3,15},{4,8},{5,1},{6,10},{7,3},{8,12},{9,5},{1... | collective-permute-start | bytes 1572872 | tf_op jit(solution)/shard_map/cot_ahead/ppermute | solution.py:50
  18.7 2.4 %collective-permute-done.6.refs_1_ = bf16[32,4608]{1,0:T(8,128)(2,1)S(1)} collective-permute-done((bf16[32,4608]{1,0:T(8,128)(2,1)S(1)}, bf16[32,4608]{1,0:T(8,128)(2,1)S(1)}, u32[]{:S(2)}, u32[]{:S(2)}) %collective-permute-start.6) | collective-permute-done | bytes 294944 | tf_op jit(solution)/shard_map/fetched/ppermute | solution.py:281
  21.5 2.0 %collective-permute-start.8 = (bf16[32,4096]{1,0:T(8,128)(2,1)S(1)}, bf16[32,4096]{1,0:T(8,128)(2,1)S(1)}, u32[]{:S(2)}, u32[]{:S(2)}) collective-permute-start(bf16[32,4096]{1,0:T(8,128)(2,1)S(1)} %get-tuple-element.32.refs_0_.refs_1_.refs_6_), channel_id=1, source_target_pairs={{0,1},{1,0},{2,3},{3,2},{4,5},{5,4},{6,7},{7,6},{8,9},{9,8},{10,11... | collective-permute-start | bytes 786440 | tf_op jit(solution)/shard_map/normed_core/ppermute | solution.py:50
  24.7 2.8 %collective-permute-start.11 = (bf16[64,4096]{1,0:T(8,128)(2,1)S(1)}, bf16[64,4096]{1,0:T(8,128)(2,1)S(1)}, u32[]{:S(2)}, u32[]{:S(2)}) collective-permute-start(bf16[64,4096]{1,0:T(8,128)(2,1)S(1)} %chip.1.refs_2_), channel_id=1, source_target_pairs={{0,4},{1,13},{2,6},{3,15},{4,8},{5,1},{6,10},{7,3},{8,12},{9,5},{1... | collective-permute-start | bytes 1572872 | tf_op jit(solution)/shard_map/ahead/ppermute | solution.py:50
  28.4 3.0 %collective-permute-done.7.refs_0_.refs_7_ = bf16[32,4096]{1,0:T(8,128)(2,1)S(1)} collective-permute-done((bf16[32,4096]{1,0:T(8,128)(2,1)S(1)}, bf16[32,4096]{1,0:T(8,128)(2,1)S(1)}, u32[]{:S(2)}, u32[]{:S(2)}) %collective-permute-start.7) | collective-permute-done | bytes 262176 | tf_op jit(solution)/shard_map/normed_z/ppermute | solution.py:50
  31.4 1.4 %collective-permute-start.10 = (bf16[16,4096]{1,0:T(8,128)(2,1)S(1)}, bf16[16,4096]{1,0:T(8,128)(2,1)S(1)}, u32[]{:S(2)}, u32[]{:S(2)}) collective-permute-start(bf16[16,4096]{1,0:T(8,128)(2,1)S(1)} %normed_z_copy_16.1), channel_id=1, source_target_pairs={{0,1},{1,0},{2,3},{3,2},{4,5},{5,4},{6,7},{7,6},{8,9},{9,8},{10,11... | collective-permute-start | bytes 393224 | tf_op jit(solution)/shard_map/normed_z_core/ppermute | solution.py:50
  32.9 2.8 %collective-permute-start.17 = (bf16[32,4608]{1,0:T(8,128)(2,1)S(1)}, bf16[32,4608]{1,0:T(8,128)(2,1)S(1)}, u32[]{:S(2)}, u32[]{:S(2)}) collective-permute-start(bf16[32,4608]{1,0:T(8,128)(2,1)S(1)} %cot_part.1.refs_1_), channel_id=1, source_target_pairs={{0,4},{1,13},{2,6},{3,15},{4,8},{5,1},{6,10},{7,3},{8,12},{9,5},{1... | collective-permute-start | bytes 884744 | tf_op jit(solution)/shard_map/cot_far/ppermute | solution.py:50
  35.8 1.3 %collective-permute-start.12 = (bf16[64,4096]{1,0:T(8,128)(2,1)S(1)}, bf16[64,4096]{1,0:T(8,128)(2,1)S(1)}, u32[]{:S(2)}, u32[]{:S(2)}) collective-permute-start(bf16[64,4096]{1,0:T(8,128)(2,1)S(1)} %chip_z.1.refs_9_), channel_id=1, source_target_pairs={{0,4},{1,13},{2,6},{3,15},{4,8},{5,1},{6,10},{7,3},{8,12},{9,5},{1... | collective-permute-start | bytes 1572872 | tf_op jit(solution)/shard_map/ahead_z/ppermute | solution.py:50
  37.8 1.6 %collective-permute-done.17.refs_0_.refs_4_ = bf16[32,4608]{1,0:T(8,128)(2,1)S(1)} collective-permute-done((bf16[32,4608]{1,0:T(8,128)(2,1)S(1)}, bf16[32,4608]{1,0:T(8,128)(2,1)S(1)}, u32[]{:S(2)}, u32[]{:S(2)}) %collective-permute-start.17) | collective-permute-done | bytes 294944 | tf_op jit(solution)/shard_map/cot_far/ppermute | solution.py:50
  39.4 2.0 %collective-permute-start.19 = (bf16[48,4096]{1,0:T(8,128)(2,1)S(1)}, bf16[48,4096]{1,0:T(8,128)(2,1)S(1)}, u32[]{:S(2)}, u32[]{:S(2)}) collective-permute-start(bf16[48,4096]{1,0:T(8,128)(2,1)S(1)} %cot_behind_part.1), channel_id=1, source_target_pairs={{0,1},{1,0},{2,3},{3,2},{4,5},{5,4},{6,7},{7,6},{8,9},{9,8},{10,11... | collective-permute-start | bytes 1179656 | tf_op jit(solution)/shard_map/cot_behind/ppermute | solution.py:50
  41.4 1.2 %collective-permute-done.5.refs_0_.refs_5_ = bf16[64,4096]{1,0:T(8,128)(2,1)S(1)} collective-permute-done((bf16[64,4096]{1,0:T(8,128)(2,1)S(1)}, bf16[64,4096]{1,0:T(8,128)(2,1)S(1)}, u32[]{:S(2)}, u32[]{:S(2)}) %collective-permute-start.5) | collective-permute-done | bytes 524320 | tf_op jit(solution)/shard_map/cot_ahead_z/ppermute | solution.py:50
  42.6 0.9 collective-permute-start.15
  45.0 2.0 %collective-permute-start.14 = (bf16[16,4096]{1,0:T(8,128)(2,1)S(1)}, bf16[16,4096]{1,0:T(8,128)(2,1)S(1)}, u32[]{:S(2)}, u32[]{:S(2)}) collective-permute-start(bf16[16,4096]{1,0:T(8,128)(2,1)S(1)} %cot_behind_z_48.1), channel_id=1, source_target_pairs={{0,1},{1,0},{2,3},{3,2},{4,5},{5,4},{6,7},{7,6},{8,9},{9,8},{10,11... | collective-permute-start | bytes 393224 | tf_op jit(solution)/shard_map/cot_behind_z_48/ppermute | solution.py:50
  47.9 1.5 %collective-permute-start.21 = (bf16[64,4096]{1,0:T(8,128)(2,1)S(1)}, bf16[64,4096]{1,0:T(8,128)(2,1)S(1)}, u32[]{:S(2)}, u32[]{:S(2)}) collective-permute-start(bf16[64,4096]{1,0:T(8,128)(2,1)S(1)} %part.1), channel_id=1, source_target_pairs={{0,4},{1,13},{2,6},{3,15},{4,8},{5,1},{6,10},{7,3},{8,12},{9,5},{1... | collective-permute-start | bytes 1572872 | tf_op jit(solution)/shard_map/far/ppermute | solution.py:50
  49.5 6.8 %hidden_near.1 = (bf16[256,896]{1,0:T(8,128)(2,1)S(1)}, bf16[256,896]{1,0:T(8,128)(2,1)S(1)}) custom-call(bf16[32,4096]{1,0:T(8,128)(2,1)S(1)} %cot.1.refs_0_.refs_6_, bf16[32,4096]{1,0:T(8,128)(2,1)S(1)} %collective-permute-done.1.refs_2_.refs_1_, bf16[32,4096]{1,0:T(8,128)(2,1)S(1)} %collective-permute-done.2.refs_1_.refs_2_, ...), custom_call_target="tpu_custom_call" | custom-call | flops 99999997952 | bytes 1 | tf_op jit(solution)/shard_map/hidden_near/pallas_call | solution.py:36
  56.4 2.3 %collective-permute-start.25 = (bf16[64,4096]{1,0:T(8,128)(2,1)S(1)}, bf16[64,4096]{1,0:T(8,128)(2,1)S(1)}, u32[]{:S(2)}, u32[]{:S(2)}) collective-permute-start(bf16[64,4096]{1,0:T(8,128)(2,1)S(1)} %far_copy.1.refs_5_), channel_id=1, source_target_pairs={{0,1},{1,0},{2,3},{3,2},{4,5},{5,4},{6,7},{7,6},{8,9},{9,8},{10,11... | collective-permute-start | bytes 1572872 | tf_op jit(solution)/shard_map/far_core/ppermute | solution.py:50
  58.8 4.5 %back_near.1 = (bf16[64,4096]{1,0:T(8,128)(2,1)S(1)}, bf16[64,4096]{1,0:T(8,128)(2,1)S(1)}, bf16[128,4096]{1,0:T(8,128)(2,1)S(1)}) custom-call(bf16[256,896]{1,0:T(8,128)(2,1)S(1)} %get-tuple-element.33.refs_1_.refs_0_, bf16[256,896]{1,0:T(8,128)(2,1)S(1)} %get-tuple-element.34.refs_1_, bf16[4096,896]{1,0:T(8,128)(2,1)S(1)} %bitcast.12, ...), custom_call_target="tpu_custom_call" | custom-call | flops 1 | bytes 1 | tf_op jit(solution)/shard_map/back_near/pallas_call | solution.py:36
  64.1 6.8 %hidden_rest.1 = (bf16[256,896]{1,0:T(8,128)(2,1)S(1)}, bf16[256,896]{1,0:T(8,128)(2,1)S(1)}) custom-call(bf16[48,4096]{1,0:T(8,128)(2,1)S(1)} %collective-permute-done.18.refs_19_.refs_0_, bf16[48,4096]{1,0:T(8,128)(2,1)S(1)} %collective-permute-done.19.refs_20_.refs_1_, bf16[48,4096]{1,0:T(8,128)(2,1)S(1)} %collective-permute-done.13.refs_15_.refs_2_, ...), custom_call_target="tpu_custom_call" | custom-call | flops 99999997952 | bytes 1 | tf_op jit(solution)/shard_map/hidden_rest/pallas_call | solution.py:36
  70.9 3.2 %back_a.1 = (bf16[192,2688]{1,0:T(8,128)(2,1)S(1)}, bf16[64,2688]{1,0:T(8,128)(2,1)S(1)}) custom-call(bf16[256,896]{1,0:T(8,128)(2,1)S(1)} %get-tuple-element.38.refs_0_, bf16[256,896]{1,0:T(8,128)(2,1)S(1)} %get-tuple-element.39.refs_1_, bf16[4096,896]{1,0:T(8,128)(2,1)S(1)} %bitcast.14, bf16[4096,896]{1,0:T(8,128)(2,1)S(1)} %bitcast.21, ...), custom_call_target="tpu_custom_call" | custom-call | flops 99999997952 | bytes 1 | tf_op jit(solution)/shard_map/back_a/pallas_call | solution.py:36
  74.2 1.8 %back_b.1 = (bf16[192,1408]{1,0:T(8,128)(2,1)S(1)}, bf16[64,1408]{1,0:T(8,128)(2,1)S(1)}) custom-call(bf16[256,896]{1,0:T(8,128)(2,1)S(1)} %get-tuple-element.38.refs_0_, bf16[256,896]{1,0:T(8,128)(2,1)S(1)} %get-tuple-element.39.refs_1_, bf16[4096,896]{1,0:T(8,128)(2,1)S(1)} %bitcast.15, bf16[4096,896]{1,0:T(8,128)(2,1)S(1)} %bitcast.22, ...), custom_call_target="tpu_custom_call" | custom-call | flops 99999997952 | bytes 1 | tf_op jit(solution)/shard_map/back_b/pallas_call | solution.py:36
  79.2 5.1 %collective-permute-done.30.refs_2_ = bf16[64,2688]{1,0:T(8,128)(2,1)S(1)} collective-permute-done((bf16[64,2688]{1,0:T(8,128)(2,1)S(1)}, bf16[64,2688]{1,0:T(8,128)(2,1)S(1)}, u32[]{:S(2)}, u32[]{:S(2)}) %collective-permute-start.30) | collective-permute-done | bytes 344096 | tf_op jit(solution)/shard_map/from_far/ppermute | solution.py:50
  84.8 3.2 %collective-permute-done.29.refs_0_ = bf16[64,2688]{1,0:T(8,128)(2,1)S(1)} collective-permute-done((bf16[64,2688]{1,0:T(8,128)(2,1)S(1)}, bf16[64,2688]{1,0:T(8,128)(2,1)S(1)}, u32[]{:S(2)}, u32[]{:S(2)}) %collective-permute-start.29) | collective-permute-done | bytes 344096 | tf_op jit(solution)/shard_map/home_x/ppermute | solution.py:50
  89.0 2.5 %collective-permute-start.31 = (bf16[32,1408]{1,0:T(8,128)(2,1)S(1)}, bf16[32,1408]{1,0:T(8,128)(2,1)S(1)}, u32[]{:S(2)}, u32[]{:S(2)}) collective-permute-start(bf16[32,1408]{1,0:T(8,128)(2,1)S(1)} %get-tuple-element.45), channel_id=1, source_target_pairs={{0,8},{1,9},{2,10},{3,11},{4,12},{5,13},{6,14},{7,15},{8,0},{9,1},... | collective-permute-start | bytes 270344 | tf_op jit(solution)/shard_map/home_far/ppermute | solution.py:50
  93.0 2.3 %collective-permute-done.31.refs_2_.refs_1_ = bf16[32,1408]{1,0:T(8,128)(2,1)S(1)} collective-permute-done((bf16[32,1408]{1,0:T(8,128)(2,1)S(1)}, bf16[32,1408]{1,0:T(8,128)(2,1)S(1)}, u32[]{:S(2)}, u32[]{:S(2)}) %collective-permute-start.31) | collective-permute-done | bytes 90144 | tf_op jit(solution)/shard_map/home_far/ppermute | solution.py:50
  95.4 1.3 %collective-permute-done.32.refs_0_.refs_2_ = bf16[64,1408]{1,0:T(8,128)(2,1)S(1)} collective-permute-done((bf16[64,1408]{1,0:T(8,128)(2,1)S(1)}, bf16[64,1408]{1,0:T(8,128)(2,1)S(1)}, u32[]{:S(2)}, u32[]{:S(2)}) %collective-permute-start.32) | collective-permute-done | bytes 180256 | tf_op jit(solution)/shard_map/home_b/ppermute | solution.py:50
  97.2 0.9 collective-permute-done.36.refs_3_
  98.1 1.0 %final.1 = bf16[32,4096]{1,0:T(8,128)(2,1)} custom-call(bf16[32,1408]{1,0:T(8,128)(2,1)S(1)} %get-tuple-element.44.refs_4_.refs_0_, bf16[32,1408]{1,0:T(8,128)(2,1)S(1)} %collective-permute-done.31.refs_2_.refs_1_, bf16[64,1408]{1,0:T(8,128)(2,1)S(1)} %collective-permute-done.32.refs_0_.refs_2_, bf16[32,1408]{1,0:T(8,128)(2,1)S(1)} %collective-permute-done.36.refs_3_, ...), custom_call_target="tpu_custom_call" | custom-call | flops 1 | bytes 1 | tf_op jit(solution)/shard_map/final/pallas_call | solution.py:36
  (103 shorter events, 14.4 us)
Async XLA Ops:
  1.4 11.7 %collective-permute-start = (bf16[32,4096]{1,0:T(8,128)(2,1)S(1)}, bf16[32,4096]{1,0:T(8,128)(2,1)S(1)}, u32[]{:S(2)}, u32[]{:S(2)}) collective-permute-start(bf16[32,4096]{1,0:T(8,128)(2,1)S(1)} %get-tuple-element.28), channel_id=1, source_target_pairs={{16,0},{32,16},{48,32},{64,48},{80,64},{96,80},{112,96},{0,112},{1... | collective-permute-start | bytes 786440 | tf_op jit(solution)/shard_map/shift/ppermute | solution.py:283
  8.1 13.1 %collective-permute-start.6 = (bf16[32,4608]{1,0:T(8,128)(2,1)S(1)}, bf16[32,4608]{1,0:T(8,128)(2,1)S(1)}, u32[]{:S(2)}, u32[]{:S(2)}) collective-permute-start(bf16[32,4608]{1,0:T(8,128)(2,1)S(1)} %get-tuple-element.30), channel_id=1, source_target_pairs={{112,0},{96,16},{80,32},{64,48},{113,1},{97,17},{81,33},{65,49},{1... | collective-permute-start | bytes 884744 | tf_op jit(solution)/shard_map/fetched/ppermute | solution.py:281
  14.7 9.5 %collective-permute-start.1 = (bf16[32,4096]{1,0:T(8,128)(2,1)S(1)}, bf16[32,4096]{1,0:T(8,128)(2,1)S(1)}, u32[]{:S(2)}, u32[]{:S(2)}) collective-permute-start(bf16[32,4096]{1,0:T(8,128)(2,1)S(1)} %cot.1.refs_0_.refs_6_), channel_id=1, source_target_pairs={{0,2},{1,3},{2,0},{3,1},{4,6},{5,7},{6,4},{7,5},{8,10},{9,11},{10,... | collective-permute-start | bytes 786440 | tf_op jit(solution)/shard_map/cot_z/ppermute | solution.py:50
  15.9 11.6 %collective-permute-start.4 = (bf16[64,4096]{1,0:T(8,128)(2,1)S(1)}, bf16[64,4096]{1,0:T(8,128)(2,1)S(1)}, u32[]{:S(2)}, u32[]{:S(2)}) collective-permute-start(bf16[64,4096]{1,0:T(8,128)(2,1)S(1)} %cot_chip.1.refs_3_), channel_id=1, source_target_pairs={{0,4},{1,13},{2,6},{3,15},{4,8},{5,1},{6,10},{7,3},{8,12},{9,5},{1... | collective-permute-start | bytes 1572872 | tf_op jit(solution)/shard_map/cot_ahead/ppermute | solution.py:50
  23.5 7.9 %collective-permute-start.7 = (bf16[32,4096]{1,0:T(8,128)(2,1)S(1)}, bf16[32,4096]{1,0:T(8,128)(2,1)S(1)}, u32[]{:S(2)}, u32[]{:S(2)}) collective-permute-start(bf16[32,4096]{1,0:T(8,128)(2,1)S(1)} %get-tuple-element.32.refs_0_.refs_1_.refs_6_), channel_id=1, source_target_pairs={{0,2},{1,3},{2,0},{3,1},{4,6},{5,7},{6,4},{7,5},{8,10},{9,11},{10,... | collective-permute-start | bytes 786440 | tf_op jit(solution)/shard_map/normed_z/ppermute | solution.py:50
  24.7 12.4 %collective-permute-start.11 = (bf16[64,4096]{1,0:T(8,128)(2,1)S(1)}, bf16[64,4096]{1,0:T(8,128)(2,1)S(1)}, u32[]{:S(2)}, u32[]{:S(2)}) collective-permute-start(bf16[64,4096]{1,0:T(8,128)(2,1)S(1)} %chip.1.refs_2_), channel_id=1, source_target_pairs={{0,4},{1,13},{2,6},{3,15},{4,8},{5,1},{6,10},{7,3},{8,12},{9,5},{1... | collective-permute-start | bytes 1572872 | tf_op jit(solution)/shard_map/ahead/ppermute | solution.py:50
  27.5 15.1 %collective-permute-start.5 = (bf16[64,4096]{1,0:T(8,128)(2,1)S(1)}, bf16[64,4096]{1,0:T(8,128)(2,1)S(1)}, u32[]{:S(2)}, u32[]{:S(2)}) collective-permute-start(bf16[64,4096]{1,0:T(8,128)(2,1)S(1)} %collective-permute-done.4.refs_0_.refs_1_.refs_4_), channel_id=1, source_target_pairs={{0,2},{1,3},{2,0},{3,1},{4,6},{5,7},{6,4},{7,5},{8,10},{9,11},{10,... | collective-permute-start | bytes 1572872 | tf_op jit(solution)/shard_map/cot_ahead_z/ppermute | solution.py:50
  31.4 4.3 %collective-permute-start.10 = (bf16[16,4096]{1,0:T(8,128)(2,1)S(1)}, bf16[16,4096]{1,0:T(8,128)(2,1)S(1)}, u32[]{:S(2)}, u32[]{:S(2)}) collective-permute-start(bf16[16,4096]{1,0:T(8,128)(2,1)S(1)} %normed_z_copy_16.1), channel_id=1, source_target_pairs={{0,1},{1,0},{2,3},{3,2},{4,5},{5,4},{6,7},{7,6},{8,9},{9,8},{10,11... | collective-permute-start | bytes 393224 | tf_op jit(solution)/shard_map/normed_z_core/ppermute | solution.py:50
  32.9 6.5 %collective-permute-start.17 = (bf16[32,4608]{1,0:T(8,128)(2,1)S(1)}, bf16[32,4608]{1,0:T(8,128)(2,1)S(1)}, u32[]{:S(2)}, u32[]{:S(2)}) collective-permute-start(bf16[32,4608]{1,0:T(8,128)(2,1)S(1)} %cot_part.1.refs_1_), channel_id=1, source_target_pairs={{0,4},{1,13},{2,6},{3,15},{4,8},{5,1},{6,10},{7,3},{8,12},{9,5},{1... | collective-permute-start | bytes 884744 | tf_op jit(solution)/shard_map/cot_far/ppermute | solution.py:50
  35.8 9.2 %collective-permute-start.12 = (bf16[64,4096]{1,0:T(8,128)(2,1)S(1)}, bf16[64,4096]{1,0:T(8,128)(2,1)S(1)}, u32[]{:S(2)}, u32[]{:S(2)}) collective-permute-start(bf16[64,4096]{1,0:T(8,128)(2,1)S(1)} %chip_z.1.refs_9_), channel_id=1, source_target_pairs={{0,4},{1,13},{2,6},{3,15},{4,8},{5,1},{6,10},{7,3},{8,12},{9,5},{1... | collective-permute-start | bytes 1572872 | tf_op jit(solution)/shard_map/ahead_z/ppermute | solution.py:50
  37.1 6.4 %collective-permute-start.3 = (bf16[32,4096]{1,0:T(8,128)(2,1)S(1)}, bf16[32,4096]{1,0:T(8,128)(2,1)S(1)}, u32[]{:S(2)}, u32[]{:S(2)}) collective-permute-start(bf16[32,4096]{1,0:T(8,128)(2,1)S(1)} %collective-permute-done.1.refs_2_.refs_1_), channel_id=1, source_target_pairs={{0,1},{1,0},{2,3},{3,2},{4,5},{5,4},{6,7},{7,6},{8,9},{9,8},{10,11... | collective-permute-start | bytes 786440 | tf_op jit(solution)/shard_map/cot_z_core/ppermute | solution.py:50
  37.1 6.5 %collective-permute-start.16 = (bf16[16,4096]{1,0:T(8,128)(2,1)S(1)}, bf16[16,4096]{1,0:T(8,128)(2,1)S(1)}, u32[]{:S(2)}, u32[]{:S(2)}) collective-permute-start(bf16[16,4096]{1,0:T(8,128)(2,1)S(1)} %behind_48.1), channel_id=1, source_target_pairs={{0,1},{1,0},{2,3},{3,2},{4,5},{5,4},{6,7},{7,6},{8,9},{9,8},{10,11... | collective-permute-start | bytes 393224 | tf_op jit(solution)/shard_map/behind_48/ppermute | solution.py:50
  39.4 7.6 %collective-permute-start.19 = (bf16[48,4096]{1,0:T(8,128)(2,1)S(1)}, bf16[48,4096]{1,0:T(8,128)(2,1)S(1)}, u32[]{:S(2)}, u32[]{:S(2)}) collective-permute-start(bf16[48,4096]{1,0:T(8,128)(2,1)S(1)} %cot_behind_part.1), channel_id=1, source_target_pairs={{0,1},{1,0},{2,3},{3,2},{4,5},{5,4},{6,7},{7,6},{8,9},{9,8},{10,11... | collective-permute-start | bytes 1179656 | tf_op jit(solution)/shard_map/cot_behind/ppermute | solution.py:50
  42.6 5.3 %collective-permute-start.15 = (bf16[48,4096]{1,0:T(8,128)(2,1)S(1)}, bf16[48,4096]{1,0:T(8,128)(2,1)S(1)}, u32[]{:S(2)}, u32[]{:S(2)}) collective-permute-start(bf16[48,4096]{1,0:T(8,128)(2,1)S(1)} %behind_0.1), channel_id=1, source_target_pairs={{0,1},{1,0},{2,3},{3,2},{4,5},{5,4},{6,7},{7,6},{8,9},{9,8},{10,11... | collective-permute-start | bytes 1179656 | tf_op jit(solution)/shard_map/behind_0/ppermute | solution.py:50
  43.5 5.9 %collective-permute-start.18 = (bf16[48,4096]{1,0:T(8,128)(2,1)S(1)}, bf16[48,4096]{1,0:T(8,128)(2,1)S(1)}, u32[]{:S(2)}, u32[]{:S(2)}) collective-permute-start(bf16[48,4096]{1,0:T(8,128)(2,1)S(1)} %cot_far_part.1), channel_id=1, source_target_pairs={{0,1},{1,0},{2,3},{3,2},{4,5},{5,4},{6,7},{7,6},{8,9},{9,8},{10,11... | collective-permute-start | bytes 1179656 | tf_op jit(solution)/shard_map/cot_far_core/ppermute | solution.py:50
  43.7 5.8 %collective-permute-start.13 = (bf16[48,4096]{1,0:T(8,128)(2,1)S(1)}, bf16[48,4096]{1,0:T(8,128)(2,1)S(1)}, u32[]{:S(2)}, u32[]{:S(2)}) collective-permute-start(bf16[48,4096]{1,0:T(8,128)(2,1)S(1)} %cot_behind_z_0.1), channel_id=1, source_target_pairs={{0,1},{1,0},{2,3},{3,2},{4,5},{5,4},{6,7},{7,6},{8,9},{9,8},{10,11... | collective-permute-start | bytes 1179656 | tf_op jit(solution)/shard_map/cot_behind_z_0/ppermute | solution.py:50
  45.0 4.4 %collective-permute-start.14 = (bf16[16,4096]{1,0:T(8,128)(2,1)S(1)}, bf16[16,4096]{1,0:T(8,128)(2,1)S(1)}, u32[]{:S(2)}, u32[]{:S(2)}) collective-permute-start(bf16[16,4096]{1,0:T(8,128)(2,1)S(1)} %cot_behind_z_48.1), channel_id=1, source_target_pairs={{0,1},{1,0},{2,3},{3,2},{4,5},{5,4},{6,7},{7,6},{8,9},{9,8},{10,11... | collective-permute-start | bytes 393224 | tf_op jit(solution)/shard_map/cot_behind_z_48/ppermute | solution.py:50
  47.0 11.6 %collective-permute-start.22 = (bf16[32,4096]{1,0:T(8,128)(2,1)S(1)}, bf16[32,4096]{1,0:T(8,128)(2,1)S(1)}, u32[]{:S(2)}, u32[]{:S(2)}) collective-permute-start(bf16[32,4096]{1,0:T(8,128)(2,1)S(1)} %cot_far_copy.1), channel_id=1, source_target_pairs={{0,2},{1,3},{2,0},{3,1},{4,6},{5,7},{6,4},{7,5},{8,10},{9,11},{10,... | collective-permute-start | bytes 786440 | tf_op jit(solution)/shard_map/cot_far_z/ppermute | solution.py:50
  47.9 8.5 %collective-permute-start.21 = (bf16[64,4096]{1,0:T(8,128)(2,1)S(1)}, bf16[64,4096]{1,0:T(8,128)(2,1)S(1)}, u32[]{:S(2)}, u32[]{:S(2)}) collective-permute-start(bf16[64,4096]{1,0:T(8,128)(2,1)S(1)} %part.1), channel_id=1, source_target_pairs={{0,4},{1,13},{2,6},{3,15},{4,8},{5,1},{6,10},{7,3},{8,12},{9,5},{1... | collective-permute-start | bytes 1572872 | tf_op jit(solution)/shard_map/far/ppermute | solution.py:50
  49.4 9.4 %collective-permute-start.20 = (bf16[64,4096]{1,0:T(8,128)(2,1)S(1)}, bf16[64,4096]{1,0:T(8,128)(2,1)S(1)}, u32[]{:S(2)}, u32[]{:S(2)}) collective-permute-start(bf16[64,4096]{1,0:T(8,128)(2,1)S(1)} %collective-permute-done.12.refs_11_.refs_1_), channel_id=1, source_target_pairs={{0,1},{1,0},{2,3},{3,2},{4,5},{5,4},{6,7},{7,6},{8,9},{9,8},{10,11... | collective-permute-start | bytes 1572872 | tf_op jit(solution)/shard_map/behind_z/ppermute | solution.py:50
  56.4 7.7 %collective-permute-start.25 = (bf16[64,4096]{1,0:T(8,128)(2,1)S(1)}, bf16[64,4096]{1,0:T(8,128)(2,1)S(1)}, u32[]{:S(2)}, u32[]{:S(2)}) collective-permute-start(bf16[64,4096]{1,0:T(8,128)(2,1)S(1)} %far_copy.1.refs_5_), channel_id=1, source_target_pairs={{0,1},{1,0},{2,3},{3,2},{4,5},{5,4},{6,7},{7,6},{8,9},{9,8},{10,11... | collective-permute-start | bytes 1572872 | tf_op jit(solution)/shard_map/far_core/ppermute | solution.py:50
  58.7 5.4 %collective-permute-start.24 = (bf16[32,4096]{1,0:T(8,128)(2,1)S(1)}, bf16[32,4096]{1,0:T(8,128)(2,1)S(1)}, u32[]{:S(2)}, u32[]{:S(2)}) collective-permute-start(bf16[32,4096]{1,0:T(8,128)(2,1)S(1)} %cot_far_z_copy.1.refs_6_), channel_id=1, source_target_pairs={{0,1},{1,0},{2,3},{3,2},{4,5},{5,4},{6,7},{7,6},{8,9},{9,8},{10,11... | collective-permute-start | bytes 786440 | tf_op jit(solution)/shard_map/cot_far_z_core/ppermute | solution.py:50
  63.3 7.6 %collective-permute-start.23 = (bf16[64,4096]{1,0:T(8,128)(2,1)S(1)}, bf16[64,4096]{1,0:T(8,128)(2,1)S(1)}, u32[]{:S(2)}, u32[]{:S(2)}) collective-permute-start(bf16[64,4096]{1,0:T(8,128)(2,1)S(1)} %get-tuple-element.36.refs_15_), channel_id=1, source_target_pairs={{0,1},{1,0},{2,3},{3,2},{4,5},{5,4},{6,7},{7,6},{8,9},{9,8},{10,11... | collective-permute-start | bytes 1572872 | tf_op jit(solution)/shard_map/home_got/ppermute | solution.py:50
  76.9 7.4 %collective-permute-start.30 = (bf16[64,2688]{1,0:T(8,128)(2,1)S(1)}, bf16[64,2688]{1,0:T(8,128)(2,1)S(1)}, u32[]{:S(2)}, u32[]{:S(2)}) collective-permute-start(bf16[64,2688]{1,0:T(8,128)(2,1)S(1)} %to_far.1.refs_2_), channel_id=1, source_target_pairs={{0,12},{1,5},{2,14},{3,7},{4,0},{5,9},{6,2},{7,11},{8,4},{9,13},{1... | collective-permute-start | bytes 1032200 | tf_op jit(solution)/shard_map/from_far/ppermute | solution.py:50
  77.1 10.9 %collective-permute-start.29 = (bf16[64,2688]{1,0:T(8,128)(2,1)S(1)}, bf16[64,2688]{1,0:T(8,128)(2,1)S(1)}, u32[]{:S(2)}, u32[]{:S(2)}) collective-permute-start(bf16[64,2688]{1,0:T(8,128)(2,1)S(1)} %to_home_x.1.refs_5_), channel_id=1, source_target_pairs={{0,12},{1,5},{2,14},{3,7},{4,0},{5,9},{6,2},{7,11},{8,4},{9,13},{1... | collective-permute-start | bytes 1032200 | tf_op jit(solution)/shard_map/home_x/ppermute | solution.py:50
  78.3 10.5 %collective-permute-start.28 = (bf16[128,1408]{1,0:T(8,128)(2,1)S(1)}, bf16[128,1408]{1,0:T(8,128)(2,1)S(1)}, u32[]{:S(2)}, u32[]{:S(2)}) collective-permute-start(bf16[128,1408]{1,0:T(8,128)(2,1)S(1)} %away.1.refs_2_), channel_id=1, source_target_pairs={{0,2},{1,3},{2,0},{3,1},{4,6},{5,7},{6,4},{7,5},{8,10},{9,11},{10,... | collective-permute-start | bytes 1081352 | tf_op jit(solution)/shard_map/from_z/ppermute | solution.py:50
  84.4 7.6 %collective-permute-start.33 = (bf16[64,2688]{1,0:T(8,128)(2,1)S(1)}, bf16[64,2688]{1,0:T(8,128)(2,1)S(1)}, u32[]{:S(2)}, u32[]{:S(2)}) collective-permute-start(bf16[64,2688]{1,0:T(8,128)(2,1)S(1)} %to_home.1.refs_1_), channel_id=1, source_target_pairs={{0,12},{1,5},{2,14},{3,7},{4,0},{5,9},{6,2},{7,11},{8,4},{9,13},{1... | collective-permute-start | bytes 1032200 | tf_op jit(solution)/shard_map/home/ppermute | solution.py:50
  88.0 3.5 %collective-permute-start.35 = (bf16[32,2688]{1,0:T(8,128)(2,1)S(1)}, bf16[32,2688]{1,0:T(8,128)(2,1)S(1)}, u32[]{:S(2)}, u32[]{:S(2)}) collective-permute-start(bf16[32,2688]{1,0:T(8,128)(2,1)S(1)} %home_x_core_z_part.1), channel_id=1, source_target_pairs={{0,1},{1,0},{2,3},{3,2},{4,5},{5,4},{6,7},{7,6},{8,9},{9,8},{10,11... | collective-permute-start | bytes 516104 | tf_op jit(solution)/shard_map/home_x_core_z/ppermute | solution.py:50
  88.2 3.3 %collective-permute-start.34 = (bf16[32,2688]{1,0:T(8,128)(2,1)S(1)}, bf16[32,2688]{1,0:T(8,128)(2,1)S(1)}, u32[]{:S(2)}, u32[]{:S(2)}) collective-permute-start(bf16[32,2688]{1,0:T(8,128)(2,1)S(1)} %home_x_core_part.1), channel_id=1, source_target_pairs={{0,1},{1,0},{2,3},{3,2},{4,5},{5,4},{6,7},{7,6},{8,9},{9,8},{10,11... | collective-permute-start | bytes 516104 | tf_op jit(solution)/shard_map/home_x_core/ppermute | solution.py:50
  88.9 7.7 %collective-permute-start.32 = (bf16[64,1408]{1,0:T(8,128)(2,1)S(1)}, bf16[64,1408]{1,0:T(8,128)(2,1)S(1)}, u32[]{:S(2)}, u32[]{:S(2)}) collective-permute-start(bf16[64,1408]{1,0:T(8,128)(2,1)S(1)} %get-tuple-element.46), channel_id=1, source_target_pairs={{0,12},{1,5},{2,14},{3,7},{4,0},{5,9},{6,2},{7,11},{8,4},{9,13},{1... | collective-permute-start | bytes 540680 | tf_op jit(solution)/shard_map/home_b/ppermute | solution.py:50
  89.0 6.4 %collective-permute-start.31 = (bf16[32,1408]{1,0:T(8,128)(2,1)S(1)}, bf16[32,1408]{1,0:T(8,128)(2,1)S(1)}, u32[]{:S(2)}, u32[]{:S(2)}) collective-permute-start(bf16[32,1408]{1,0:T(8,128)(2,1)S(1)} %get-tuple-element.45), channel_id=1, source_target_pairs={{0,8},{1,9},{2,10},{3,11},{4,12},{5,13},{6,14},{7,15},{8,0},{9,1},... | collective-permute-start | bytes 270344 | tf_op jit(solution)/shard_map/home_far/ppermute | solution.py:50
  92.2 5.9 %collective-permute-start.37 = (bf16[32,2688]{1,0:T(8,128)(2,1)S(1)}, bf16[32,2688]{1,0:T(8,128)(2,1)S(1)}, u32[]{:S(2)}, u32[]{:S(2)}) collective-permute-start(bf16[32,2688]{1,0:T(8,128)(2,1)S(1)} %get-tuple-element.48), channel_id=1, source_target_pairs={{0,2},{1,3},{2,0},{3,1},{4,6},{5,7},{6,4},{7,5},{8,10},{9,11},{10,... | collective-permute-start | bytes 516104 | tf_op jit(solution)/shard_map/total_z/ppermute | solution.py:50
  (16 other events, 263.2 us)

commit v4 on v3

--- a/solution.py
+++ b/solution.py
@@ -13,11 +13,11 @@
 MIB = 1024 * 1024
 LONG = 10**11
 Y_FIRST = 2688
-EXTRA = 512
-SHORT = 10**9
 PARTS = (0, 48), (48, 16)
-HIDDEN_LIMIT = 10
-BACK_LIMIT = 10
+EXTRA = 128
+SHORT = 4 * 10**9
+HIDDEN_LIMIT = 8
+BACK_LIMIT = 8
 
 
 def like(*shape, dtype=bf16):
@@ -188,7 +188,21 @@
 
 
 def back(name, start, n, outs, grads, w_gate, w_up, after=(), flops=1):
-    def body(g, u, w_gate, w_up, *results):
+    rows, units = sum(g.shape[0] for g, _ in grads), w_gate.shape[1]
+
+    def body(*refs):
+        pairs, (w_gate, w_up), results, all_rows = (
+            refs[: 2 * len(grads)],
+            refs[2 * len(grads) : 2 * len(grads) + 2],
+            refs[2 * len(grads) + 2 : -2],
+            refs[-2:],
+        )
+        at = 0
+        for k in range(len(grads)):
+            for ref, whole in zip(pairs[2 * k : 2 * k + 2], all_rows):
+                whole[at : at + ref.shape[0]] = ref[...]
+            at += pairs[2 * k].shape[0]
+        g, u = all_rows
         cols = slice(start, start + n)
         transposed = (((1,), (1,)), ((), ()))
         dn = lax.dot_general(g[...], w_gate[cols, :], transposed, preferred_element_type=f32) + lax.dot_general(
@@ -201,7 +215,18 @@
                 at += count
 
     shapes = tuple(like(sum(count for _, count in spans), n) for spans in outs)
-    return local_kernel(name, body, shapes, *grads, w_gate, w_up, after=after, flops=flops, limit=BACK_LIMIT)
+    return local_kernel(
+        name,
+        body,
+        shapes,
+        *[x for pair in grads for x in pair],
+        w_gate,
+        w_up,
+        after=after,
+        scratch=[pltpu.VMEM((rows, units), bf16)] * 2,
+        flops=flops,
+        limit=BACK_LIMIT,
+    )
 
 
 def add(name, width, outs, *pieces, after=()):
@@ -285,6 +310,7 @@
     weights = w_gate, w_up, w_down
     cot = join("cot", cot, after=(own_stash,))
     cot_z = over_tensor("cot_z", cot, other_z)
+    cot_far = over_tensor("cot_far", cot, across_y)
     cot_core = over_tensor("cot_core", cot, other_core)
     cot_chip = join("cot_chip", cot, cot_core)
     cot_ahead = over_tensor("cot_ahead", cot_chip, along_y)
@@ -301,89 +327,107 @@
     )
     normed_z = over_tensor("normed_z", normed, other_z)
     normed_core = over_tensor("normed_core", normed, other_core)
-    chip = join("chip", normed, normed_core, after=(cot_z,))
+    chip = join("chip", normed, normed_core, after=(cot_z, cot_far))
     ahead = over_tensor("ahead", chip, along_y)
-    cot_part = join("cot_part", (cot_ahead, 0, 32), after=(normed, chip), columns=d + EXTRA)
-    cot_far = over_tensor("cot_far", cot_part, along_y)
-    cot_ahead_z = over_tensor("cot_ahead_z", cot_ahead, other_z)
+    cot_ahead_copy = join("cot_ahead_copy", cot_ahead, after=(normed, chip))
+    cot_ahead_z = over_tensor("cot_ahead_z", cot_ahead_copy, other_z)
+    cot_behind = over_tensor("cot_behind", cot_ahead, other_core)
     cot_z_core = over_tensor("cot_z_core", cot_z, other_core)
 
-    normed_z_copies = [
-        join(f"normed_z_copy_{at}", (normed_z, at, 16), after=(cot_part,), flops=SHORT) for at in (0, 16)
+    normed_z_copy = join("normed_z_copy", normed_z, after=(cot_ahead_copy,), flops=SHORT)
+    normed_z_core = over_tensor("normed_z_core", normed_z_copy, other_core)
+    chip_z = join("chip_z", normed_z, normed_z_core)
+    ahead_z = over_tensor("ahead_z", chip_z, along_y)
+    cot_far_core = over_tensor("cot_far_core", cot_far, other_core)
+    behind = [over_tensor(f"behind_{at}", join(f"behind_{at}", (ahead, at, 32)), other_core) for at in (0, 32)]
+
+    g1, u1 = hidden(
+        "hidden_near",
+        (cot, cot_z, cot_core, cot_z_core, cot_ahead, cot_behind),
+        ((0, 0, 32), (1, 0, 32), (2, 0, 32), (3, 0, 32), (4, 0, 64), (5, 0, 64)),
+        (normed, normed_z, normed_core, chip_z, ahead, *behind),
+        ((0, 0, 32), (1, 0, 32), (2, 0, 32), (3, 32, 32), (4, 0, 64), (5, 0, 32), (6, 0, 32)),
+        weights,
+        after=(cot_far_core,),
+    )
+    cot_behind_z = [
+        over_tensor(f"cot_behind_z_{at}", join(f"cot_behind_z_{at}", (cot_ahead_z, at, n), after=(g1,)), other_core)
+        for at, n in PARTS
     ]
-    normed_z_core = [over_tensor("normed_z_core", part, other_core) for part in normed_z_copies]
-    chip_z = join("chip_z", normed_z, *normed_z_core)
-    ahead_z = over_tensor("ahead_z", chip_z, along_y)
-    behind = [over_tensor(f"behind_{at}", join(f"behind_{at}", (ahead, at, n)), other_core) for at, n in PARTS]
-    cot_behind_z = [
-        over_tensor(f"cot_behind_z_{at}", join(f"cot_behind_z_{at}", (cot_ahead_z, at, n)), other_core) for at, n in PARTS
-    ]
-    cot_far_core = over_tensor("cot_far_core", join("cot_far_part", cot_far, (cot_ahead, 0, 16), columns=d), other_core)
-    cot_behind = over_tensor("cot_behind", join("cot_behind_part", (cot_ahead, 16, 48)), other_core)
-    cot_far_z = over_tensor("cot_far_z", join("cot_far_copy", cot_far, columns=d), other_z)
-    part = join("part", (ahead, 0, 32), (ahead_z, 0, 32))
+    cot_far_z = over_tensor("cot_far_z", cot_far, other_z)
+    part = join("part", (ahead, 0, 32), (ahead_z, 0, 32), after=(g1,))
     far = over_tensor("far", part, along_y)
     behind_z = over_tensor("behind_z", ahead_z, other_core)
-
-    home_blocks = tuple((k, 0, 32) for k in range(4))
-    near_blocks = home_blocks + tuple((4 + k, 32 * h, 32) for h in range(2) for k in range(2))
-    g1, u1 = hidden(
-        "hidden_near",
-        (cot, cot_z, cot_core, cot_z_core, cot_ahead, cot_ahead_z),
-        near_blocks,
-        (normed, normed_z, normed_core, chip_z, ahead, ahead_z),
-        tuple((k, 32 if k == 3 else start, n) for k, start, n in near_blocks),
-        weights,
-        after=(*cot_behind_z, *behind, cot_far_core, cot_behind),
-        flops=LONG,
-    )
-    far_copy = join("far_copy", far, after=(g1,))
-    far_core = over_tensor("far_core", far_copy, other_core)
-    cot_far_z_copy = join("cot_far_z_copy", cot_far_z, after=(g1,))
-    cot_far_z_core = over_tensor("cot_far_z_core", cot_far_z_copy, other_core)
-    home_keep, home_send, ahead_keep = back(
+    home_keep, side_keep, near_send = back(
         "back_near",
         0,
         d,
-        (((0, 64),), ((64, 64),), ((128, 128),)),
-        (g1, u1),
+        (((0, 64),), ((128, 64),), ((64, 64), (192, 64))),
+        ((g1, u1),),
         w_gate,
         w_up,
-        after=(behind_z, far_copy, cot_far_z_copy),
-    )
-    home_got = over_tensor("home_got", home_send, other_core)
+        after=(part, *cot_behind_z),
+        flops=LONG,
+    )
+    near_got = over_tensor("near_got", near_send, other_core)
     g2, u2 = hidden(
-        "hidden_rest",
-        (cot_far_core, cot_behind, *cot_behind_z, cot_far, cot_far_z, cot_far_z_core),
-        ((0, 32, 16), (1, 0, 16), (2, 0, 32), (1, 16, 32), (2, 32, 16), (3, 0, 16),
-         (4, 0, 32), (5, 0, 32), (0, 0, 32), (6, 0, 32)),
-        (*behind, behind_z, far, far_core),
-        ((0, 0, 32), (2, 0, 32), (0, 32, 16), (1, 0, 16), (2, 32, 32), (3, 0, 64), (4, 0, 64)),
+        "hidden_side_z",
+        (cot_ahead_z, *cot_behind_z),
+        ((0, 0, 64), (1, 0, 48), (2, 0, 16)),
+        (ahead_z, behind_z),
+        ((0, 0, 64), (1, 0, 64)),
         weights,
-        after=(home_send,),
+        after=(near_send,),
+    )
+    far_copy = join("far_copy", far, cot_far_z, after=(g2,))
+    far_core = over_tensor("far_core", far_copy, other_core)
+    split = Y_FIRST
+    g3, u3 = hidden(
+        "hidden_far",
+        (cot_far, far_copy, cot_far_core, far_core),
+        ((0, 0, 32), (1, 64, 32), (2, 0, 32), (3, 64, 32)),
+        (far_copy, far_core),
+        ((0, 0, 64), (1, 0, 64)),
+        weights,
         flops=LONG,
     )
-    split = Y_FIRST
-    rest = ((0, 128), (192, 64)), ((128, 64),)
-    send_a, far_a = back("back_a", 0, split, rest, (g2, u2), w_gate, w_up, after=(home_got,), flops=LONG)
+    grads = (g2, u2), (g3, u3)
+    rest = ((0, 64),), ((128, 64),), ((64, 64), (192, 64))
+    side_a, far_a, send_a = back("back_a", 0, split, rest, grads, w_gate, w_up, after=(near_got,), flops=LONG)
     got_a = over_tensor("got_a", send_a, other_core)
-    send_b, far_b = back("back_b", split, d - split, rest, (g2, u2), w_gate, w_up, after=(far_a,), flops=LONG)
+    side_b, far_b, send_b = back("back_b", split, d - split, rest, grads, w_gate, w_up, after=(far_a,), flops=LONG)
     got_b = over_tensor("got_b", send_b, other_core)
 
-    to_far = add("to_far", split, [[(64, ((0, 0), (1, 128)))]], far_a, got_a, after=(far_b,))
+    to_far = add("to_far", split, [[(64, ((0, 0), (1, 64)))]], far_a, got_a, after=(far_b,))
     from_far = over_tensor("from_far", to_far, back_y)
-    to_home_x = add("to_home_x", split, [[(64, ((0, 64), (1, 64)))]], ahead_keep, got_a, after=(to_far,))
+    to_home_x = add(
+        "to_home_x", split, [[(32, ((0, 32), (1, 96))), (32, ((2, 32), (3, 32)))]], side_keep, near_got, side_a, got_a, after=(to_far,)
+    )
     home_x = over_tensor("home_x", to_home_x, back_y)
-    pieces_b = (home_keep, split), (home_got, split), (ahead_keep, split), got_b, far_b
-
-    def terms_b(z):
-        at = 32 * z
-        return ((0, at), (1, at)), ((2, at), (3, at)), ((2, 64 + at), (3, 64 + at)), ((4, at), (3, 128 + at))
-
-    away = add("away", d - split, [[(32, t) for t in terms_b(1)]], *pieces_b, after=(to_home_x,))
+    away = add(
+        "away",
+        d - split,
+        [[(32, ((0, 32), (1, 32))), (64, ((2, 0), (3, 0))), (32, ((4, 32), (3, 96)))]],
+        (home_keep, split),
+        (near_got, split),
+        side_b,
+        got_b,
+        far_b,
+        after=(to_home_x,),
+    )
     from_z = over_tensor("from_z", away, other_z)
-    near = add("near", split, [[(64, ((0, 0), (1, 0)))]], home_keep, home_got, after=(away,))
-    to_home = add("to_home", split, [[(64, ((0, 0), (1, 0), (2, 0)))]], ahead_keep, got_a, from_far, after=(near,))
+    near = add("near", split, [[(64, ((0, 0), (1, 0)))]], home_keep, near_got, after=(away,))
+    to_home = add(
+        "to_home",
+        split,
+        [[(32, ((0, 0), (1, 64), (4, 0))), (32, ((2, 0), (3, 0), (4, 32)))]],
+        side_keep,
+        near_got,
+        side_a,
+        got_a,
+        from_far,
+        after=(near,),
+    )
     home = over_tensor("home", to_home, back_y)
     home_x_core = tuple(
         over_tensor(name, join(name + "_part", (home_x, at, 32), after=(to_home,)), other_core)
@@ -393,9 +437,17 @@
     held, held_side, held_far = add(
         "held",
         d - split,
-        [[(32, terms_b(0)[k] + ((5, 32 * k),)) for k in ks] for ks in ((0,), (1, 2), (3,))],
-        *pieces_b,
+        [
+            [(32, ((0, 0), (1, 0), (2, 0)))],
+            [(64, ((3, 0), (1, 64), (2, 32)))],
+            [(32, ((4, 0), (5, 64), (2, 96)))],
+        ],
+        (home_keep, split),
+        (near_got, split),
         from_z,
+        (side_keep, split),
+        far_b,
+        got_b,
         after=(home_own,),
     )
     home_b = over_tensor("home_b", held_side, back_y)

time: 99.3 us -> 96.9 us (0.976)
  starting transfers between devices: 43.4 us -> 38.3 us
  Pallas kernels: 27 us -> 29.3 us
    ppermute x36 -> x34, starting transfers between devices: 35.4 us -> 30.3 us  [over_tensor(): lax.ppermute(shard, 'tensor', [(i, move(i)) for i in range(lax.axis_size(...]
    pallas_call x36 -> x32, Pallas kernels: 27 us -> 29.3 us  [local_kernel(): pl.pallas_call(run, out_shape=outs, in_specs=[anywhere if hbm else VMEM]...]
    ppermute x1, waiting for transfers between devices: 2.42 us -> 1.34 us  [on_device(): fetched = lax.ppermute(payload, 'section', stash_pairs)]
    ppermute x36 -> x34, waiting for transfers between devices: 22.2 us -> 22.7 us  [over_tensor(): lax.ppermute(shard, 'tensor', [(i, move(i)) for i in range(lax.axis_size(...]
  transfers between devices with their start and end apart: 38 -> 36, of which waited for: 16 -> 13; matrix products, arithmetic and copies ran while one was open for 0% -> 0% of each run, Pallas kernels for 22% -> 25%
where the time goes in v4:
time: 96.9 us; the launch traced here: 95.8 us
  starting transfers between devices  38.3 us (40%)
  Pallas kernels  29.3 us (30%)
  waiting for transfers between devices  27.7 us (29%)
    ppermute x34, starting transfers between devices, over_tensor(): lax.ppermute(shard, 'tensor', [(i, move(i)) for i in range(lax.axis_size(...  30.3 us
    pallas_call x32, Pallas kernels, local_kernel(): pl.pallas_call(run, out_shape=outs, in_specs=[anywhere if hbm else VMEM]...  29.3 us
    ppermute x34, waiting for transfers between devices, over_tensor(): lax.ppermute(shard, 'tensor', [(i, move(i)) for i in range(lax.axis_size(...  22.7 us
    ppermute x1, starting transfers between devices, on_device(): cot = lax.ppermute(cot_source, 'section', shift_pairs)  6.69 us
    ppermute x1, waiting for transfers between devices, on_device(): cot = lax.ppermute(cot_source, 'section', shift_pairs)  3.69 us
  transfers between devices with their start and end apart: 36, of which 13 were waited for; matrix products, arithmetic and copies ran while one was open for 0% of the time, Pallas kernels for 25%

profile of v4, /device:TPU:1, one launch (start us, length us, event | category | flops | bytes accessed | tf_op | source)
XLA Modules:
  0.0 95.8 jit_solution(10175964327056732598)
XLA Ops:
  0.0 1.4 %prepare.1 = (bf16[32,4224]{1,0:T(8,128)(2,1)S(1)}, bf16[32,4352]{1,0:T(8,128)(2,1)S(1)}, f32[1,4096]{1,0:T(1,128)S(1)}, bf16[32,4096]{1,0:T(8,128)(2,1)S(1)}) custom-call(s32[8]{0:T(128)} %refs_0_.1, s32[8]{0:T(128)} %refs_1_.1, bf16[2,32,4096]{2,1,0:T(8,128)(2,1)} %bitcast.28, bf16[2,32]{1,0:T(2,128)(2,1)} %bitcast.31, bf16[2,32,4096]{2,1,0:T(8,128)(2,1)} %bitcast.29, ...), custom_call_target="tpu_custom_call" | custom-call | flops 1 | bytes 1 | tf_op jit(solution)/shard_map/prepare/pallas_call | solution.py:36
  1.4 6.7 %collective-permute-start = (bf16[32,4096]{1,0:T(8,128)(2,1)S(1)}, bf16[32,4096]{1,0:T(8,128)(2,1)S(1)}, u32[]{:S(2)}, u32[]{:S(2)}) collective-permute-start(bf16[32,4096]{1,0:T(8,128)(2,1)S(1)} %get-tuple-element.32), channel_id=1, source_target_pairs={{16,0},{32,16},{48,32},{64,48},{80,64},{96,80},{112,96},{0,112},{1... | collective-permute-start | bytes 786440 | tf_op jit(solution)/shard_map/shift/ppermute | solution.py:308
  8.1 1.3 %collective-permute-start.6 = (bf16[32,4224]{1,0:T(8,128)(2,1)S(1)}, bf16[32,4224]{1,0:T(8,128)(2,1)S(1)}, u32[]{:S(2)}, u32[]{:S(2)}) collective-permute-start(bf16[32,4224]{1,0:T(8,128)(2,1)S(1)} %get-tuple-element.34), channel_id=1, source_target_pairs={{112,0},{96,16},{80,32},{64,48},{113,1},{97,17},{81,33},{65,49},{1... | collective-permute-start | bytes 811016 | tf_op jit(solution)/shard_map/fetched/ppermute | solution.py:306
  9.4 3.7 %collective-permute-done.refs_0_ = bf16[32,4096]{1,0:T(8,128)(2,1)S(1)} collective-permute-done((bf16[32,4096]{1,0:T(8,128)(2,1)S(1)}, bf16[32,4096]{1,0:T(8,128)(2,1)S(1)}, u32[]{:S(2)}, u32[]{:S(2)}) %collective-permute-start) | collective-permute-done | bytes 262176 | tf_op jit(solution)/shard_map/shift/ppermute | solution.py:308
  13.1 1.6 %collective-permute-start.2 = (bf16[32,4096]{1,0:T(8,128)(2,1)S(1)}, bf16[32,4096]{1,0:T(8,128)(2,1)S(1)}, u32[]{:S(2)}, u32[]{:S(2)}) collective-permute-start(bf16[32,4096]{1,0:T(8,128)(2,1)S(1)} %cot.1.refs_0_.refs_6_), channel_id=1, source_target_pairs={{0,1},{1,0},{2,3},{3,2},{4,5},{5,4},{6,7},{7,6},{8,9},{9,8},{10,11... | collective-permute-start | bytes 786440 | tf_op jit(solution)/shard_map/cot_core/ppermute | solution.py:50
  14.7 2.9 %collective-permute-start.9 = (bf16[32,4096]{1,0:T(8,128)(2,1)S(1)}, bf16[32,4096]{1,0:T(8,128)(2,1)S(1)}, u32[]{:S(2)}, u32[]{:S(2)}) collective-permute-start(bf16[32,4096]{1,0:T(8,128)(2,1)S(1)} %cot.1.refs_0_.refs_6_), channel_id=1, source_target_pairs={{0,8},{1,9},{2,10},{3,11},{4,12},{5,13},{6,14},{7,15},{8,0},{9,1},... | collective-permute-start | bytes 786440 | tf_op jit(solution)/shard_map/cot_far/ppermute | solution.py:50
  18.4 0.8 collective-permute-start.4
  19.3 1.3 %collective-permute-done.6.refs_1_ = bf16[32,4224]{1,0:T(8,128)(2,1)S(1)} collective-permute-done((bf16[32,4224]{1,0:T(8,128)(2,1)S(1)}, bf16[32,4224]{1,0:T(8,128)(2,1)S(1)}, u32[]{:S(2)}, u32[]{:S(2)}) %collective-permute-start.6) | collective-permute-done | bytes 270368 | tf_op jit(solution)/shard_map/fetched/ppermute | solution.py:306
  20.9 2.0 %collective-permute-start.8 = (bf16[32,4096]{1,0:T(8,128)(2,1)S(1)}, bf16[32,4096]{1,0:T(8,128)(2,1)S(1)}, u32[]{:S(2)}, u32[]{:S(2)}) collective-permute-start(bf16[32,4096]{1,0:T(8,128)(2,1)S(1)} %get-tuple-element.36.refs_0_.refs_1_.refs_6_), channel_id=1, source_target_pairs={{0,1},{1,0},{2,3},{3,2},{4,5},{5,4},{6,7},{7,6},{8,9},{9,8},{10,11... | collective-permute-start | bytes 786440 | tf_op jit(solution)/shard_map/normed_core/ppermute | solution.py:50
  22.9 0.8 collective-permute-start.7
  24.1 1.1 %collective-permute-done.1.refs_2_.refs_1_ = bf16[32,4096]{1,0:T(8,128)(2,1)S(1)} collective-permute-done((bf16[32,4096]{1,0:T(8,128)(2,1)S(1)}, bf16[32,4096]{1,0:T(8,128)(2,1)S(1)}, u32[]{:S(2)}, u32[]{:S(2)}) %collective-permute-start.1) | collective-permute-done | bytes 262176 | tf_op jit(solution)/shard_map/cot_z/ppermute | solution.py:50
  25.2 1.8 %collective-permute-start.11 = (bf16[64,4096]{1,0:T(8,128)(2,1)S(1)}, bf16[64,4096]{1,0:T(8,128)(2,1)S(1)}, u32[]{:S(2)}, u32[]{:S(2)}) collective-permute-start(bf16[64,4096]{1,0:T(8,128)(2,1)S(1)} %chip.1.refs_2_), channel_id=1, source_target_pairs={{0,4},{1,13},{2,6},{3,15},{4,8},{5,1},{6,10},{7,3},{8,12},{9,5},{1... | collective-permute-start | bytes 1572872 | tf_op jit(solution)/shard_map/ahead/ppermute | solution.py:50
  27.2 3.4 %collective-permute-done.4.refs_0_.refs_4_ = bf16[64,4096]{1,0:T(8,128)(2,1)S(1)} collective-permute-done((bf16[64,4096]{1,0:T(8,128)(2,1)S(1)}, bf16[64,4096]{1,0:T(8,128)(2,1)S(1)}, u32[]{:S(2)}, u32[]{:S(2)}) %collective-permute-start.4) | collective-permute-done | bytes 524320 | tf_op jit(solution)/shard_map/cot_ahead/ppermute | solution.py:50
  32.8 3.3 %collective-permute-done.11.refs_0_.refs_10_ = bf16[64,4096]{1,0:T(8,128)(2,1)S(1)} collective-permute-done((bf16[64,4096]{1,0:T(8,128)(2,1)S(1)}, bf16[64,4096]{1,0:T(8,128)(2,1)S(1)}, u32[]{:S(2)}, u32[]{:S(2)}) %collective-permute-start.11) | collective-permute-done | bytes 524320 | tf_op jit(solution)/shard_map/ahead/ppermute | solution.py:50
  36.2 1.0 %collective-permute-start.3 = (bf16[32,4096]{1,0:T(8,128)(2,1)S(1)}, bf16[32,4096]{1,0:T(8,128)(2,1)S(1)}, u32[]{:S(2)}, u32[]{:S(2)}) collective-permute-start(bf16[32,4096]{1,0:T(8,128)(2,1)S(1)} %collective-permute-done.1.refs_2_.refs_1_), channel_id=1, source_target_pairs={{0,1},{1,0},{2,3},{3,2},{4,5},{5,4},{6,7},{7,6},{8,9},{9,8},{10,11... | collective-permute-start | bytes 786440 | tf_op jit(solution)/shard_map/cot_z_core/ppermute | solution.py:50
  38.3 1.5 %collective-permute-start.15 = (bf16[64,4096]{1,0:T(8,128)(2,1)S(1)}, bf16[64,4096]{1,0:T(8,128)(2,1)S(1)}, u32[]{:S(2)}, u32[]{:S(2)}) collective-permute-start(bf16[64,4096]{1,0:T(8,128)(2,1)S(1)} %chip_z.1.refs_9_), channel_id=1, source_target_pairs={{0,4},{1,13},{2,6},{3,15},{4,8},{5,1},{6,10},{7,3},{8,12},{9,5},{1... | collective-permute-start | bytes 1572872 | tf_op jit(solution)/shard_map/ahead_z/ppermute | solution.py:50
  39.9 6.8 %hidden_near.1 = (bf16[256,896]{1,0:T(8,128)(2,1)S(1)}, bf16[256,896]{1,0:T(8,128)(2,1)S(1)}) custom-call(bf16[32,4096]{1,0:T(8,128)(2,1)S(1)} %cot.1.refs_0_.refs_6_, bf16[32,4096]{1,0:T(8,128)(2,1)S(1)} %collective-permute-done.1.refs_2_.refs_1_, bf16[32,4096]{1,0:T(8,128)(2,1)S(1)} %collective-permute-done.2.refs_1_.refs_2_, ...), custom_call_target="tpu_custom_call" | custom-call | flops 1 | bytes 1 | tf_op jit(solution)/shard_map/hidden_near/pallas_call | solution.py:36
  48.4 1.8 %collective-permute-start.21 = (bf16[64,4096]{1,0:T(8,128)(2,1)S(1)}, bf16[64,4096]{1,0:T(8,128)(2,1)S(1)}, u32[]{:S(2)}, u32[]{:S(2)}) collective-permute-start(bf16[64,4096]{1,0:T(8,128)(2,1)S(1)} %part.1.refs_4_), channel_id=1, source_target_pairs={{0,4},{1,13},{2,6},{3,15},{4,8},{5,1},{6,10},{7,3},{8,12},{9,5},{1... | collective-permute-start | bytes 1572872 | tf_op jit(solution)/shard_map/far/ppermute | solution.py:50
  50.2 4.5 %back_near.1 = (bf16[64,4096]{1,0:T(8,128)(2,1)S(1)}, bf16[64,4096]{1,0:T(8,128)(2,1)S(1)}, bf16[128,4096]{1,0:T(8,128)(2,1)S(1)}) custom-call(bf16[256,896]{1,0:T(8,128)(2,1)S(1)} %get-tuple-element.37.refs_2_.refs_1_.refs_0_, bf16[256,896]{1,0:T(8,128)(2,1)S(1)} %get-tuple-element.38.refs_1_, bf16[4096,896]{1,0:T(8,128)(2,1)S(1)} %bitcast.17, ...), custom_call_target="tpu_custom_call" | custom-call | flops 99999997952 | bytes 1 | tf_op jit(solution)/shard_map/back_near/pallas_call | solution.py:36
  54.8 4.6 %hidden_side_z.1 = (bf16[128,896]{1,0:T(8,128)(2,1)S(1)}, bf16[128,896]{1,0:T(8,128)(2,1)S(1)}) custom-call(bf16[64,4096]{1,0:T(8,128)(2,1)S(1)} %collective-permute-done.16.refs_0_, bf16[48,4096]{1,0:T(8,128)(2,1)S(1)} %collective-permute-done.17.refs_5_.refs_1_, bf16[16,4096]{1,0:T(8,128)(2,1)S(1)} %collective-permute-done.18.refs_6_.refs_2_, ...), custom_call_target="tpu_custom_call" | custom-call | flops 1 | bytes 1 | tf_op jit(solution)/shard_map/hidden_side_z/pallas_call | solution.py:36
  60.4 1.6 %collective-permute-done.23.refs_3_.refs_5_ = bf16[96,4096]{1,0:T(8,128)(2,1)S(1)} collective-permute-done((bf16[96,4096]{1,0:T(8,128)(2,1)S(1)}, bf16[96,4096]{1,0:T(8,128)(2,1)S(1)}, u32[]{:S(2)}, u32[]{:S(2)}) %collective-permute-start.23) | collective-permute-done | bytes 786464 | tf_op jit(solution)/shard_map/far_core/ppermute | solution.py:50
  62.0 4.6 %hidden_far.1 = (bf16[128,896]{1,0:T(8,128)(2,1)S(1)}, bf16[128,896]{1,0:T(8,128)(2,1)S(1)}) custom-call(bf16[32,4096]{1,0:T(8,128)(2,1)S(1)} %collective-permute-done.9.refs_3_.refs_0_, bf16[96,4096]{1,0:T(8,128)(2,1)S(1)} %far_copy.1.refs_1_.refs_4_, bf16[32,4096]{1,0:T(8,128)(2,1)S(1)} %collective-permute-done.14.refs_16_.refs_2_, ...), custom_call_target="tpu_custom_call" | custom-call | flops 99999997952 | bytes 1 | tf_op jit(solution)/shard_map/hidden_far/pallas_call | solution.py:36
  66.6 3.2 %back_a.1 = (bf16[64,2688]{1,0:T(8,128)(2,1)S(1)}, bf16[64,2688]{1,0:T(8,128)(2,1)S(1)}, bf16[128,2688]{1,0:T(8,128)(2,1)S(1)}) custom-call(bf16[128,896]{1,0:T(8,128)(2,1)S(1)} %get-tuple-element.41.refs_2_.refs_0_, bf16[128,896]{1,0:T(8,128)(2,1)S(1)} %get-tuple-element.42.refs_1_, bf16[128,896]{1,0:T(8,128)(2,1)S(1)} %get-tuple-element.43.refs_2_, ...), custom_call_target="tpu_custom_call" | custom-call | flops 99999997952 | bytes 1 | tf_op jit(solution)/shard_map/back_a/pallas_call | solution.py:36
  70.2 1.8 %back_b.1 = (bf16[64,1408]{1,0:T(8,128)(2,1)S(1)}, bf16[64,1408]{1,0:T(8,128)(2,1)S(1)}, bf16[128,1408]{1,0:T(8,128)(2,1)S(1)}) custom-call(bf16[128,896]{1,0:T(8,128)(2,1)S(1)} %get-tuple-element.41.refs_2_.refs_0_, bf16[128,896]{1,0:T(8,128)(2,1)S(1)} %get-tuple-element.42.refs_1_, bf16[128,896]{1,0:T(8,128)(2,1)S(1)} %get-tuple-element.43.refs_2_, ...), custom_call_target="tpu_custom_call" | custom-call | flops 99999997952 | bytes 1 | tf_op jit(solution)/shard_map/back_b/pallas_call | solution.py:36
  73.2 1.1 %collective-permute-start.27 = (bf16[64,2688]{1,0:T(8,128)(2,1)S(1)}, bf16[64,2688]{1,0:T(8,128)(2,1)S(1)}, u32[]{:S(2)}, u32[]{:S(2)}) collective-permute-start(bf16[64,2688]{1,0:T(8,128)(2,1)S(1)} %to_home_x.1.refs_5_), channel_id=1, source_target_pairs={{0,12},{1,5},{2,14},{3,7},{4,0},{5,9},{6,2},{7,11},{8,4},{9,13},{1... | collective-permute-start | bytes 1032200 | tf_op jit(solution)/shard_map/home_x/ppermute | solution.py:50
  75.3 4.4 %collective-permute-done.28.refs_4_ = bf16[64,2688]{1,0:T(8,128)(2,1)S(1)} collective-permute-done((bf16[64,2688]{1,0:T(8,128)(2,1)S(1)}, bf16[64,2688]{1,0:T(8,128)(2,1)S(1)}, u32[]{:S(2)}, u32[]{:S(2)}) %collective-permute-start.28) | collective-permute-done | bytes 344096 | tf_op jit(solution)/shard_map/from_far/ppermute | solution.py:50
  79.9 3.5 %collective-permute-done.27.refs_0_ = bf16[64,2688]{1,0:T(8,128)(2,1)S(1)} collective-permute-done((bf16[64,2688]{1,0:T(8,128)(2,1)S(1)}, bf16[64,2688]{1,0:T(8,128)(2,1)S(1)}, u32[]{:S(2)}, u32[]{:S(2)}) %collective-permute-start.27) | collective-permute-done | bytes 344096 | tf_op jit(solution)/shard_map/home_x/ppermute | solution.py:50
  84.7 3.5 %collective-permute-start.29 = (bf16[32,1408]{1,0:T(8,128)(2,1)S(1)}, bf16[32,1408]{1,0:T(8,128)(2,1)S(1)}, u32[]{:S(2)}, u32[]{:S(2)}) collective-permute-start(bf16[32,1408]{1,0:T(8,128)(2,1)S(1)} %get-tuple-element.53), channel_id=1, source_target_pairs={{0,8},{1,9},{2,10},{3,11},{4,12},{5,13},{6,14},{7,15},{8,0},{9,1},... | collective-permute-start | bytes 270344 | tf_op jit(solution)/shard_map/home_far/ppermute | solution.py:50
  89.1 2.9 %collective-permute-done.29.refs_2_.refs_1_ = bf16[32,1408]{1,0:T(8,128)(2,1)S(1)} collective-permute-done((bf16[32,1408]{1,0:T(8,128)(2,1)S(1)}, bf16[32,1408]{1,0:T(8,128)(2,1)S(1)}, u32[]{:S(2)}, u32[]{:S(2)}) %collective-permute-start.29) | collective-permute-done | bytes 90144 | tf_op jit(solution)/shard_map/home_far/ppermute | solution.py:50
  92.0 1.9 %collective-permute-start.34 = (bf16[32,1408]{1,0:T(8,128)(2,1)S(1)}, bf16[32,1408]{1,0:T(8,128)(2,1)S(1)}, u32[]{:S(2)}, u32[]{:S(2)}) collective-permute-start(bf16[32,1408]{1,0:T(8,128)(2,1)S(1)} %home_b_part.1), channel_id=1, source_target_pairs={{0,1},{1,0},{2,3},{3,2},{4,5},{5,4},{6,7},{7,6},{8,9},{9,8},{10,11... | collective-permute-start | bytes 270344 | tf_op jit(solution)/shard_map/home_b_core/ppermute | solution.py:50
  93.9 0.9 collective-permute-done.34.refs_3_
  94.8 1.0 %final.1 = bf16[32,4096]{1,0:T(8,128)(2,1)} custom-call(bf16[32,1408]{1,0:T(8,128)(2,1)S(1)} %get-tuple-element.52.refs_4_.refs_0_, bf16[32,1408]{1,0:T(8,128)(2,1)S(1)} %collective-permute-done.29.refs_2_.refs_1_, bf16[64,1408]{1,0:T(8,128)(2,1)S(1)} %collective-permute-done.30.refs_0_.refs_2_, bf16[32,1408]{1,0:T(8,128)(2,1)S(1)} %collective-permute-done.34.refs_3_, ...), custom_call_target="tpu_custom_call" | custom-call | flops 1 | bytes 1 | tf_op jit(solution)/shard_map/final/pallas_call | solution.py:36
  (92 shorter events, 12.6 us)
Async XLA Ops:
  1.4 11.7 %collective-permute-start = (bf16[32,4096]{1,0:T(8,128)(2,1)S(1)}, bf16[32,4096]{1,0:T(8,128)(2,1)S(1)}, u32[]{:S(2)}, u32[]{:S(2)}) collective-permute-start(bf16[32,4096]{1,0:T(8,128)(2,1)S(1)} %get-tuple-element.32), channel_id=1, source_target_pairs={{16,0},{32,16},{48,32},{64,48},{80,64},{96,80},{112,96},{0,112},{1... | collective-permute-start | bytes 786440 | tf_op jit(solution)/shard_map/shift/ppermute | solution.py:308
  8.1 12.5 %collective-permute-start.6 = (bf16[32,4224]{1,0:T(8,128)(2,1)S(1)}, bf16[32,4224]{1,0:T(8,128)(2,1)S(1)}, u32[]{:S(2)}, u32[]{:S(2)}) collective-permute-start(bf16[32,4224]{1,0:T(8,128)(2,1)S(1)} %get-tuple-element.34), channel_id=1, source_target_pairs={{112,0},{96,16},{80,32},{64,48},{113,1},{97,17},{81,33},{65,49},{1... | collective-permute-start | bytes 811016 | tf_op jit(solution)/shard_map/fetched/ppermute | solution.py:306
  13.1 5.3 %collective-permute-start.2 = (bf16[32,4096]{1,0:T(8,128)(2,1)S(1)}, bf16[32,4096]{1,0:T(8,128)(2,1)S(1)}, u32[]{:S(2)}, u32[]{:S(2)}) collective-permute-start(bf16[32,4096]{1,0:T(8,128)(2,1)S(1)} %cot.1.refs_0_.refs_6_), channel_id=1, source_target_pairs={{0,1},{1,0},{2,3},{3,2},{4,5},{5,4},{6,7},{7,6},{8,9},{9,8},{10,11... | collective-permute-start | bytes 786440 | tf_op jit(solution)/shard_map/cot_core/ppermute | solution.py:50
  14.7 9.4 %collective-permute-start.9 = (bf16[32,4096]{1,0:T(8,128)(2,1)S(1)}, bf16[32,4096]{1,0:T(8,128)(2,1)S(1)}, u32[]{:S(2)}, u32[]{:S(2)}) collective-permute-start(bf16[32,4096]{1,0:T(8,128)(2,1)S(1)} %cot.1.refs_0_.refs_6_), channel_id=1, source_target_pairs={{0,8},{1,9},{2,10},{3,11},{4,12},{5,13},{6,14},{7,15},{8,0},{9,1},... | collective-permute-start | bytes 786440 | tf_op jit(solution)/shard_map/cot_far/ppermute | solution.py:50
  17.7 7.5 %collective-permute-start.1 = (bf16[32,4096]{1,0:T(8,128)(2,1)S(1)}, bf16[32,4096]{1,0:T(8,128)(2,1)S(1)}, u32[]{:S(2)}, u32[]{:S(2)}) collective-permute-start(bf16[32,4096]{1,0:T(8,128)(2,1)S(1)} %cot.1.refs_0_.refs_6_), channel_id=1, source_target_pairs={{0,2},{1,3},{2,0},{3,1},{4,6},{5,7},{6,4},{7,5},{8,10},{9,11},{10,... | collective-permute-start | bytes 786440 | tf_op jit(solution)/shard_map/cot_z/ppermute | solution.py:50
  18.4 12.1 %collective-permute-start.4 = (bf16[64,4096]{1,0:T(8,128)(2,1)S(1)}, bf16[64,4096]{1,0:T(8,128)(2,1)S(1)}, u32[]{:S(2)}, u32[]{:S(2)}) collective-permute-start(bf16[64,4096]{1,0:T(8,128)(2,1)S(1)} %cot_chip.1.refs_3_), channel_id=1, source_target_pairs={{0,4},{1,13},{2,6},{3,15},{4,8},{5,1},{6,10},{7,3},{8,12},{9,5},{1... | collective-permute-start | bytes 1572872 | tf_op jit(solution)/shard_map/cot_ahead/ppermute | solution.py:50
  20.9 4.3 %collective-permute-start.8 = (bf16[32,4096]{1,0:T(8,128)(2,1)S(1)}, bf16[32,4096]{1,0:T(8,128)(2,1)S(1)}, u32[]{:S(2)}, u32[]{:S(2)}) collective-permute-start(bf16[32,4096]{1,0:T(8,128)(2,1)S(1)} %get-tuple-element.36.refs_0_.refs_1_.refs_6_), channel_id=1, source_target_pairs={{0,1},{1,0},{2,3},{3,2},{4,5},{5,4},{6,7},{7,6},{8,9},{9,8},{10,11... | collective-permute-start | bytes 786440 | tf_op jit(solution)/shard_map/normed_core/ppermute | solution.py:50
  22.9 8.4 %collective-permute-start.7 = (bf16[32,4096]{1,0:T(8,128)(2,1)S(1)}, bf16[32,4096]{1,0:T(8,128)(2,1)S(1)}, u32[]{:S(2)}, u32[]{:S(2)}) collective-permute-start(bf16[32,4096]{1,0:T(8,128)(2,1)S(1)} %get-tuple-element.36.refs_0_.refs_1_.refs_6_), channel_id=1, source_target_pairs={{0,2},{1,3},{2,0},{3,1},{4,6},{5,7},{6,4},{7,5},{8,10},{9,11},{10,... | collective-permute-start | bytes 786440 | tf_op jit(solution)/shard_map/normed_z/ppermute | solution.py:50
  25.2 11.0 %collective-permute-start.11 = (bf16[64,4096]{1,0:T(8,128)(2,1)S(1)}, bf16[64,4096]{1,0:T(8,128)(2,1)S(1)}, u32[]{:S(2)}, u32[]{:S(2)}) collective-permute-start(bf16[64,4096]{1,0:T(8,128)(2,1)S(1)} %chip.1.refs_2_), channel_id=1, source_target_pairs={{0,4},{1,13},{2,6},{3,15},{4,8},{5,1},{6,10},{7,3},{8,12},{9,5},{1... | collective-permute-start | bytes 1572872 | tf_op jit(solution)/shard_map/ahead/ppermute | solution.py:50
  27.0 10.2 %collective-permute-start.14 = (bf16[32,4096]{1,0:T(8,128)(2,1)S(1)}, bf16[32,4096]{1,0:T(8,128)(2,1)S(1)}, u32[]{:S(2)}, u32[]{:S(2)}) collective-permute-start(bf16[32,4096]{1,0:T(8,128)(2,1)S(1)} %collective-permute-done.9.refs_3_.refs_0_), channel_id=1, source_target_pairs={{0,1},{1,0},{2,3},{3,2},{4,5},{5,4},{6,7},{7,6},{8,9},{9,8},{10,11... | collective-permute-start | bytes 786440 | tf_op jit(solution)/shard_map/cot_far_core/ppermute | solution.py:50
  30.6 9.1 %collective-permute-start.5 = (bf16[64,4096]{1,0:T(8,128)(2,1)S(1)}, bf16[64,4096]{1,0:T(8,128)(2,1)S(1)}, u32[]{:S(2)}, u32[]{:S(2)}) collective-permute-start(bf16[64,4096]{1,0:T(8,128)(2,1)S(1)} %collective-permute-done.4.refs_0_.refs_4_), channel_id=1, source_target_pairs={{0,1},{1,0},{2,3},{3,2},{4,5},{5,4},{6,7},{7,6},{8,9},{9,8},{10,11... | collective-permute-start | bytes 1572872 | tf_op jit(solution)/shard_map/cot_behind/ppermute | solution.py:50
  31.3 6.0 %collective-permute-start.10 = (bf16[32,4096]{1,0:T(8,128)(2,1)S(1)}, bf16[32,4096]{1,0:T(8,128)(2,1)S(1)}, u32[]{:S(2)}, u32[]{:S(2)}) collective-permute-start(bf16[32,4096]{1,0:T(8,128)(2,1)S(1)} %normed_z_copy.1), channel_id=1, source_target_pairs={{0,1},{1,0},{2,3},{3,2},{4,5},{5,4},{6,7},{7,6},{8,9},{9,8},{10,11... | collective-permute-start | bytes 786440 | tf_op jit(solution)/shard_map/normed_z_core/ppermute | solution.py:50
  32.1 14.6 %collective-permute-start.16 = (bf16[64,4096]{1,0:T(8,128)(2,1)S(1)}, bf16[64,4096]{1,0:T(8,128)(2,1)S(1)}, u32[]{:S(2)}, u32[]{:S(2)}) collective-permute-start(bf16[64,4096]{1,0:T(8,128)(2,1)S(1)} %cot_ahead_copy.1.refs_1_), channel_id=1, source_target_pairs={{0,2},{1,3},{2,0},{3,1},{4,6},{5,7},{6,4},{7,5},{8,10},{9,11},{10,... | collective-permute-start | bytes 1572872 | tf_op jit(solution)/shard_map/cot_ahead_z/ppermute | solution.py:50
  37.2 2.6 %collective-permute-start.12 = (bf16[32,4096]{1,0:T(8,128)(2,1)S(1)}, bf16[32,4096]{1,0:T(8,128)(2,1)S(1)}, u32[]{:S(2)}, u32[]{:S(2)}) collective-permute-start(bf16[32,4096]{1,0:T(8,128)(2,1)S(1)} %behind_0.1), channel_id=1, source_target_pairs={{0,1},{1,0},{2,3},{3,2},{4,5},{5,4},{6,7},{7,6},{8,9},{9,8},{10,11... | collective-permute-start | bytes 786440 | tf_op jit(solution)/shard_map/behind_0/ppermute | solution.py:50
  38.3 10.0 %collective-permute-start.15 = (bf16[64,4096]{1,0:T(8,128)(2,1)S(1)}, bf16[64,4096]{1,0:T(8,128)(2,1)S(1)}, u32[]{:S(2)}, u32[]{:S(2)}) collective-permute-start(bf16[64,4096]{1,0:T(8,128)(2,1)S(1)} %chip_z.1.refs_9_), channel_id=1, source_target_pairs={{0,4},{1,13},{2,6},{3,15},{4,8},{5,1},{6,10},{7,3},{8,12},{9,5},{1... | collective-permute-start | bytes 1572872 | tf_op jit(solution)/shard_map/ahead_z/ppermute | solution.py:50
  46.7 3.5 %collective-permute-start.17 = (bf16[48,4096]{1,0:T(8,128)(2,1)S(1)}, bf16[48,4096]{1,0:T(8,128)(2,1)S(1)}, u32[]{:S(2)}, u32[]{:S(2)}) collective-permute-start(bf16[48,4096]{1,0:T(8,128)(2,1)S(1)} %cot_behind_z_0.1), channel_id=1, source_target_pairs={{0,1},{1,0},{2,3},{3,2},{4,5},{5,4},{6,7},{7,6},{8,9},{9,8},{10,11... | collective-permute-start | bytes 1179656 | tf_op jit(solution)/shard_map/cot_behind_z_0/ppermute | solution.py:50
  47.0 3.2 %collective-permute-start.18 = (bf16[16,4096]{1,0:T(8,128)(2,1)S(1)}, bf16[16,4096]{1,0:T(8,128)(2,1)S(1)}, u32[]{:S(2)}, u32[]{:S(2)}) collective-permute-start(bf16[16,4096]{1,0:T(8,128)(2,1)S(1)} %cot_behind_z_48.1), channel_id=1, source_target_pairs={{0,1},{1,0},{2,3},{3,2},{4,5},{5,4},{6,7},{7,6},{8,9},{9,8},{10,11... | collective-permute-start | bytes 393224 | tf_op jit(solution)/shard_map/cot_behind_z_48/ppermute | solution.py:50
  47.6 11.8 %collective-permute-start.22 = (bf16[32,4096]{1,0:T(8,128)(2,1)S(1)}, bf16[32,4096]{1,0:T(8,128)(2,1)S(1)}, u32[]{:S(2)}, u32[]{:S(2)}) collective-permute-start(bf16[32,4096]{1,0:T(8,128)(2,1)S(1)} %collective-permute-done.9.refs_3_.refs_0_), channel_id=1, source_target_pairs={{0,2},{1,3},{2,0},{3,1},{4,6},{5,7},{6,4},{7,5},{8,10},{9,11},{10,... | collective-permute-start | bytes 786440 | tf_op jit(solution)/shard_map/cot_far_z/ppermute | solution.py:50
  48.4 11.0 %collective-permute-start.21 = (bf16[64,4096]{1,0:T(8,128)(2,1)S(1)}, bf16[64,4096]{1,0:T(8,128)(2,1)S(1)}, u32[]{:S(2)}, u32[]{:S(2)}) collective-permute-start(bf16[64,4096]{1,0:T(8,128)(2,1)S(1)} %part.1.refs_4_), channel_id=1, source_target_pairs={{0,4},{1,13},{2,6},{3,15},{4,8},{5,1},{6,10},{7,3},{8,12},{9,5},{1... | collective-permute-start | bytes 1572872 | tf_op jit(solution)/shard_map/far/ppermute | solution.py:50
  50.2 4.6 %collective-permute-start.20 = (bf16[64,4096]{1,0:T(8,128)(2,1)S(1)}, bf16[64,4096]{1,0:T(8,128)(2,1)S(1)}, u32[]{:S(2)}, u32[]{:S(2)}) collective-permute-start(bf16[64,4096]{1,0:T(8,128)(2,1)S(1)} %collective-permute-done.15.refs_1_.refs_3_), channel_id=1, source_target_pairs={{0,1},{1,0},{2,3},{3,2},{4,5},{5,4},{6,7},{7,6},{8,9},{9,8},{10,11... | collective-permute-start | bytes 1572872 | tf_op jit(solution)/shard_map/behind_z/ppermute | solution.py:50
  60.0 6.5 %collective-permute-start.19 = (bf16[128,4096]{1,0:T(8,128)(2,1)S(1)}, bf16[128,4096]{1,0:T(8,128)(2,1)S(1)}, u32[]{:S(2)}, u32[]{:S(2)}) collective-permute-start(bf16[128,4096]{1,0:T(8,128)(2,1)S(1)} %get-tuple-element.40.refs_8_), channel_id=1, source_target_pairs={{0,1},{1,0},{2,3},{3,2},{4,5},{5,4},{6,7},{7,6},{8,9},{9,8},{10,11... | collective-permute-start | bytes 3145736 | tf_op jit(solution)/shard_map/near_got/ppermute | solution.py:50
  69.8 2.5 %collective-permute-start.25 = (bf16[128,2688]{1,0:T(8,128)(2,1)S(1)}, bf16[128,2688]{1,0:T(8,128)(2,1)S(1)}, u32[]{:S(2)}, u32[]{:S(2)}) collective-permute-start(bf16[128,2688]{1,0:T(8,128)(2,1)S(1)} %get-tuple-element.51), channel_id=1, source_target_pairs={{0,1},{1,0},{2,3},{3,2},{4,5},{5,4},{6,7},{7,6},{8,9},{9,8},{10,11... | collective-permute-start | bytes 2064392 | tf_op jit(solution)/shard_map/got_a/ppermute | solution.py:50
  72.4 7.4 %collective-permute-start.28 = (bf16[64,2688]{1,0:T(8,128)(2,1)S(1)}, bf16[64,2688]{1,0:T(8,128)(2,1)S(1)}, u32[]{:S(2)}, u32[]{:S(2)}) collective-permute-start(bf16[64,2688]{1,0:T(8,128)(2,1)S(1)} %to_far.1.refs_4_), channel_id=1, source_target_pairs={{0,12},{1,5},{2,14},{3,7},{4,0},{5,9},{6,2},{7,11},{8,4},{9,13},{1... | collective-permute-start | bytes 1032200 | tf_op jit(solution)/shard_map/from_far/ppermute | solution.py:50
  73.2 10.2 %collective-permute-start.27 = (bf16[64,2688]{1,0:T(8,128)(2,1)S(1)}, bf16[64,2688]{1,0:T(8,128)(2,1)S(1)}, u32[]{:S(2)}, u32[]{:S(2)}) collective-permute-start(bf16[64,2688]{1,0:T(8,128)(2,1)S(1)} %to_home_x.1.refs_5_), channel_id=1, source_target_pairs={{0,12},{1,5},{2,14},{3,7},{4,0},{5,9},{6,2},{7,11},{8,4},{9,13},{1... | collective-permute-start | bytes 1032200 | tf_op jit(solution)/shard_map/home_x/ppermute | solution.py:50
  74.4 9.8 %collective-permute-start.26 = (bf16[128,1408]{1,0:T(8,128)(2,1)S(1)}, bf16[128,1408]{1,0:T(8,128)(2,1)S(1)}, u32[]{:S(2)}, u32[]{:S(2)}) collective-permute-start(bf16[128,1408]{1,0:T(8,128)(2,1)S(1)} %away.1.refs_2_), channel_id=1, source_target_pairs={{0,2},{1,3},{2,0},{3,1},{4,6},{5,7},{6,4},{7,5},{8,10},{9,11},{10,... | collective-permute-start | bytes 1081352 | tf_op jit(solution)/shard_map/from_z/ppermute | solution.py:50
  79.9 8.3 %collective-permute-start.31 = (bf16[64,2688]{1,0:T(8,128)(2,1)S(1)}, bf16[64,2688]{1,0:T(8,128)(2,1)S(1)}, u32[]{:S(2)}, u32[]{:S(2)}) collective-permute-start(bf16[64,2688]{1,0:T(8,128)(2,1)S(1)} %to_home.1.refs_1_), channel_id=1, source_target_pairs={{0,12},{1,5},{2,14},{3,7},{4,0},{5,9},{6,2},{7,11},{8,4},{9,13},{1... | collective-permute-start | bytes 1032200 | tf_op jit(solution)/shard_map/home/ppermute | solution.py:50
  83.4 4.7 %collective-permute-start.33 = (bf16[32,2688]{1,0:T(8,128)(2,1)S(1)}, bf16[32,2688]{1,0:T(8,128)(2,1)S(1)}, u32[]{:S(2)}, u32[]{:S(2)}) collective-permute-start(bf16[32,2688]{1,0:T(8,128)(2,1)S(1)} %home_x_core_z_part.1), channel_id=1, source_target_pairs={{0,1},{1,0},{2,3},{3,2},{4,5},{5,4},{6,7},{7,6},{8,9},{9,8},{10,11... | collective-permute-start | bytes 516104 | tf_op jit(solution)/shard_map/home_x_core_z/ppermute | solution.py:50
  83.9 4.3 %collective-permute-start.32 = (bf16[32,2688]{1,0:T(8,128)(2,1)S(1)}, bf16[32,2688]{1,0:T(8,128)(2,1)S(1)}, u32[]{:S(2)}, u32[]{:S(2)}) collective-permute-start(bf16[32,2688]{1,0:T(8,128)(2,1)S(1)} %home_x_core_part.1), channel_id=1, source_target_pairs={{0,1},{1,0},{2,3},{3,2},{4,5},{5,4},{6,7},{7,6},{8,9},{9,8},{10,11... | collective-permute-start | bytes 516104 | tf_op jit(solution)/shard_map/home_x_core/ppermute | solution.py:50
  84.3 7.7 %collective-permute-start.30 = (bf16[64,1408]{1,0:T(8,128)(2,1)S(1)}, bf16[64,1408]{1,0:T(8,128)(2,1)S(1)}, u32[]{:S(2)}, u32[]{:S(2)}) collective-permute-start(bf16[64,1408]{1,0:T(8,128)(2,1)S(1)} %get-tuple-element.54), channel_id=1, source_target_pairs={{0,12},{1,5},{2,14},{3,7},{4,0},{5,9},{6,2},{7,11},{8,4},{9,13},{1... | collective-permute-start | bytes 540680 | tf_op jit(solution)/shard_map/home_b/ppermute | solution.py:50
  84.7 7.3 %collective-permute-start.29 = (bf16[32,1408]{1,0:T(8,128)(2,1)S(1)}, bf16[32,1408]{1,0:T(8,128)(2,1)S(1)}, u32[]{:S(2)}, u32[]{:S(2)}) collective-permute-start(bf16[32,1408]{1,0:T(8,128)(2,1)S(1)} %get-tuple-element.53), channel_id=1, source_target_pairs={{0,8},{1,9},{2,10},{3,11},{4,12},{5,13},{6,14},{7,15},{8,0},{9,1},... | collective-permute-start | bytes 270344 | tf_op jit(solution)/shard_map/home_far/ppermute | solution.py:50
  88.3 6.5 %collective-permute-start.35 = (bf16[32,2688]{1,0:T(8,128)(2,1)S(1)}, bf16[32,2688]{1,0:T(8,128)(2,1)S(1)}, u32[]{:S(2)}, u32[]{:S(2)}) collective-permute-start(bf16[32,2688]{1,0:T(8,128)(2,1)S(1)} %get-tuple-element.56), channel_id=1, source_target_pairs={{0,2},{1,3},{2,0},{3,1},{4,6},{5,7},{6,4},{7,5},{8,10},{9,11},{10,... | collective-permute-start | bytes 516104 | tf_op jit(solution)/shard_map/total_z/ppermute | solution.py:50
  92.0 2.8 %collective-permute-start.34 = (bf16[32,1408]{1,0:T(8,128)(2,1)S(1)}, bf16[32,1408]{1,0:T(8,128)(2,1)S(1)}, u32[]{:S(2)}, u32[]{:S(2)}) collective-permute-start(bf16[32,1408]{1,0:T(8,128)(2,1)S(1)} %home_b_part.1), channel_id=1, source_target_pairs={{0,1},{1,0},{2,3},{3,2},{4,5},{5,4},{6,7},{7,6},{8,9},{9,8},{10,11... | collective-permute-start | bytes 270344 | tf_op jit(solution)/shard_map/home_b_core/ppermute | solution.py:50
  (13 other events, 157.9 us)

commit v5 on v4

--- a/solution.py
+++ b/solution.py
@@ -88,8 +88,8 @@
     return local_kernel(name, body, like(rows, columns), *[p for p, _, _ in pieces], after=after, flops=flops)
 
 
-def prepare_kernel(keep_hbm, roster_hbm, parked, parked_scale, local, local_scale, gain, pending,
-                   payload, own, gain_copy, cot, codes, scales, keep, roster, sems):
+def prepare_kernel(keep_hbm, roster_hbm, parked, parked_scale, local, local_scale, gain,
+                   payload, own, gain_copy, codes, scales, keep, roster, sems):
     mine = lax.axis_index("section")
     mirror = lax.axis_size("section") - 1 - mine
     d = gain.shape[1]
@@ -102,7 +102,6 @@
                 (local, codes.at[1]),
                 (local_scale, scales.at[1]),
                 (gain, gain_copy),
-                (pending, cot),
                 (keep_hbm, keep),
                 (roster_hbm, roster),
             )
@@ -124,7 +123,7 @@
         pl.when(slot <= 0)(lambda: choose(0))
         pl.when(slot > 0)(lambda: choose(1))
 
-    for k in (6, 7, 0, 1):
+    for k in (5, 6, 0, 1):
         copies[k].wait()
     put(payload, 0, roster[mirror] - keep[mirror])
     copies[2].wait()
@@ -133,7 +132,6 @@
     is_parked = (roster[mine] >= keep[mine]).astype(f32)
     own[:, d + EXTRA :] = jnp.full((own.shape[0], 128), is_parked, f32).astype(bf16)
     copies[4].wait()
-    copies[5].wait()
 
 
 def norm_kernel(own, parked, gain, normed, unit, inv):
@@ -281,10 +279,10 @@
     stash_pairs = [(sections - 1 - i, i) for i in range(sections // 2)]
     shift_pairs = [((i + 1) % sections, i) for i in range(sections)]
 
-    payload, own_stash, gain, cot_source = local_kernel(
+    payload, own_stash, gain = local_kernel(
         "prepare",
         prepare_kernel,
-        (like(shard, d + EXTRA), like(shard, d + EXTRA + 128), like(1, d, dtype=f32), like(shard, d)),
+        (like(shard, d + EXTRA), like(shard, d + EXTRA + 128), like(1, d, dtype=f32)),
         keep_count,
         roster,
         parked_codes[0],
@@ -292,20 +290,19 @@
         local_codes[0],
         local_scales[0],
         norm_gain,
-        pending[0],
         hbm=True,
         scratch=[
             pltpu.VMEM((2, 2, shard, d), bf16),
             pltpu.VMEM((2, 2, shard), bf16),
             pltpu.SMEM(keep_count.shape, jnp.int32),
             pltpu.SMEM(roster.shape, jnp.int32),
-            pltpu.SemaphoreType.DMA((8,)),
+            pltpu.SemaphoreType.DMA((7,)),
         ],
     )
     with jax.named_scope("fetched"):
         fetched = lax.ppermute(payload, "section", stash_pairs)
     with jax.named_scope("shift"):
-        cot = lax.ppermute(cot_source, "section", shift_pairs)
+        cot = lax.ppermute(pending[0], "section", shift_pairs)
     w_gate, w_up, w_down = w_gate[0], w_up[0], w_down[0]
     weights = w_gate, w_up, w_down
     cot = join("cot", cot, after=(own_stash,))

time: 96.9 us -> 95.6 us (0.987)
  waiting for transfers between devices: 27.7 us -> 25.6 us
  starting transfers between devices: 38.3 us -> 40.2 us
    ppermute x34, waiting for transfers between devices: 22.7 us -> 20.5 us  [over_tensor(): lax.ppermute(shard, 'tensor', [(i, move(i)) for i in range(lax.axis_size(...]
    ppermute x34, starting transfers between devices: 30.3 us -> 32.2 us  [over_tensor(): lax.ppermute(shard, 'tensor', [(i, move(i)) for i in range(lax.axis_size(...]
    ppermute x1, waiting for transfers between devices: 3.69 us -> 2.61 us  [on_device(): cot = lax.ppermute(pending[0], 'section', shift_pairs)]
    ppermute x1, waiting for transfers between devices: 1.34 us -> 2.42 us  [on_device(): fetched = lax.ppermute(payload, 'section', stash_pairs)]
  transfers between devices with their start and end apart: 36 -> 36, of which waited for: 13 -> 12; matrix products, arithmetic and copies ran while one was open for 0% -> 0% of each run, Pallas kernels for 25% -> 26%
where the time goes in v5:
time: 95.6 us; the launch traced here: 95.5 us
  starting transfers between devices  40.2 us (42%)
  Pallas kernels  29.3 us (31%)
  waiting for transfers between devices  25.6 us (27%)
    ppermute x34, starting transfers between devices, over_tensor(): lax.ppermute(shard, 'tensor', [(i, move(i)) for i in range(lax.axis_size(...  32.2 us
    pallas_call x32, Pallas kernels, local_kernel(): pl.pallas_call(run, out_shape=outs, in_specs=[anywhere if hbm else VMEM]...  29.3 us
    ppermute x34, waiting for transfers between devices, over_tensor(): lax.ppermute(shard, 'tensor', [(i, move(i)) for i in range(lax.axis_size(...  20.5 us
    ppermute x1, starting transfers between devices, on_device(): cot = lax.ppermute(pending[0], 'section', shift_pairs)  6.62 us
    ppermute x1, waiting for transfers between devices, on_device(): cot = lax.ppermute(pending[0], 'section', shift_pairs)  2.61 us
    ppermute x1, waiting for transfers between devices, on_device(): fetched = lax.ppermute(payload, 'section', stash_pairs)  2.42 us
  transfers between devices with their start and end apart: 36, of which 12 were waited for; matrix products, arithmetic and copies ran while one was open for 0% of the time, Pallas kernels for 26%

profile of v5, /device:TPU:1, one launch (start us, length us, event | category | flops | bytes accessed | tf_op | source)
XLA Modules:
  0.0 95.5 jit_solution(2353386346935221402)
XLA Ops:
  0.0 6.6 %collective-permute-start = (bf16[32,4096]{1,0:T(8,128)(2,1)}, bf16[32,4096]{1,0:T(8,128)(2,1)S(1)}, u32[]{:S(2)}, u32[]{:S(2)}) collective-permute-start(bf16[32,4096]{1,0:T(8,128)(2,1)} %bitcast.32), channel_id=1, source_target_pairs={{16,0},{32,16},{48,32},{64,48},{80,64},{96,80},{112,96},{0,112},{1... | collective-permute-start | bytes 786440 | tf_op jit(solution)/shard_map/shift/ppermute | solution.py:305
  6.6 1.4 %prepare.1 = (bf16[32,4224]{1,0:T(8,128)(2,1)S(1)}, bf16[32,4352]{1,0:T(8,128)(2,1)S(1)}, f32[1,4096]{1,0:T(1,128)S(1)}) custom-call(s32[8]{0:T(128)} %refs_0_.1, s32[8]{0:T(128)} %refs_1_.1, bf16[2,32,4096]{2,1,0:T(8,128)(2,1)} %bitcast.28, bf16[2,32]{1,0:T(2,128)(2,1)} %bitcast.30, bf16[2,32,4096]{2,1,0:T(8,128)(2,1)} %bitcast.29, bf16[2,32]{1,0:T(2,128)(2,1)} %bitcast.31, ...), custom_call_target="tpu_custom_call" | custom-call | flops 1 | bytes 1 | tf_op jit(solution)/shard_map/prepare/pallas_call | solution.py:36
  8.0 1.3 %collective-permute-start.6 = (bf16[32,4224]{1,0:T(8,128)(2,1)S(1)}, bf16[32,4224]{1,0:T(8,128)(2,1)S(1)}, u32[]{:S(2)}, u32[]{:S(2)}) collective-permute-start(bf16[32,4224]{1,0:T(8,128)(2,1)S(1)} %get-tuple-element.32), channel_id=1, source_target_pairs={{112,0},{96,16},{80,32},{64,48},{113,1},{97,17},{81,33},{65,49},{1... | collective-permute-start | bytes 811016 | tf_op jit(solution)/shard_map/fetched/ppermute | solution.py:303
  9.3 2.6 %collective-permute-done.refs_0_ = bf16[32,4096]{1,0:T(8,128)(2,1)S(1)} collective-permute-done((bf16[32,4096]{1,0:T(8,128)(2,1)}, bf16[32,4096]{1,0:T(8,128)(2,1)S(1)}, u32[]{:S(2)}, u32[]{:S(2)}) %collective-permute-start) | collective-permute-done | bytes 262176 | tf_op jit(solution)/shard_map/shift/ppermute | solution.py:305
  11.9 1.6 %collective-permute-start.2 = (bf16[32,4096]{1,0:T(8,128)(2,1)S(1)}, bf16[32,4096]{1,0:T(8,128)(2,1)S(1)}, u32[]{:S(2)}, u32[]{:S(2)}) collective-permute-start(bf16[32,4096]{1,0:T(8,128)(2,1)S(1)} %cot.1.refs_0_.refs_6_), channel_id=1, source_target_pairs={{0,1},{1,0},{2,3},{3,2},{4,5},{5,4},{6,7},{7,6},{8,9},{9,8},{10,11... | collective-permute-start | bytes 786440 | tf_op jit(solution)/shard_map/cot_core/ppermute | solution.py:50
  13.6 2.9 %collective-permute-start.9 = (bf16[32,4096]{1,0:T(8,128)(2,1)S(1)}, bf16[32,4096]{1,0:T(8,128)(2,1)S(1)}, u32[]{:S(2)}, u32[]{:S(2)}) collective-permute-start(bf16[32,4096]{1,0:T(8,128)(2,1)S(1)} %cot.1.refs_0_.refs_6_), channel_id=1, source_target_pairs={{0,8},{1,9},{2,10},{3,11},{4,12},{5,13},{6,14},{7,15},{8,0},{9,1},... | collective-permute-start | bytes 786440 | tf_op jit(solution)/shard_map/cot_far/ppermute | solution.py:50
  17.3 0.8 collective-permute-start.4
  18.1 2.4 %collective-permute-done.6.refs_1_ = bf16[32,4224]{1,0:T(8,128)(2,1)S(1)} collective-permute-done((bf16[32,4224]{1,0:T(8,128)(2,1)S(1)}, bf16[32,4224]{1,0:T(8,128)(2,1)S(1)}, u32[]{:S(2)}, u32[]{:S(2)}) %collective-permute-start.6) | collective-permute-done | bytes 270368 | tf_op jit(solution)/shard_map/fetched/ppermute | solution.py:303
  20.8 2.0 %collective-permute-start.8 = (bf16[32,4096]{1,0:T(8,128)(2,1)S(1)}, bf16[32,4096]{1,0:T(8,128)(2,1)S(1)}, u32[]{:S(2)}, u32[]{:S(2)}) collective-permute-start(bf16[32,4096]{1,0:T(8,128)(2,1)S(1)} %get-tuple-element.34.refs_0_.refs_1_.refs_6_), channel_id=1, source_target_pairs={{0,1},{1,0},{2,3},{3,2},{4,5},{5,4},{6,7},{7,6},{8,9},{9,8},{10,11... | collective-permute-start | bytes 786440 | tf_op jit(solution)/shard_map/normed_core/ppermute | solution.py:50
  24.1 2.8 %collective-permute-start.11 = (bf16[64,4096]{1,0:T(8,128)(2,1)S(1)}, bf16[64,4096]{1,0:T(8,128)(2,1)S(1)}, u32[]{:S(2)}, u32[]{:S(2)}) collective-permute-start(bf16[64,4096]{1,0:T(8,128)(2,1)S(1)} %chip.1.refs_2_), channel_id=1, source_target_pairs={{0,4},{1,13},{2,6},{3,15},{4,8},{5,1},{6,10},{7,3},{8,12},{9,5},{1... | collective-permute-start | bytes 1572872 | tf_op jit(solution)/shard_map/ahead/ppermute | solution.py:50
  26.9 2.5 %collective-permute-done.4.refs_0_.refs_4_ = bf16[64,4096]{1,0:T(8,128)(2,1)S(1)} collective-permute-done((bf16[64,4096]{1,0:T(8,128)(2,1)S(1)}, bf16[64,4096]{1,0:T(8,128)(2,1)S(1)}, u32[]{:S(2)}, u32[]{:S(2)}) %collective-permute-start.4) | collective-permute-done | bytes 524320 | tf_op jit(solution)/shard_map/cot_ahead/ppermute | solution.py:50
  29.6 1.2 %collective-permute-done.7.refs_0_.refs_7_ = bf16[32,4096]{1,0:T(8,128)(2,1)S(1)} collective-permute-done((bf16[32,4096]{1,0:T(8,128)(2,1)S(1)}, bf16[32,4096]{1,0:T(8,128)(2,1)S(1)}, u32[]{:S(2)}, u32[]{:S(2)}) %collective-permute-start.7) | collective-permute-done | bytes 262176 | tf_op jit(solution)/shard_map/normed_z/ppermute | solution.py:50
  30.8 1.0 collective-permute-start.10
  32.5 2.6 %collective-permute-done.11.refs_0_.refs_10_ = bf16[64,4096]{1,0:T(8,128)(2,1)S(1)} collective-permute-done((bf16[64,4096]{1,0:T(8,128)(2,1)S(1)}, bf16[64,4096]{1,0:T(8,128)(2,1)S(1)}, u32[]{:S(2)}, u32[]{:S(2)}) %collective-permute-start.11) | collective-permute-done | bytes 524320 | tf_op jit(solution)/shard_map/ahead/ppermute | solution.py:50
  36.9 1.7 %collective-permute-start.15 = (bf16[64,4096]{1,0:T(8,128)(2,1)S(1)}, bf16[64,4096]{1,0:T(8,128)(2,1)S(1)}, u32[]{:S(2)}, u32[]{:S(2)}) collective-permute-start(bf16[64,4096]{1,0:T(8,128)(2,1)S(1)} %chip_z.1.refs_9_), channel_id=1, source_target_pairs={{0,4},{1,13},{2,6},{3,15},{4,8},{5,1},{6,10},{7,3},{8,12},{9,5},{1... | collective-permute-start | bytes 1572872 | tf_op jit(solution)/shard_map/ahead_z/ppermute | solution.py:50
  38.7 6.8 %hidden_near.1 = (bf16[256,896]{1,0:T(8,128)(2,1)S(1)}, bf16[256,896]{1,0:T(8,128)(2,1)S(1)}) custom-call(bf16[32,4096]{1,0:T(8,128)(2,1)S(1)} %cot.1.refs_0_.refs_6_, bf16[32,4096]{1,0:T(8,128)(2,1)S(1)} %collective-permute-done.1.refs_2_.refs_1_, bf16[32,4096]{1,0:T(8,128)(2,1)S(1)} %collective-permute-done.2.refs_1_.refs_2_, ...), custom_call_target="tpu_custom_call" | custom-call | flops 1 | bytes 1 | tf_op jit(solution)/shard_map/hidden_near/pallas_call | solution.py:36
  46.5 0.8 collective-permute-start.22
  47.3 2.8 %collective-permute-start.21 = (bf16[64,4096]{1,0:T(8,128)(2,1)S(1)}, bf16[64,4096]{1,0:T(8,128)(2,1)S(1)}, u32[]{:S(2)}, u32[]{:S(2)}) collective-permute-start(bf16[64,4096]{1,0:T(8,128)(2,1)S(1)} %part.1.refs_4_), channel_id=1, source_target_pairs={{0,4},{1,13},{2,6},{3,15},{4,8},{5,1},{6,10},{7,3},{8,12},{9,5},{1... | collective-permute-start | bytes 1572872 | tf_op jit(solution)/shard_map/far/ppermute | solution.py:50
  50.1 4.5 %back_near.1 = (bf16[64,4096]{1,0:T(8,128)(2,1)S(1)}, bf16[64,4096]{1,0:T(8,128)(2,1)S(1)}, bf16[128,4096]{1,0:T(8,128)(2,1)S(1)}) custom-call(bf16[256,896]{1,0:T(8,128)(2,1)S(1)} %get-tuple-element.35.refs_2_.refs_1_.refs_0_, bf16[256,896]{1,0:T(8,128)(2,1)S(1)} %get-tuple-element.36.refs_1_, bf16[4096,896]{1,0:T(8,128)(2,1)S(1)} %bitcast.17, ...), custom_call_target="tpu_custom_call" | custom-call | flops 99999997952 | bytes 1 | tf_op jit(solution)/shard_map/back_near/pallas_call | solution.py:36
  54.7 4.6 %hidden_side_z.1 = (bf16[128,896]{1,0:T(8,128)(2,1)S(1)}, bf16[128,896]{1,0:T(8,128)(2,1)S(1)}) custom-call(bf16[64,4096]{1,0:T(8,128)(2,1)S(1)} %collective-permute-done.16.refs_0_, bf16[48,4096]{1,0:T(8,128)(2,1)S(1)} %collective-permute-done.17.refs_5_.refs_1_, bf16[16,4096]{1,0:T(8,128)(2,1)S(1)} %collective-permute-done.18.refs_6_.refs_2_, ...), custom_call_target="tpu_custom_call" | custom-call | flops 1 | bytes 1 | tf_op jit(solution)/shard_map/hidden_side_z/pallas_call | solution.py:36
  60.3 1.6 %collective-permute-done.23.refs_3_.refs_5_ = bf16[96,4096]{1,0:T(8,128)(2,1)S(1)} collective-permute-done((bf16[96,4096]{1,0:T(8,128)(2,1)S(1)}, bf16[96,4096]{1,0:T(8,128)(2,1)S(1)}, u32[]{:S(2)}, u32[]{:S(2)}) %collective-permute-start.23) | collective-permute-done | bytes 786464 | tf_op jit(solution)/shard_map/far_core/ppermute | solution.py:50
  61.9 4.6 %hidden_far.1 = (bf16[128,896]{1,0:T(8,128)(2,1)S(1)}, bf16[128,896]{1,0:T(8,128)(2,1)S(1)}) custom-call(bf16[32,4096]{1,0:T(8,128)(2,1)S(1)} %collective-permute-done.9.refs_3_.refs_0_, bf16[96,4096]{1,0:T(8,128)(2,1)S(1)} %far_copy.1.refs_1_.refs_4_, bf16[32,4096]{1,0:T(8,128)(2,1)S(1)} %collective-permute-done.14.refs_16_.refs_2_, ...), custom_call_target="tpu_custom_call" | custom-call | flops 99999997952 | bytes 1 | tf_op jit(solution)/shard_map/hidden_far/pallas_call | solution.py:36
  66.5 3.2 %back_a.1 = (bf16[64,2688]{1,0:T(8,128)(2,1)S(1)}, bf16[64,2688]{1,0:T(8,128)(2,1)S(1)}, bf16[128,2688]{1,0:T(8,128)(2,1)S(1)}) custom-call(bf16[128,896]{1,0:T(8,128)(2,1)S(1)} %get-tuple-element.39.refs_2_.refs_0_, bf16[128,896]{1,0:T(8,128)(2,1)S(1)} %get-tuple-element.40.refs_1_, bf16[128,896]{1,0:T(8,128)(2,1)S(1)} %get-tuple-element.41.refs_2_, ...), custom_call_target="tpu_custom_call" | custom-call | flops 99999997952 | bytes 1 | tf_op jit(solution)/shard_map/back_a/pallas_call | solution.py:36
  70.1 1.8 %back_b.1 = (bf16[64,1408]{1,0:T(8,128)(2,1)S(1)}, bf16[64,1408]{1,0:T(8,128)(2,1)S(1)}, bf16[128,1408]{1,0:T(8,128)(2,1)S(1)}) custom-call(bf16[128,896]{1,0:T(8,128)(2,1)S(1)} %get-tuple-element.39.refs_2_.refs_0_, bf16[128,896]{1,0:T(8,128)(2,1)S(1)} %get-tuple-element.40.refs_1_, bf16[128,896]{1,0:T(8,128)(2,1)S(1)} %get-tuple-element.41.refs_2_, ...), custom_call_target="tpu_custom_call" | custom-call | flops 99999997952 | bytes 1 | tf_op jit(solution)/shard_map/back_b/pallas_call | solution.py:36
  73.1 1.1 %collective-permute-start.27 = (bf16[64,2688]{1,0:T(8,128)(2,1)S(1)}, bf16[64,2688]{1,0:T(8,128)(2,1)S(1)}, u32[]{:S(2)}, u32[]{:S(2)}) collective-permute-start(bf16[64,2688]{1,0:T(8,128)(2,1)S(1)} %to_home_x.1.refs_5_), channel_id=1, source_target_pairs={{0,12},{1,5},{2,14},{3,7},{4,0},{5,9},{6,2},{7,11},{8,4},{9,13},{1... | collective-permute-start | bytes 1032200 | tf_op jit(solution)/shard_map/home_x/ppermute | solution.py:50
  75.2 4.4 %collective-permute-done.28.refs_4_ = bf16[64,2688]{1,0:T(8,128)(2,1)S(1)} collective-permute-done((bf16[64,2688]{1,0:T(8,128)(2,1)S(1)}, bf16[64,2688]{1,0:T(8,128)(2,1)S(1)}, u32[]{:S(2)}, u32[]{:S(2)}) %collective-permute-start.28) | collective-permute-done | bytes 344096 | tf_op jit(solution)/shard_map/from_far/ppermute | solution.py:50
  79.9 3.5 %collective-permute-done.27.refs_0_ = bf16[64,2688]{1,0:T(8,128)(2,1)S(1)} collective-permute-done((bf16[64,2688]{1,0:T(8,128)(2,1)S(1)}, bf16[64,2688]{1,0:T(8,128)(2,1)S(1)}, u32[]{:S(2)}, u32[]{:S(2)}) %collective-permute-start.27) | collective-permute-done | bytes 344096 | tf_op jit(solution)/shard_map/home_x/ppermute | solution.py:50
  84.6 2.9 %collective-permute-start.29 = (bf16[32,1408]{1,0:T(8,128)(2,1)S(1)}, bf16[32,1408]{1,0:T(8,128)(2,1)S(1)}, u32[]{:S(2)}, u32[]{:S(2)}) collective-permute-start(bf16[32,1408]{1,0:T(8,128)(2,1)S(1)} %get-tuple-element.51), channel_id=1, source_target_pairs={{0,8},{1,9},{2,10},{3,11},{4,12},{5,13},{6,14},{7,15},{8,0},{9,1},... | collective-permute-start | bytes 270344 | tf_op jit(solution)/shard_map/home_far/ppermute | solution.py:50
  88.4 2.9 %collective-permute-done.29.refs_2_.refs_1_ = bf16[32,1408]{1,0:T(8,128)(2,1)S(1)} collective-permute-done((bf16[32,1408]{1,0:T(8,128)(2,1)S(1)}, bf16[32,1408]{1,0:T(8,128)(2,1)S(1)}, u32[]{:S(2)}, u32[]{:S(2)}) %collective-permute-start.29) | collective-permute-done | bytes 90144 | tf_op jit(solution)/shard_map/home_far/ppermute | solution.py:50
  91.3 2.2 %collective-permute-start.34 = (bf16[32,1408]{1,0:T(8,128)(2,1)S(1)}, bf16[32,1408]{1,0:T(8,128)(2,1)S(1)}, u32[]{:S(2)}, u32[]{:S(2)}) collective-permute-start(bf16[32,1408]{1,0:T(8,128)(2,1)S(1)} %home_b_part.1), channel_id=1, source_target_pairs={{0,1},{1,0},{2,3},{3,2},{4,5},{5,4},{6,7},{7,6},{8,9},{9,8},{10,11... | collective-permute-start | bytes 270344 | tf_op jit(solution)/shard_map/home_b_core/ppermute | solution.py:50
  93.5 0.9 collective-permute-done.34.refs_3_
  94.5 1.0 %final.1 = bf16[32,4096]{1,0:T(8,128)(2,1)} custom-call(bf16[32,1408]{1,0:T(8,128)(2,1)S(1)} %get-tuple-element.50.refs_4_.refs_0_, bf16[32,1408]{1,0:T(8,128)(2,1)S(1)} %collective-permute-done.29.refs_2_.refs_1_, bf16[64,1408]{1,0:T(8,128)(2,1)S(1)} %collective-permute-done.30.refs_0_.refs_2_, bf16[32,1408]{1,0:T(8,128)(2,1)S(1)} %collective-permute-done.34.refs_3_, ...), custom_call_target="tpu_custom_call" | custom-call | flops 1 | bytes 1 | tf_op jit(solution)/shard_map/final/pallas_call | solution.py:36
  (92 shorter events, 11.9 us)
Async XLA Ops:
  0.0 11.9 %collective-permute-start = (bf16[32,4096]{1,0:T(8,128)(2,1)}, bf16[32,4096]{1,0:T(8,128)(2,1)S(1)}, u32[]{:S(2)}, u32[]{:S(2)}) collective-permute-start(bf16[32,4096]{1,0:T(8,128)(2,1)} %bitcast.32), channel_id=1, source_target_pairs={{16,0},{32,16},{48,32},{64,48},{80,64},{96,80},{112,96},{0,112},{1... | collective-permute-start | bytes 786440 | tf_op jit(solution)/shard_map/shift/ppermute | solution.py:305
  8.0 12.5 %collective-permute-start.6 = (bf16[32,4224]{1,0:T(8,128)(2,1)S(1)}, bf16[32,4224]{1,0:T(8,128)(2,1)S(1)}, u32[]{:S(2)}, u32[]{:S(2)}) collective-permute-start(bf16[32,4224]{1,0:T(8,128)(2,1)S(1)} %get-tuple-element.32), channel_id=1, source_target_pairs={{112,0},{96,16},{80,32},{64,48},{113,1},{97,17},{81,33},{65,49},{1... | collective-permute-start | bytes 811016 | tf_op jit(solution)/shard_map/fetched/ppermute | solution.py:303
  11.9 5.3 %collective-permute-start.2 = (bf16[32,4096]{1,0:T(8,128)(2,1)S(1)}, bf16[32,4096]{1,0:T(8,128)(2,1)S(1)}, u32[]{:S(2)}, u32[]{:S(2)}) collective-permute-start(bf16[32,4096]{1,0:T(8,128)(2,1)S(1)} %cot.1.refs_0_.refs_6_), channel_id=1, source_target_pairs={{0,1},{1,0},{2,3},{3,2},{4,5},{5,4},{6,7},{7,6},{8,9},{9,8},{10,11... | collective-permute-start | bytes 786440 | tf_op jit(solution)/shard_map/cot_core/ppermute | solution.py:50
  13.6 10.1 %collective-permute-start.9 = (bf16[32,4096]{1,0:T(8,128)(2,1)S(1)}, bf16[32,4096]{1,0:T(8,128)(2,1)S(1)}, u32[]{:S(2)}, u32[]{:S(2)}) collective-permute-start(bf16[32,4096]{1,0:T(8,128)(2,1)S(1)} %cot.1.refs_0_.refs_6_), channel_id=1, source_target_pairs={{0,8},{1,9},{2,10},{3,11},{4,12},{5,13},{6,14},{7,15},{8,0},{9,1},... | collective-permute-start | bytes 786440 | tf_op jit(solution)/shard_map/cot_far/ppermute | solution.py:50
  16.5 7.5 %collective-permute-start.1 = (bf16[32,4096]{1,0:T(8,128)(2,1)S(1)}, bf16[32,4096]{1,0:T(8,128)(2,1)S(1)}, u32[]{:S(2)}, u32[]{:S(2)}) collective-permute-start(bf16[32,4096]{1,0:T(8,128)(2,1)S(1)} %cot.1.refs_0_.refs_6_), channel_id=1, source_target_pairs={{0,2},{1,3},{2,0},{3,1},{4,6},{5,7},{6,4},{7,5},{8,10},{9,11},{10,... | collective-permute-start | bytes 786440 | tf_op jit(solution)/shard_map/cot_z/ppermute | solution.py:50
  17.3 12.1 %collective-permute-start.4 = (bf16[64,4096]{1,0:T(8,128)(2,1)S(1)}, bf16[64,4096]{1,0:T(8,128)(2,1)S(1)}, u32[]{:S(2)}, u32[]{:S(2)}) collective-permute-start(bf16[64,4096]{1,0:T(8,128)(2,1)S(1)} %cot_chip.1.refs_3_), channel_id=1, source_target_pairs={{0,4},{1,13},{2,6},{3,15},{4,8},{5,1},{6,10},{7,3},{8,12},{9,5},{1... | collective-permute-start | bytes 1572872 | tf_op jit(solution)/shard_map/cot_ahead/ppermute | solution.py:50
  20.8 3.2 %collective-permute-start.8 = (bf16[32,4096]{1,0:T(8,128)(2,1)S(1)}, bf16[32,4096]{1,0:T(8,128)(2,1)S(1)}, u32[]{:S(2)}, u32[]{:S(2)}) collective-permute-start(bf16[32,4096]{1,0:T(8,128)(2,1)S(1)} %get-tuple-element.34.refs_0_.refs_1_.refs_6_), channel_id=1, source_target_pairs={{0,1},{1,0},{2,3},{3,2},{4,5},{5,4},{6,7},{7,6},{8,9},{9,8},{10,11... | collective-permute-start | bytes 786440 | tf_op jit(solution)/shard_map/normed_core/ppermute | solution.py:50
  22.9 7.9 %collective-permute-start.7 = (bf16[32,4096]{1,0:T(8,128)(2,1)S(1)}, bf16[32,4096]{1,0:T(8,128)(2,1)S(1)}, u32[]{:S(2)}, u32[]{:S(2)}) collective-permute-start(bf16[32,4096]{1,0:T(8,128)(2,1)S(1)} %get-tuple-element.34.refs_0_.refs_1_.refs_6_), channel_id=1, source_target_pairs={{0,2},{1,3},{2,0},{3,1},{4,6},{5,7},{6,4},{7,5},{8,10},{9,11},{10,... | collective-permute-start | bytes 786440 | tf_op jit(solution)/shard_map/normed_z/ppermute | solution.py:50
  24.1 10.9 %collective-permute-start.11 = (bf16[64,4096]{1,0:T(8,128)(2,1)S(1)}, bf16[64,4096]{1,0:T(8,128)(2,1)S(1)}, u32[]{:S(2)}, u32[]{:S(2)}) collective-permute-start(bf16[64,4096]{1,0:T(8,128)(2,1)S(1)} %chip.1.refs_2_), channel_id=1, source_target_pairs={{0,4},{1,13},{2,6},{3,15},{4,8},{5,1},{6,10},{7,3},{8,12},{9,5},{1... | collective-permute-start | bytes 1572872 | tf_op jit(solution)/shard_map/ahead/ppermute | solution.py:50
  26.9 8.9 %collective-permute-start.14 = (bf16[32,4096]{1,0:T(8,128)(2,1)S(1)}, bf16[32,4096]{1,0:T(8,128)(2,1)S(1)}, u32[]{:S(2)}, u32[]{:S(2)}) collective-permute-start(bf16[32,4096]{1,0:T(8,128)(2,1)S(1)} %collective-permute-done.9.refs_3_.refs_0_), channel_id=1, source_target_pairs={{0,1},{1,0},{2,3},{3,2},{4,5},{5,4},{6,7},{7,6},{8,9},{9,8},{10,11... | collective-permute-start | bytes 786440 | tf_op jit(solution)/shard_map/cot_far_core/ppermute | solution.py:50
  29.5 9.1 %collective-permute-start.5 = (bf16[64,4096]{1,0:T(8,128)(2,1)S(1)}, bf16[64,4096]{1,0:T(8,128)(2,1)S(1)}, u32[]{:S(2)}, u32[]{:S(2)}) collective-permute-start(bf16[64,4096]{1,0:T(8,128)(2,1)S(1)} %collective-permute-done.4.refs_0_.refs_4_), channel_id=1, source_target_pairs={{0,1},{1,0},{2,3},{3,2},{4,5},{5,4},{6,7},{7,6},{8,9},{9,8},{10,11... | collective-permute-start | bytes 1572872 | tf_op jit(solution)/shard_map/cot_behind/ppermute | solution.py:50
  30.8 5.1 %collective-permute-start.10 = (bf16[32,4096]{1,0:T(8,128)(2,1)S(1)}, bf16[32,4096]{1,0:T(8,128)(2,1)S(1)}, u32[]{:S(2)}, u32[]{:S(2)}) collective-permute-start(bf16[32,4096]{1,0:T(8,128)(2,1)S(1)} %normed_z_copy.1), channel_id=1, source_target_pairs={{0,1},{1,0},{2,3},{3,2},{4,5},{5,4},{6,7},{7,6},{8,9},{9,8},{10,11... | collective-permute-start | bytes 786440 | tf_op jit(solution)/shard_map/normed_z_core/ppermute | solution.py:50
  31.7 13.8 %collective-permute-start.16 = (bf16[64,4096]{1,0:T(8,128)(2,1)S(1)}, bf16[64,4096]{1,0:T(8,128)(2,1)S(1)}, u32[]{:S(2)}, u32[]{:S(2)}) collective-permute-start(bf16[64,4096]{1,0:T(8,128)(2,1)S(1)} %cot_ahead_copy.1.refs_1_), channel_id=1, source_target_pairs={{0,2},{1,3},{2,0},{3,1},{4,6},{5,7},{6,4},{7,5},{8,10},{9,11},{10,... | collective-permute-start | bytes 1572872 | tf_op jit(solution)/shard_map/cot_ahead_z/ppermute | solution.py:50
  35.8 2.8 %collective-permute-start.12 = (bf16[32,4096]{1,0:T(8,128)(2,1)S(1)}, bf16[32,4096]{1,0:T(8,128)(2,1)S(1)}, u32[]{:S(2)}, u32[]{:S(2)}) collective-permute-start(bf16[32,4096]{1,0:T(8,128)(2,1)S(1)} %behind_0.1), channel_id=1, source_target_pairs={{0,1},{1,0},{2,3},{3,2},{4,5},{5,4},{6,7},{7,6},{8,9},{9,8},{10,11... | collective-permute-start | bytes 786440 | tf_op jit(solution)/shard_map/behind_0/ppermute | solution.py:50
  35.9 2.7 %collective-permute-start.13 = (bf16[32,4096]{1,0:T(8,128)(2,1)S(1)}, bf16[32,4096]{1,0:T(8,128)(2,1)S(1)}, u32[]{:S(2)}, u32[]{:S(2)}) collective-permute-start(bf16[32,4096]{1,0:T(8,128)(2,1)S(1)} %behind_32.1), channel_id=1, source_target_pairs={{0,1},{1,0},{2,3},{3,2},{4,5},{5,4},{6,7},{7,6},{8,9},{9,8},{10,11... | collective-permute-start | bytes 786440 | tf_op jit(solution)/shard_map/behind_32/ppermute | solution.py:50
  36.9 10.4 %collective-permute-start.15 = (bf16[64,4096]{1,0:T(8,128)(2,1)S(1)}, bf16[64,4096]{1,0:T(8,128)(2,1)S(1)}, u32[]{:S(2)}, u32[]{:S(2)}) collective-permute-start(bf16[64,4096]{1,0:T(8,128)(2,1)S(1)} %chip_z.1.refs_9_), channel_id=1, source_target_pairs={{0,4},{1,13},{2,6},{3,15},{4,8},{5,1},{6,10},{7,3},{8,12},{9,5},{1... | collective-permute-start | bytes 1572872 | tf_op jit(solution)/shard_map/ahead_z/ppermute | solution.py:50
  45.6 4.6 %collective-permute-start.17 = (bf16[48,4096]{1,0:T(8,128)(2,1)S(1)}, bf16[48,4096]{1,0:T(8,128)(2,1)S(1)}, u32[]{:S(2)}, u32[]{:S(2)}) collective-permute-start(bf16[48,4096]{1,0:T(8,128)(2,1)S(1)} %cot_behind_z_0.1), channel_id=1, source_target_pairs={{0,1},{1,0},{2,3},{3,2},{4,5},{5,4},{6,7},{7,6},{8,9},{9,8},{10,11... | collective-permute-start | bytes 1179656 | tf_op jit(solution)/shard_map/cot_behind_z_0/ppermute | solution.py:50
  46.4 3.8 %collective-permute-start.18 = (bf16[16,4096]{1,0:T(8,128)(2,1)S(1)}, bf16[16,4096]{1,0:T(8,128)(2,1)S(1)}, u32[]{:S(2)}, u32[]{:S(2)}) collective-permute-start(bf16[16,4096]{1,0:T(8,128)(2,1)S(1)} %cot_behind_z_48.1), channel_id=1, source_target_pairs={{0,1},{1,0},{2,3},{3,2},{4,5},{5,4},{6,7},{7,6},{8,9},{9,8},{10,11... | collective-permute-start | bytes 393224 | tf_op jit(solution)/shard_map/cot_behind_z_48/ppermute | solution.py:50
  46.5 12.8 %collective-permute-start.22 = (bf16[32,4096]{1,0:T(8,128)(2,1)S(1)}, bf16[32,4096]{1,0:T(8,128)(2,1)S(1)}, u32[]{:S(2)}, u32[]{:S(2)}) collective-permute-start(bf16[32,4096]{1,0:T(8,128)(2,1)S(1)} %collective-permute-done.9.refs_3_.refs_0_), channel_id=1, source_target_pairs={{0,2},{1,3},{2,0},{3,1},{4,6},{5,7},{6,4},{7,5},{8,10},{9,11},{10,... | collective-permute-start | bytes 786440 | tf_op jit(solution)/shard_map/cot_far_z/ppermute | solution.py:50
  47.3 12.0 %collective-permute-start.21 = (bf16[64,4096]{1,0:T(8,128)(2,1)S(1)}, bf16[64,4096]{1,0:T(8,128)(2,1)S(1)}, u32[]{:S(2)}, u32[]{:S(2)}) collective-permute-start(bf16[64,4096]{1,0:T(8,128)(2,1)S(1)} %part.1.refs_4_), channel_id=1, source_target_pairs={{0,4},{1,13},{2,6},{3,15},{4,8},{5,1},{6,10},{7,3},{8,12},{9,5},{1... | collective-permute-start | bytes 1572872 | tf_op jit(solution)/shard_map/far/ppermute | solution.py:50
  50.1 4.6 %collective-permute-start.20 = (bf16[64,4096]{1,0:T(8,128)(2,1)S(1)}, bf16[64,4096]{1,0:T(8,128)(2,1)S(1)}, u32[]{:S(2)}, u32[]{:S(2)}) collective-permute-start(bf16[64,4096]{1,0:T(8,128)(2,1)S(1)} %collective-permute-done.15.refs_1_.refs_3_), channel_id=1, source_target_pairs={{0,1},{1,0},{2,3},{3,2},{4,5},{5,4},{6,7},{7,6},{8,9},{9,8},{10,11... | collective-permute-start | bytes 1572872 | tf_op jit(solution)/shard_map/behind_z/ppermute | solution.py:50
  60.0 6.5 %collective-permute-start.19 = (bf16[128,4096]{1,0:T(8,128)(2,1)S(1)}, bf16[128,4096]{1,0:T(8,128)(2,1)S(1)}, u32[]{:S(2)}, u32[]{:S(2)}) collective-permute-start(bf16[128,4096]{1,0:T(8,128)(2,1)S(1)} %get-tuple-element.38.refs_8_), channel_id=1, source_target_pairs={{0,1},{1,0},{2,3},{3,2},{4,5},{5,4},{6,7},{7,6},{8,9},{9,8},{10,11... | collective-permute-start | bytes 3145736 | tf_op jit(solution)/shard_map/near_got/ppermute | solution.py:50
  72.3 7.4 %collective-permute-start.28 = (bf16[64,2688]{1,0:T(8,128)(2,1)S(1)}, bf16[64,2688]{1,0:T(8,128)(2,1)S(1)}, u32[]{:S(2)}, u32[]{:S(2)}) collective-permute-start(bf16[64,2688]{1,0:T(8,128)(2,1)S(1)} %to_far.1.refs_4_), channel_id=1, source_target_pairs={{0,12},{1,5},{2,14},{3,7},{4,0},{5,9},{6,2},{7,11},{8,4},{9,13},{1... | collective-permute-start | bytes 1032200 | tf_op jit(solution)/shard_map/from_far/ppermute | solution.py:50
  73.1 10.2 %collective-permute-start.27 = (bf16[64,2688]{1,0:T(8,128)(2,1)S(1)}, bf16[64,2688]{1,0:T(8,128)(2,1)S(1)}, u32[]{:S(2)}, u32[]{:S(2)}) collective-permute-start(bf16[64,2688]{1,0:T(8,128)(2,1)S(1)} %to_home_x.1.refs_5_), channel_id=1, source_target_pairs={{0,12},{1,5},{2,14},{3,7},{4,0},{5,9},{6,2},{7,11},{8,4},{9,13},{1... | collective-permute-start | bytes 1032200 | tf_op jit(solution)/shard_map/home_x/ppermute | solution.py:50
  74.3 9.7 %collective-permute-start.26 = (bf16[128,1408]{1,0:T(8,128)(2,1)S(1)}, bf16[128,1408]{1,0:T(8,128)(2,1)S(1)}, u32[]{:S(2)}, u32[]{:S(2)}) collective-permute-start(bf16[128,1408]{1,0:T(8,128)(2,1)S(1)} %away.1.refs_2_), channel_id=1, source_target_pairs={{0,2},{1,3},{2,0},{3,1},{4,6},{5,7},{6,4},{7,5},{8,10},{9,11},{10,... | collective-permute-start | bytes 1081352 | tf_op jit(solution)/shard_map/from_z/ppermute | solution.py:50
  79.8 7.7 %collective-permute-start.31 = (bf16[64,2688]{1,0:T(8,128)(2,1)S(1)}, bf16[64,2688]{1,0:T(8,128)(2,1)S(1)}, u32[]{:S(2)}, u32[]{:S(2)}) collective-permute-start(bf16[64,2688]{1,0:T(8,128)(2,1)S(1)} %to_home.1.refs_1_), channel_id=1, source_target_pairs={{0,12},{1,5},{2,14},{3,7},{4,0},{5,9},{6,2},{7,11},{8,4},{9,13},{1... | collective-permute-start | bytes 1032200 | tf_op jit(solution)/shard_map/home/ppermute | solution.py:50
  83.4 4.1 %collective-permute-start.33 = (bf16[32,2688]{1,0:T(8,128)(2,1)S(1)}, bf16[32,2688]{1,0:T(8,128)(2,1)S(1)}, u32[]{:S(2)}, u32[]{:S(2)}) collective-permute-start(bf16[32,2688]{1,0:T(8,128)(2,1)S(1)} %home_x_core_z_part.1), channel_id=1, source_target_pairs={{0,1},{1,0},{2,3},{3,2},{4,5},{5,4},{6,7},{7,6},{8,9},{9,8},{10,11... | collective-permute-start | bytes 516104 | tf_op jit(solution)/shard_map/home_x_core_z/ppermute | solution.py:50
  83.8 3.7 %collective-permute-start.32 = (bf16[32,2688]{1,0:T(8,128)(2,1)S(1)}, bf16[32,2688]{1,0:T(8,128)(2,1)S(1)}, u32[]{:S(2)}, u32[]{:S(2)}) collective-permute-start(bf16[32,2688]{1,0:T(8,128)(2,1)S(1)} %home_x_core_part.1), channel_id=1, source_target_pairs={{0,1},{1,0},{2,3},{3,2},{4,5},{5,4},{6,7},{7,6},{8,9},{9,8},{10,11... | collective-permute-start | bytes 516104 | tf_op jit(solution)/shard_map/home_x_core/ppermute | solution.py:50
  84.2 7.1 %collective-permute-start.30 = (bf16[64,1408]{1,0:T(8,128)(2,1)S(1)}, bf16[64,1408]{1,0:T(8,128)(2,1)S(1)}, u32[]{:S(2)}, u32[]{:S(2)}) collective-permute-start(bf16[64,1408]{1,0:T(8,128)(2,1)S(1)} %get-tuple-element.52), channel_id=1, source_target_pairs={{0,12},{1,5},{2,14},{3,7},{4,0},{5,9},{6,2},{7,11},{8,4},{9,13},{1... | collective-permute-start | bytes 540680 | tf_op jit(solution)/shard_map/home_b/ppermute | solution.py:50
  84.6 6.7 %collective-permute-start.29 = (bf16[32,1408]{1,0:T(8,128)(2,1)S(1)}, bf16[32,1408]{1,0:T(8,128)(2,1)S(1)}, u32[]{:S(2)}, u32[]{:S(2)}) collective-permute-start(bf16[32,1408]{1,0:T(8,128)(2,1)S(1)} %get-tuple-element.51), channel_id=1, source_target_pairs={{0,8},{1,9},{2,10},{3,11},{4,12},{5,13},{6,14},{7,15},{8,0},{9,1},... | collective-permute-start | bytes 270344 | tf_op jit(solution)/shard_map/home_far/ppermute | solution.py:50
  87.6 6.9 %collective-permute-start.35 = (bf16[32,2688]{1,0:T(8,128)(2,1)S(1)}, bf16[32,2688]{1,0:T(8,128)(2,1)S(1)}, u32[]{:S(2)}, u32[]{:S(2)}) collective-permute-start(bf16[32,2688]{1,0:T(8,128)(2,1)S(1)} %get-tuple-element.54), channel_id=1, source_target_pairs={{0,2},{1,3},{2,0},{3,1},{4,6},{5,7},{6,4},{7,5},{8,10},{9,11},{10,... | collective-permute-start | bytes 516104 | tf_op jit(solution)/shard_map/total_z/ppermute | solution.py:50
  91.3 3.2 %collective-permute-start.34 = (bf16[32,1408]{1,0:T(8,128)(2,1)S(1)}, bf16[32,1408]{1,0:T(8,128)(2,1)S(1)}, u32[]{:S(2)}, u32[]{:S(2)}) collective-permute-start(bf16[32,1408]{1,0:T(8,128)(2,1)S(1)} %home_b_part.1), channel_id=1, source_target_pairs={{0,1},{1,0},{2,3},{3,2},{4,5},{5,4},{6,7},{7,6},{8,9},{9,8},{10,11... | collective-permute-start | bytes 270344 | tf_op jit(solution)/shard_map/home_b_core/ppermute | solution.py:50
  (13 other events, 149.4 us)

commit v6 on v5

--- a/solution.py
+++ b/solution.py
@@ -305,7 +305,6 @@
         cot = lax.ppermute(pending[0], "section", shift_pairs)
     w_gate, w_up, w_down = w_gate[0], w_up[0], w_down[0]
     weights = w_gate, w_up, w_down
-    cot = join("cot", cot, after=(own_stash,))
     cot_z = over_tensor("cot_z", cot, other_z)
     cot_far = over_tensor("cot_far", cot, across_y)
     cot_core = over_tensor("cot_core", cot, other_core)

time: 95.6 us -> 95.6 us (level)
    pallas_call x32 -> x31, Pallas kernels: 29.3 us -> 29.3 us  [local_kernel(): pl.pallas_call(run, out_shape=outs, in_specs=[anywhere if hbm else VMEM]...]
  transfers between devices with their start and end apart: 36 -> 36, of which waited for: 12 -> 13; matrix products, arithmetic and copies ran while one was open for 0% -> 0% of each run, Pallas kernels for 26% -> 26%
where the time goes in v6:
time: 95.6 us; the launch traced here: 95.5 us
  starting transfers between devices  40.2 us (42%)
  Pallas kernels  29.3 us (31%)
  waiting for transfers between devices  25.6 us (27%)
    ppermute x34, starting transfers between devices, over_tensor(): lax.ppermute(shard, 'tensor', [(i, move(i)) for i in range(lax.axis_size(...  32.3 us
    pallas_call x31, Pallas kernels, local_kernel(): pl.pallas_call(run, out_shape=outs, in_specs=[anywhere if hbm else VMEM]...  29.3 us
    ppermute x34, waiting for transfers between devices, over_tensor(): lax.ppermute(shard, 'tensor', [(i, move(i)) for i in range(lax.axis_size(...  20.4 us
    ppermute x1, starting transfers between devices, on_device(): cot = lax.ppermute(pending[0], 'section', shift_pairs)  6.62 us
    ppermute x1, waiting for transfers between devices, on_device(): cot = lax.ppermute(pending[0], 'section', shift_pairs)  2.61 us
    ppermute x1, waiting for transfers between devices, on_device(): fetched = lax.ppermute(payload, 'section', stash_pairs)  2.54 us
  transfers between devices with their start and end apart: 36, of which 13 were waited for; matrix products, arithmetic and copies ran while one was open for 0% of the time, Pallas kernels for 26%

profile of v6, /device:TPU:1, one launch (start us, length us, event | category | flops | bytes accessed | tf_op | source)
XLA Modules:
  0.0 95.5 jit_solution(17359172579578112325)
XLA Ops:
  0.0 6.6 %collective-permute-start = (bf16[32,4096]{1,0:T(8,128)(2,1)}, bf16[32,4096]{1,0:T(8,128)(2,1)S(1)}, u32[]{:S(2)}, u32[]{:S(2)}) collective-permute-start(bf16[32,4096]{1,0:T(8,128)(2,1)} %bitcast.32), channel_id=1, source_target_pairs={{16,0},{32,16},{48,32},{64,48},{80,64},{96,80},{112,96},{0,112},{1... | collective-permute-start | bytes 786440 | tf_op jit(solution)/shard_map/shift/ppermute | solution.py:305
  6.6 1.4 %prepare.1 = (bf16[32,4224]{1,0:T(8,128)(2,1)S(1)}, bf16[32,4352]{1,0:T(8,128)(2,1)S(1)}, f32[1,4096]{1,0:T(1,128)S(1)}) custom-call(s32[8]{0:T(128)} %refs_0_.1, s32[8]{0:T(128)} %refs_1_.1, bf16[2,32,4096]{2,1,0:T(8,128)(2,1)} %bitcast.28, bf16[2,32]{1,0:T(2,128)(2,1)} %bitcast.30, bf16[2,32,4096]{2,1,0:T(8,128)(2,1)} %bitcast.29, bf16[2,32]{1,0:T(2,128)(2,1)} %bitcast.31, ...), custom_call_target="tpu_custom_call" | custom-call | flops 1 | bytes 1 | tf_op jit(solution)/shard_map/prepare/pallas_call | solution.py:36
  8.0 1.3 %collective-permute-start.6 = (bf16[32,4224]{1,0:T(8,128)(2,1)S(1)}, bf16[32,4224]{1,0:T(8,128)(2,1)S(1)}, u32[]{:S(2)}, u32[]{:S(2)}) collective-permute-start(bf16[32,4224]{1,0:T(8,128)(2,1)S(1)} %get-tuple-element.32), channel_id=1, source_target_pairs={{112,0},{96,16},{80,32},{64,48},{113,1},{97,17},{81,33},{65,49},{1... | collective-permute-start | bytes 811016 | tf_op jit(solution)/shard_map/fetched/ppermute | solution.py:303
  9.3 2.6 %collective-permute-done.refs_0_.refs_6_ = bf16[32,4096]{1,0:T(8,128)(2,1)S(1)} collective-permute-done((bf16[32,4096]{1,0:T(8,128)(2,1)}, bf16[32,4096]{1,0:T(8,128)(2,1)S(1)}, u32[]{:S(2)}, u32[]{:S(2)}) %collective-permute-start) | collective-permute-done | bytes 262176 | tf_op jit(solution)/shard_map/shift/ppermute | solution.py:305
  11.9 1.5 %collective-permute-start.2 = (bf16[32,4096]{1,0:T(8,128)(2,1)S(1)}, bf16[32,4096]{1,0:T(8,128)(2,1)S(1)}, u32[]{:S(2)}, u32[]{:S(2)}) collective-permute-start(bf16[32,4096]{1,0:T(8,128)(2,1)S(1)} %collective-permute-done.refs_0_.refs_6_), channel_id=1, source_target_pairs={{0,1},{1,0},{2,3},{3,2},{4,5},{5,4},{6,7},{7,6},{8,9},{9,8},{10,11... | collective-permute-start | bytes 786440 | tf_op jit(solution)/shard_map/cot_core/ppermute | solution.py:50
  13.5 2.9 %collective-permute-start.9 = (bf16[32,4096]{1,0:T(8,128)(2,1)S(1)}, bf16[32,4096]{1,0:T(8,128)(2,1)S(1)}, u32[]{:S(2)}, u32[]{:S(2)}) collective-permute-start(bf16[32,4096]{1,0:T(8,128)(2,1)S(1)} %collective-permute-done.refs_0_.refs_6_), channel_id=1, source_target_pairs={{0,8},{1,9},{2,10},{3,11},{4,12},{5,13},{6,14},{7,15},{8,0},{9,1},... | collective-permute-start | bytes 786440 | tf_op jit(solution)/shard_map/cot_far/ppermute | solution.py:50
  17.2 0.8 collective-permute-start.4
  18.0 2.5 %collective-permute-done.6.refs_1_ = bf16[32,4224]{1,0:T(8,128)(2,1)S(1)} collective-permute-done((bf16[32,4224]{1,0:T(8,128)(2,1)S(1)}, bf16[32,4224]{1,0:T(8,128)(2,1)S(1)}, u32[]{:S(2)}, u32[]{:S(2)}) %collective-permute-start.6) | collective-permute-done | bytes 270368 | tf_op jit(solution)/shard_map/fetched/ppermute | solution.py:303
  20.8 2.0 %collective-permute-start.8 = (bf16[32,4096]{1,0:T(8,128)(2,1)S(1)}, bf16[32,4096]{1,0:T(8,128)(2,1)S(1)}, u32[]{:S(2)}, u32[]{:S(2)}) collective-permute-start(bf16[32,4096]{1,0:T(8,128)(2,1)S(1)} %get-tuple-element.34.refs_0_.refs_1_.refs_6_), channel_id=1, source_target_pairs={{0,1},{1,0},{2,3},{3,2},{4,5},{5,4},{6,7},{7,6},{8,9},{9,8},{10,11... | collective-permute-start | bytes 786440 | tf_op jit(solution)/shard_map/normed_core/ppermute | solution.py:50
  24.1 2.8 %collective-permute-start.11 = (bf16[64,4096]{1,0:T(8,128)(2,1)S(1)}, bf16[64,4096]{1,0:T(8,128)(2,1)S(1)}, u32[]{:S(2)}, u32[]{:S(2)}) collective-permute-start(bf16[64,4096]{1,0:T(8,128)(2,1)S(1)} %chip.1.refs_2_), channel_id=1, source_target_pairs={{0,4},{1,13},{2,6},{3,15},{4,8},{5,1},{6,10},{7,3},{8,12},{9,5},{1... | collective-permute-start | bytes 1572872 | tf_op jit(solution)/shard_map/ahead/ppermute | solution.py:50
  26.9 2.4 %collective-permute-done.4.refs_0_.refs_4_ = bf16[64,4096]{1,0:T(8,128)(2,1)S(1)} collective-permute-done((bf16[64,4096]{1,0:T(8,128)(2,1)S(1)}, bf16[64,4096]{1,0:T(8,128)(2,1)S(1)}, u32[]{:S(2)}, u32[]{:S(2)}) %collective-permute-start.4) | collective-permute-done | bytes 524320 | tf_op jit(solution)/shard_map/cot_ahead/ppermute | solution.py:50
  29.5 1.3 %collective-permute-done.7.refs_0_.refs_7_ = bf16[32,4096]{1,0:T(8,128)(2,1)S(1)} collective-permute-done((bf16[32,4096]{1,0:T(8,128)(2,1)S(1)}, bf16[32,4096]{1,0:T(8,128)(2,1)S(1)}, u32[]{:S(2)}, u32[]{:S(2)}) %collective-permute-start.7) | collective-permute-done | bytes 262176 | tf_op jit(solution)/shard_map/normed_z/ppermute | solution.py:50
  30.8 1.0 collective-permute-start.10
  32.5 2.4 %collective-permute-done.11.refs_0_.refs_10_ = bf16[64,4096]{1,0:T(8,128)(2,1)S(1)} collective-permute-done((bf16[64,4096]{1,0:T(8,128)(2,1)S(1)}, bf16[64,4096]{1,0:T(8,128)(2,1)S(1)}, u32[]{:S(2)}, u32[]{:S(2)}) %collective-permute-start.11) | collective-permute-done | bytes 524320 | tf_op jit(solution)/shard_map/ahead/ppermute | solution.py:50
  36.8 1.7 %collective-permute-start.15 = (bf16[64,4096]{1,0:T(8,128)(2,1)S(1)}, bf16[64,4096]{1,0:T(8,128)(2,1)S(1)}, u32[]{:S(2)}, u32[]{:S(2)}) collective-permute-start(bf16[64,4096]{1,0:T(8,128)(2,1)S(1)} %chip_z.1.refs_9_), channel_id=1, source_target_pairs={{0,4},{1,13},{2,6},{3,15},{4,8},{5,1},{6,10},{7,3},{8,12},{9,5},{1... | collective-permute-start | bytes 1572872 | tf_op jit(solution)/shard_map/ahead_z/ppermute | solution.py:50
  38.6 6.8 %hidden_near.1 = (bf16[256,896]{1,0:T(8,128)(2,1)S(1)}, bf16[256,896]{1,0:T(8,128)(2,1)S(1)}) custom-call(bf16[32,4096]{1,0:T(8,128)(2,1)S(1)} %collective-permute-done.refs_0_.refs_6_, bf16[32,4096]{1,0:T(8,128)(2,1)S(1)} %collective-permute-done.1.refs_2_.refs_1_, bf16[32,4096]{1,0:T(8,128)(2,1)S(1)} %collective-permute-done.2.refs_1_.refs_2_, ...), custom_call_target="tpu_custom_call" | custom-call | flops 1 | bytes 1 | tf_op jit(solution)/shard_map/hidden_near/pallas_call | solution.py:36
  45.5 0.9 collective-permute-start.17
  47.3 2.8 %collective-permute-start.21 = (bf16[64,4096]{1,0:T(8,128)(2,1)S(1)}, bf16[64,4096]{1,0:T(8,128)(2,1)S(1)}, u32[]{:S(2)}, u32[]{:S(2)}) collective-permute-start(bf16[64,4096]{1,0:T(8,128)(2,1)S(1)} %part.1.refs_4_), channel_id=1, source_target_pairs={{0,4},{1,13},{2,6},{3,15},{4,8},{5,1},{6,10},{7,3},{8,12},{9,5},{1... | collective-permute-start | bytes 1572872 | tf_op jit(solution)/shard_map/far/ppermute | solution.py:50
  50.1 4.5 %back_near.1 = (bf16[64,4096]{1,0:T(8,128)(2,1)S(1)}, bf16[64,4096]{1,0:T(8,128)(2,1)S(1)}, bf16[128,4096]{1,0:T(8,128)(2,1)S(1)}) custom-call(bf16[256,896]{1,0:T(8,128)(2,1)S(1)} %get-tuple-element.35.refs_2_.refs_1_.refs_0_, bf16[256,896]{1,0:T(8,128)(2,1)S(1)} %get-tuple-element.36.refs_1_, bf16[4096,896]{1,0:T(8,128)(2,1)S(1)} %bitcast.17, ...), custom_call_target="tpu_custom_call" | custom-call | flops 99999997952 | bytes 1 | tf_op jit(solution)/shard_map/back_near/pallas_call | solution.py:36
  54.7 4.6 %hidden_side_z.1 = (bf16[128,896]{1,0:T(8,128)(2,1)S(1)}, bf16[128,896]{1,0:T(8,128)(2,1)S(1)}) custom-call(bf16[64,4096]{1,0:T(8,128)(2,1)S(1)} %collective-permute-done.16.refs_0_, bf16[48,4096]{1,0:T(8,128)(2,1)S(1)} %collective-permute-done.17.refs_5_.refs_1_, bf16[16,4096]{1,0:T(8,128)(2,1)S(1)} %collective-permute-done.18.refs_6_.refs_2_, ...), custom_call_target="tpu_custom_call" | custom-call | flops 1 | bytes 1 | tf_op jit(solution)/shard_map/hidden_side_z/pallas_call | solution.py:36
  60.3 1.6 %collective-permute-done.23.refs_3_.refs_5_ = bf16[96,4096]{1,0:T(8,128)(2,1)S(1)} collective-permute-done((bf16[96,4096]{1,0:T(8,128)(2,1)S(1)}, bf16[96,4096]{1,0:T(8,128)(2,1)S(1)}, u32[]{:S(2)}, u32[]{:S(2)}) %collective-permute-start.23) | collective-permute-done | bytes 786464 | tf_op jit(solution)/shard_map/far_core/ppermute | solution.py:50
  61.9 4.6 %hidden_far.1 = (bf16[128,896]{1,0:T(8,128)(2,1)S(1)}, bf16[128,896]{1,0:T(8,128)(2,1)S(1)}) custom-call(bf16[32,4096]{1,0:T(8,128)(2,1)S(1)} %collective-permute-done.9.refs_3_.refs_0_, bf16[96,4096]{1,0:T(8,128)(2,1)S(1)} %far_copy.1.refs_1_.refs_4_, bf16[32,4096]{1,0:T(8,128)(2,1)S(1)} %collective-permute-done.14.refs_16_.refs_2_, ...), custom_call_target="tpu_custom_call" | custom-call | flops 99999997952 | bytes 1 | tf_op jit(solution)/shard_map/hidden_far/pallas_call | solution.py:36
  66.5 3.2 %back_a.1 = (bf16[64,2688]{1,0:T(8,128)(2,1)S(1)}, bf16[64,2688]{1,0:T(8,128)(2,1)S(1)}, bf16[128,2688]{1,0:T(8,128)(2,1)S(1)}) custom-call(bf16[128,896]{1,0:T(8,128)(2,1)S(1)} %get-tuple-element.39.refs_2_.refs_0_, bf16[128,896]{1,0:T(8,128)(2,1)S(1)} %get-tuple-element.40.refs_1_, bf16[128,896]{1,0:T(8,128)(2,1)S(1)} %get-tuple-element.41.refs_2_, ...), custom_call_target="tpu_custom_call" | custom-call | flops 99999997952 | bytes 1 | tf_op jit(solution)/shard_map/back_a/pallas_call | solution.py:36
  70.1 1.8 %back_b.1 = (bf16[64,1408]{1,0:T(8,128)(2,1)S(1)}, bf16[64,1408]{1,0:T(8,128)(2,1)S(1)}, bf16[128,1408]{1,0:T(8,128)(2,1)S(1)}) custom-call(bf16[128,896]{1,0:T(8,128)(2,1)S(1)} %get-tuple-element.39.refs_2_.refs_0_, bf16[128,896]{1,0:T(8,128)(2,1)S(1)} %get-tuple-element.40.refs_1_, bf16[128,896]{1,0:T(8,128)(2,1)S(1)} %get-tuple-element.41.refs_2_, ...), custom_call_target="tpu_custom_call" | custom-call | flops 99999997952 | bytes 1 | tf_op jit(solution)/shard_map/back_b/pallas_call | solution.py:36
  73.1 1.1 %collective-permute-start.27 = (bf16[64,2688]{1,0:T(8,128)(2,1)S(1)}, bf16[64,2688]{1,0:T(8,128)(2,1)S(1)}, u32[]{:S(2)}, u32[]{:S(2)}) collective-permute-start(bf16[64,2688]{1,0:T(8,128)(2,1)S(1)} %to_home_x.1.refs_5_), channel_id=1, source_target_pairs={{0,12},{1,5},{2,14},{3,7},{4,0},{5,9},{6,2},{7,11},{8,4},{9,13},{1... | collective-permute-start | bytes 1032200 | tf_op jit(solution)/shard_map/home_x/ppermute | solution.py:50
  75.2 4.4 %collective-permute-done.28.refs_4_ = bf16[64,2688]{1,0:T(8,128)(2,1)S(1)} collective-permute-done((bf16[64,2688]{1,0:T(8,128)(2,1)S(1)}, bf16[64,2688]{1,0:T(8,128)(2,1)S(1)}, u32[]{:S(2)}, u32[]{:S(2)}) %collective-permute-start.28) | collective-permute-done | bytes 344096 | tf_op jit(solution)/shard_map/from_far/ppermute | solution.py:50
  79.9 3.5 %collective-permute-done.27.refs_0_ = bf16[64,2688]{1,0:T(8,128)(2,1)S(1)} collective-permute-done((bf16[64,2688]{1,0:T(8,128)(2,1)S(1)}, bf16[64,2688]{1,0:T(8,128)(2,1)S(1)}, u32[]{:S(2)}, u32[]{:S(2)}) %collective-permute-start.27) | collective-permute-done | bytes 344096 | tf_op jit(solution)/shard_map/home_x/ppermute | solution.py:50
  84.6 2.9 %collective-permute-start.29 = (bf16[32,1408]{1,0:T(8,128)(2,1)S(1)}, bf16[32,1408]{1,0:T(8,128)(2,1)S(1)}, u32[]{:S(2)}, u32[]{:S(2)}) collective-permute-start(bf16[32,1408]{1,0:T(8,128)(2,1)S(1)} %get-tuple-element.51), channel_id=1, source_target_pairs={{0,8},{1,9},{2,10},{3,11},{4,12},{5,13},{6,14},{7,15},{8,0},{9,1},... | collective-permute-start | bytes 270344 | tf_op jit(solution)/shard_map/home_far/ppermute | solution.py:50
  88.4 2.9 %collective-permute-done.29.refs_2_.refs_1_ = bf16[32,1408]{1,0:T(8,128)(2,1)S(1)} collective-permute-done((bf16[32,1408]{1,0:T(8,128)(2,1)S(1)}, bf16[32,1408]{1,0:T(8,128)(2,1)S(1)}, u32[]{:S(2)}, u32[]{:S(2)}) %collective-permute-start.29) | collective-permute-done | bytes 90144 | tf_op jit(solution)/shard_map/home_far/ppermute | solution.py:50
  91.3 2.2 %collective-permute-start.34 = (bf16[32,1408]{1,0:T(8,128)(2,1)S(1)}, bf16[32,1408]{1,0:T(8,128)(2,1)S(1)}, u32[]{:S(2)}, u32[]{:S(2)}) collective-permute-start(bf16[32,1408]{1,0:T(8,128)(2,1)S(1)} %home_b_part.1), channel_id=1, source_target_pairs={{0,1},{1,0},{2,3},{3,2},{4,5},{5,4},{6,7},{7,6},{8,9},{9,8},{10,11... | collective-permute-start | bytes 270344 | tf_op jit(solution)/shard_map/home_b_core/ppermute | solution.py:50
  93.5 0.9 collective-permute-done.34.refs_3_
  94.5 1.0 %final.1 = bf16[32,4096]{1,0:T(8,128)(2,1)} custom-call(bf16[32,1408]{1,0:T(8,128)(2,1)S(1)} %get-tuple-element.50.refs_4_.refs_0_, bf16[32,1408]{1,0:T(8,128)(2,1)S(1)} %collective-permute-done.29.refs_2_.refs_1_, bf16[64,1408]{1,0:T(8,128)(2,1)S(1)} %collective-permute-done.30.refs_0_.refs_2_, bf16[32,1408]{1,0:T(8,128)(2,1)S(1)} %collective-permute-done.34.refs_3_, ...), custom_call_target="tpu_custom_call" | custom-call | flops 1 | bytes 1 | tf_op jit(solution)/shard_map/final/pallas_call | solution.py:36
  (91 shorter events, 11.9 us)
Async XLA Ops:
  0.0 11.9 %collective-permute-start = (bf16[32,4096]{1,0:T(8,128)(2,1)}, bf16[32,4096]{1,0:T(8,128)(2,1)S(1)}, u32[]{:S(2)}, u32[]{:S(2)}) collective-permute-start(bf16[32,4096]{1,0:T(8,128)(2,1)} %bitcast.32), channel_id=1, source_target_pairs={{16,0},{32,16},{48,32},{64,48},{80,64},{96,80},{112,96},{0,112},{1... | collective-permute-start | bytes 786440 | tf_op jit(solution)/shard_map/shift/ppermute | solution.py:305
  8.0 12.5 %collective-permute-start.6 = (bf16[32,4224]{1,0:T(8,128)(2,1)S(1)}, bf16[32,4224]{1,0:T(8,128)(2,1)S(1)}, u32[]{:S(2)}, u32[]{:S(2)}) collective-permute-start(bf16[32,4224]{1,0:T(8,128)(2,1)S(1)} %get-tuple-element.32), channel_id=1, source_target_pairs={{112,0},{96,16},{80,32},{64,48},{113,1},{97,17},{81,33},{65,49},{1... | collective-permute-start | bytes 811016 | tf_op jit(solution)/shard_map/fetched/ppermute | solution.py:303
  11.9 5.2 %collective-permute-start.2 = (bf16[32,4096]{1,0:T(8,128)(2,1)S(1)}, bf16[32,4096]{1,0:T(8,128)(2,1)S(1)}, u32[]{:S(2)}, u32[]{:S(2)}) collective-permute-start(bf16[32,4096]{1,0:T(8,128)(2,1)S(1)} %collective-permute-done.refs_0_.refs_6_), channel_id=1, source_target_pairs={{0,1},{1,0},{2,3},{3,2},{4,5},{5,4},{6,7},{7,6},{8,9},{9,8},{10,11... | collective-permute-start | bytes 786440 | tf_op jit(solution)/shard_map/cot_core/ppermute | solution.py:50
  13.5 10.2 %collective-permute-start.9 = (bf16[32,4096]{1,0:T(8,128)(2,1)S(1)}, bf16[32,4096]{1,0:T(8,128)(2,1)S(1)}, u32[]{:S(2)}, u32[]{:S(2)}) collective-permute-start(bf16[32,4096]{1,0:T(8,128)(2,1)S(1)} %collective-permute-done.refs_0_.refs_6_), channel_id=1, source_target_pairs={{0,8},{1,9},{2,10},{3,11},{4,12},{5,13},{6,14},{7,15},{8,0},{9,1},... | collective-permute-start | bytes 786440 | tf_op jit(solution)/shard_map/cot_far/ppermute | solution.py:50
  16.4 7.6 %collective-permute-start.1 = (bf16[32,4096]{1,0:T(8,128)(2,1)S(1)}, bf16[32,4096]{1,0:T(8,128)(2,1)S(1)}, u32[]{:S(2)}, u32[]{:S(2)}) collective-permute-start(bf16[32,4096]{1,0:T(8,128)(2,1)S(1)} %collective-permute-done.refs_0_.refs_6_), channel_id=1, source_target_pairs={{0,2},{1,3},{2,0},{3,1},{4,6},{5,7},{6,4},{7,5},{8,10},{9,11},{10,... | collective-permute-start | bytes 786440 | tf_op jit(solution)/shard_map/cot_z/ppermute | solution.py:50
  17.2 12.1 %collective-permute-start.4 = (bf16[64,4096]{1,0:T(8,128)(2,1)S(1)}, bf16[64,4096]{1,0:T(8,128)(2,1)S(1)}, u32[]{:S(2)}, u32[]{:S(2)}) collective-permute-start(bf16[64,4096]{1,0:T(8,128)(2,1)S(1)} %cot_chip.1.refs_3_), channel_id=1, source_target_pairs={{0,4},{1,13},{2,6},{3,15},{4,8},{5,1},{6,10},{7,3},{8,12},{9,5},{1... | collective-permute-start | bytes 1572872 | tf_op jit(solution)/shard_map/cot_ahead/ppermute | solution.py:50
  20.8 3.2 %collective-permute-start.8 = (bf16[32,4096]{1,0:T(8,128)(2,1)S(1)}, bf16[32,4096]{1,0:T(8,128)(2,1)S(1)}, u32[]{:S(2)}, u32[]{:S(2)}) collective-permute-start(bf16[32,4096]{1,0:T(8,128)(2,1)S(1)} %get-tuple-element.34.refs_0_.refs_1_.refs_6_), channel_id=1, source_target_pairs={{0,1},{1,0},{2,3},{3,2},{4,5},{5,4},{6,7},{7,6},{8,9},{9,8},{10,11... | collective-permute-start | bytes 786440 | tf_op jit(solution)/shard_map/normed_core/ppermute | solution.py:50
  22.9 7.9 %collective-permute-start.7 = (bf16[32,4096]{1,0:T(8,128)(2,1)S(1)}, bf16[32,4096]{1,0:T(8,128)(2,1)S(1)}, u32[]{:S(2)}, u32[]{:S(2)}) collective-permute-start(bf16[32,4096]{1,0:T(8,128)(2,1)S(1)} %get-tuple-element.34.refs_0_.refs_1_.refs_6_), channel_id=1, source_target_pairs={{0,2},{1,3},{2,0},{3,1},{4,6},{5,7},{6,4},{7,5},{8,10},{9,11},{10,... | collective-permute-start | bytes 786440 | tf_op jit(solution)/shard_map/normed_z/ppermute | solution.py:50
  24.1 10.8 %collective-permute-start.11 = (bf16[64,4096]{1,0:T(8,128)(2,1)S(1)}, bf16[64,4096]{1,0:T(8,128)(2,1)S(1)}, u32[]{:S(2)}, u32[]{:S(2)}) collective-permute-start(bf16[64,4096]{1,0:T(8,128)(2,1)S(1)} %chip.1.refs_2_), channel_id=1, source_target_pairs={{0,4},{1,13},{2,6},{3,15},{4,8},{5,1},{6,10},{7,3},{8,12},{9,5},{1... | collective-permute-start | bytes 1572872 | tf_op jit(solution)/shard_map/ahead/ppermute | solution.py:50
  26.9 8.8 %collective-permute-start.14 = (bf16[32,4096]{1,0:T(8,128)(2,1)S(1)}, bf16[32,4096]{1,0:T(8,128)(2,1)S(1)}, u32[]{:S(2)}, u32[]{:S(2)}) collective-permute-start(bf16[32,4096]{1,0:T(8,128)(2,1)S(1)} %collective-permute-done.9.refs_3_.refs_0_), channel_id=1, source_target_pairs={{0,1},{1,0},{2,3},{3,2},{4,5},{5,4},{6,7},{7,6},{8,9},{9,8},{10,11... | collective-permute-start | bytes 786440 | tf_op jit(solution)/shard_map/cot_far_core/ppermute | solution.py:50
  29.4 9.1 %collective-permute-start.5 = (bf16[64,4096]{1,0:T(8,128)(2,1)S(1)}, bf16[64,4096]{1,0:T(8,128)(2,1)S(1)}, u32[]{:S(2)}, u32[]{:S(2)}) collective-permute-start(bf16[64,4096]{1,0:T(8,128)(2,1)S(1)} %collective-permute-done.4.refs_0_.refs_4_), channel_id=1, source_target_pairs={{0,1},{1,0},{2,3},{3,2},{4,5},{5,4},{6,7},{7,6},{8,9},{9,8},{10,11... | collective-permute-start | bytes 1572872 | tf_op jit(solution)/shard_map/cot_behind/ppermute | solution.py:50
  30.8 5.0 %collective-permute-start.10 = (bf16[32,4096]{1,0:T(8,128)(2,1)S(1)}, bf16[32,4096]{1,0:T(8,128)(2,1)S(1)}, u32[]{:S(2)}, u32[]{:S(2)}) collective-permute-start(bf16[32,4096]{1,0:T(8,128)(2,1)S(1)} %normed_z_copy.1), channel_id=1, source_target_pairs={{0,1},{1,0},{2,3},{3,2},{4,5},{5,4},{6,7},{7,6},{8,9},{9,8},{10,11... | collective-permute-start | bytes 786440 | tf_op jit(solution)/shard_map/normed_z_core/ppermute | solution.py:50
  31.7 13.7 %collective-permute-start.16 = (bf16[64,4096]{1,0:T(8,128)(2,1)S(1)}, bf16[64,4096]{1,0:T(8,128)(2,1)S(1)}, u32[]{:S(2)}, u32[]{:S(2)}) collective-permute-start(bf16[64,4096]{1,0:T(8,128)(2,1)S(1)} %cot_ahead_copy.1.refs_1_), channel_id=1, source_target_pairs={{0,2},{1,3},{2,0},{3,1},{4,6},{5,7},{6,4},{7,5},{8,10},{9,11},{10,... | collective-permute-start | bytes 1572872 | tf_op jit(solution)/shard_map/cot_ahead_z/ppermute | solution.py:50
  35.7 2.8 %collective-permute-start.12 = (bf16[32,4096]{1,0:T(8,128)(2,1)S(1)}, bf16[32,4096]{1,0:T(8,128)(2,1)S(1)}, u32[]{:S(2)}, u32[]{:S(2)}) collective-permute-start(bf16[32,4096]{1,0:T(8,128)(2,1)S(1)} %behind_0.1), channel_id=1, source_target_pairs={{0,1},{1,0},{2,3},{3,2},{4,5},{5,4},{6,7},{7,6},{8,9},{9,8},{10,11... | collective-permute-start | bytes 786440 | tf_op jit(solution)/shard_map/behind_0/ppermute | solution.py:50
  35.8 2.7 %collective-permute-start.13 = (bf16[32,4096]{1,0:T(8,128)(2,1)S(1)}, bf16[32,4096]{1,0:T(8,128)(2,1)S(1)}, u32[]{:S(2)}, u32[]{:S(2)}) collective-permute-start(bf16[32,4096]{1,0:T(8,128)(2,1)S(1)} %behind_32.1), channel_id=1, source_target_pairs={{0,1},{1,0},{2,3},{3,2},{4,5},{5,4},{6,7},{7,6},{8,9},{9,8},{10,11... | collective-permute-start | bytes 786440 | tf_op jit(solution)/shard_map/behind_32/ppermute | solution.py:50
  36.8 10.5 %collective-permute-start.15 = (bf16[64,4096]{1,0:T(8,128)(2,1)S(1)}, bf16[64,4096]{1,0:T(8,128)(2,1)S(1)}, u32[]{:S(2)}, u32[]{:S(2)}) collective-permute-start(bf16[64,4096]{1,0:T(8,128)(2,1)S(1)} %chip_z.1.refs_9_), channel_id=1, source_target_pairs={{0,4},{1,13},{2,6},{3,15},{4,8},{5,1},{6,10},{7,3},{8,12},{9,5},{1... | collective-permute-start | bytes 1572872 | tf_op jit(solution)/shard_map/ahead_z/ppermute | solution.py:50
  45.5 4.7 %collective-permute-start.17 = (bf16[48,4096]{1,0:T(8,128)(2,1)S(1)}, bf16[48,4096]{1,0:T(8,128)(2,1)S(1)}, u32[]{:S(2)}, u32[]{:S(2)}) collective-permute-start(bf16[48,4096]{1,0:T(8,128)(2,1)S(1)} %cot_behind_z_0.1), channel_id=1, source_target_pairs={{0,1},{1,0},{2,3},{3,2},{4,5},{5,4},{6,7},{7,6},{8,9},{9,8},{10,11... | collective-permute-start | bytes 1179656 | tf_op jit(solution)/shard_map/cot_behind_z_0/ppermute | solution.py:50
  46.4 3.8 %collective-permute-start.18 = (bf16[16,4096]{1,0:T(8,128)(2,1)S(1)}, bf16[16,4096]{1,0:T(8,128)(2,1)S(1)}, u32[]{:S(2)}, u32[]{:S(2)}) collective-permute-start(bf16[16,4096]{1,0:T(8,128)(2,1)S(1)} %cot_behind_z_48.1), channel_id=1, source_target_pairs={{0,1},{1,0},{2,3},{3,2},{4,5},{5,4},{6,7},{7,6},{8,9},{9,8},{10,11... | collective-permute-start | bytes 393224 | tf_op jit(solution)/shard_map/cot_behind_z_48/ppermute | solution.py:50
  46.5 12.8 %collective-permute-start.22 = (bf16[32,4096]{1,0:T(8,128)(2,1)S(1)}, bf16[32,4096]{1,0:T(8,128)(2,1)S(1)}, u32[]{:S(2)}, u32[]{:S(2)}) collective-permute-start(bf16[32,4096]{1,0:T(8,128)(2,1)S(1)} %collective-permute-done.9.refs_3_.refs_0_), channel_id=1, source_target_pairs={{0,2},{1,3},{2,0},{3,1},{4,6},{5,7},{6,4},{7,5},{8,10},{9,11},{10,... | collective-permute-start | bytes 786440 | tf_op jit(solution)/shard_map/cot_far_z/ppermute | solution.py:50
  47.3 12.0 %collective-permute-start.21 = (bf16[64,4096]{1,0:T(8,128)(2,1)S(1)}, bf16[64,4096]{1,0:T(8,128)(2,1)S(1)}, u32[]{:S(2)}, u32[]{:S(2)}) collective-permute-start(bf16[64,4096]{1,0:T(8,128)(2,1)S(1)} %part.1.refs_4_), channel_id=1, source_target_pairs={{0,4},{1,13},{2,6},{3,15},{4,8},{5,1},{6,10},{7,3},{8,12},{9,5},{1... | collective-permute-start | bytes 1572872 | tf_op jit(solution)/shard_map/far/ppermute | solution.py:50
  50.1 4.6 %collective-permute-start.20 = (bf16[64,4096]{1,0:T(8,128)(2,1)S(1)}, bf16[64,4096]{1,0:T(8,128)(2,1)S(1)}, u32[]{:S(2)}, u32[]{:S(2)}) collective-permute-start(bf16[64,4096]{1,0:T(8,128)(2,1)S(1)} %collective-permute-done.15.refs_1_.refs_3_), channel_id=1, source_target_pairs={{0,1},{1,0},{2,3},{3,2},{4,5},{5,4},{6,7},{7,6},{8,9},{9,8},{10,11... | collective-permute-start | bytes 1572872 | tf_op jit(solution)/shard_map/behind_z/ppermute | solution.py:50
  60.0 6.5 %collective-permute-start.19 = (bf16[128,4096]{1,0:T(8,128)(2,1)S(1)}, bf16[128,4096]{1,0:T(8,128)(2,1)S(1)}, u32[]{:S(2)}, u32[]{:S(2)}) collective-permute-start(bf16[128,4096]{1,0:T(8,128)(2,1)S(1)} %get-tuple-element.38.refs_8_), channel_id=1, source_target_pairs={{0,1},{1,0},{2,3},{3,2},{4,5},{5,4},{6,7},{7,6},{8,9},{9,8},{10,11... | collective-permute-start | bytes 3145736 | tf_op jit(solution)/shard_map/near_got/ppermute | solution.py:50
  72.3 7.4 %collective-permute-start.28 = (bf16[64,2688]{1,0:T(8,128)(2,1)S(1)}, bf16[64,2688]{1,0:T(8,128)(2,1)S(1)}, u32[]{:S(2)}, u32[]{:S(2)}) collective-permute-start(bf16[64,2688]{1,0:T(8,128)(2,1)S(1)} %to_far.1.refs_4_), channel_id=1, source_target_pairs={{0,12},{1,5},{2,14},{3,7},{4,0},{5,9},{6,2},{7,11},{8,4},{9,13},{1... | collective-permute-start | bytes 1032200 | tf_op jit(solution)/shard_map/from_far/ppermute | solution.py:50
  73.1 10.2 %collective-permute-start.27 = (bf16[64,2688]{1,0:T(8,128)(2,1)S(1)}, bf16[64,2688]{1,0:T(8,128)(2,1)S(1)}, u32[]{:S(2)}, u32[]{:S(2)}) collective-permute-start(bf16[64,2688]{1,0:T(8,128)(2,1)S(1)} %to_home_x.1.refs_5_), channel_id=1, source_target_pairs={{0,12},{1,5},{2,14},{3,7},{4,0},{5,9},{6,2},{7,11},{8,4},{9,13},{1... | collective-permute-start | bytes 1032200 | tf_op jit(solution)/shard_map/home_x/ppermute | solution.py:50
  74.3 9.7 %collective-permute-start.26 = (bf16[128,1408]{1,0:T(8,128)(2,1)S(1)}, bf16[128,1408]{1,0:T(8,128)(2,1)S(1)}, u32[]{:S(2)}, u32[]{:S(2)}) collective-permute-start(bf16[128,1408]{1,0:T(8,128)(2,1)S(1)} %away.1.refs_2_), channel_id=1, source_target_pairs={{0,2},{1,3},{2,0},{3,1},{4,6},{5,7},{6,4},{7,5},{8,10},{9,11},{10,... | collective-permute-start | bytes 1081352 | tf_op jit(solution)/shard_map/from_z/ppermute | solution.py:50
  79.8 7.7 %collective-permute-start.31 = (bf16[64,2688]{1,0:T(8,128)(2,1)S(1)}, bf16[64,2688]{1,0:T(8,128)(2,1)S(1)}, u32[]{:S(2)}, u32[]{:S(2)}) collective-permute-start(bf16[64,2688]{1,0:T(8,128)(2,1)S(1)} %to_home.1.refs_1_), channel_id=1, source_target_pairs={{0,12},{1,5},{2,14},{3,7},{4,0},{5,9},{6,2},{7,11},{8,4},{9,13},{1... | collective-permute-start | bytes 1032200 | tf_op jit(solution)/shard_map/home/ppermute | solution.py:50
  83.4 4.1 %collective-permute-start.33 = (bf16[32,2688]{1,0:T(8,128)(2,1)S(1)}, bf16[32,2688]{1,0:T(8,128)(2,1)S(1)}, u32[]{:S(2)}, u32[]{:S(2)}) collective-permute-start(bf16[32,2688]{1,0:T(8,128)(2,1)S(1)} %home_x_core_z_part.1), channel_id=1, source_target_pairs={{0,1},{1,0},{2,3},{3,2},{4,5},{5,4},{6,7},{7,6},{8,9},{9,8},{10,11... | collective-permute-start | bytes 516104 | tf_op jit(solution)/shard_map/home_x_core_z/ppermute | solution.py:50
  83.8 3.7 %collective-permute-start.32 = (bf16[32,2688]{1,0:T(8,128)(2,1)S(1)}, bf16[32,2688]{1,0:T(8,128)(2,1)S(1)}, u32[]{:S(2)}, u32[]{:S(2)}) collective-permute-start(bf16[32,2688]{1,0:T(8,128)(2,1)S(1)} %home_x_core_part.1), channel_id=1, source_target_pairs={{0,1},{1,0},{2,3},{3,2},{4,5},{5,4},{6,7},{7,6},{8,9},{9,8},{10,11... | collective-permute-start | bytes 516104 | tf_op jit(solution)/shard_map/home_x_core/ppermute | solution.py:50
  84.2 7.1 %collective-permute-start.30 = (bf16[64,1408]{1,0:T(8,128)(2,1)S(1)}, bf16[64,1408]{1,0:T(8,128)(2,1)S(1)}, u32[]{:S(2)}, u32[]{:S(2)}) collective-permute-start(bf16[64,1408]{1,0:T(8,128)(2,1)S(1)} %get-tuple-element.52), channel_id=1, source_target_pairs={{0,12},{1,5},{2,14},{3,7},{4,0},{5,9},{6,2},{7,11},{8,4},{9,13},{1... | collective-permute-start | bytes 540680 | tf_op jit(solution)/shard_map/home_b/ppermute | solution.py:50
  84.6 6.7 %collective-permute-start.29 = (bf16[32,1408]{1,0:T(8,128)(2,1)S(1)}, bf16[32,1408]{1,0:T(8,128)(2,1)S(1)}, u32[]{:S(2)}, u32[]{:S(2)}) collective-permute-start(bf16[32,1408]{1,0:T(8,128)(2,1)S(1)} %get-tuple-element.51), channel_id=1, source_target_pairs={{0,8},{1,9},{2,10},{3,11},{4,12},{5,13},{6,14},{7,15},{8,0},{9,1},... | collective-permute-start | bytes 270344 | tf_op jit(solution)/shard_map/home_far/ppermute | solution.py:50
  87.6 6.9 %collective-permute-start.35 = (bf16[32,2688]{1,0:T(8,128)(2,1)S(1)}, bf16[32,2688]{1,0:T(8,128)(2,1)S(1)}, u32[]{:S(2)}, u32[]{:S(2)}) collective-permute-start(bf16[32,2688]{1,0:T(8,128)(2,1)S(1)} %get-tuple-element.54), channel_id=1, source_target_pairs={{0,2},{1,3},{2,0},{3,1},{4,6},{5,7},{6,4},{7,5},{8,10},{9,11},{10,... | collective-permute-start | bytes 516104 | tf_op jit(solution)/shard_map/total_z/ppermute | solution.py:50
  91.3 3.2 %collective-permute-start.34 = (bf16[32,1408]{1,0:T(8,128)(2,1)S(1)}, bf16[32,1408]{1,0:T(8,128)(2,1)S(1)}, u32[]{:S(2)}, u32[]{:S(2)}) collective-permute-start(bf16[32,1408]{1,0:T(8,128)(2,1)S(1)} %home_b_part.1), channel_id=1, source_target_pairs={{0,1},{1,0},{2,3},{3,2},{4,5},{5,4},{6,7},{7,6},{8,9},{9,8},{10,11... | collective-permute-start | bytes 270344 | tf_op jit(solution)/shard_map/home_b_core/ppermute | solution.py:50
  (13 other events, 149.0 us)
